TPU v7x, 32 devices: a whole 2x2x4 slice. The times are simulated.
32 devices in a mesh: dp: 2 (over y), row: 4 (over z), col: 4 (over x, core).
Axes of the slice: x: 2, y: 2, z: 4, core: 2. Of those that a mesh axis runs over, the one named last changes fastest.
Arguments:
- inputs: bfloat16 [8192, 2048], P(('dp', 'col')), may hold values from -6 to 6
- prefix_len: int32 [8], P(('dp', 'col')), may hold values from 102 to 512
- norm1_gain: float32 [2048], replicated, may hold values from 0.25 to 1.75
- norm1_shift: float32 [2048], replicated, may hold values from -1.5 to 1.5
- w_qkv: float32 [3, 2048, 2048], P(None, ('dp', 'col'), 'row'), may hold values from -0.1875 to 0.1875
- b_qv: float32 [2, 2048], P(None, 'row'), may hold values from -2.5 to 2.5
- w_out: float32 [2048, 2048], P('row', ('dp', 'col')), may hold values from -0.5 to 0.5
- b_out: float32 [2048], replicated, may hold values from -2.5 to 2.5
- norm2_gain: float32 [2048], replicated, may hold values from 0.25 to 1.75
- norm2_shift: float32 [2048], replicated, may hold values from -1.5 to 1.5
- w_in: float32 [2048, 8192], P(('dp', 'col'), 'row'), may hold values from -0.125 to 0.125
- b_in: float32 [8192], P('row'), may hold values from -2.5 to 2.5
- w_down: float32 [8192, 2048], P('row', ('dp', 'col')), may hold values from -0.09375 to 0.09375
- b_down: float32 [2048], replicated, may hold values from -2.5 to 2.5
- d_output: bfloat16 [8192, 2048], P(('dp', 'col')), may hold values from -6 to 6
Outputs:
- output: bfloat16 [8192, 2048], P(('dp', 'col'))
- d_inputs: float32 [8192, 2048], P(('dp', 'col'))
- d_norm1_gain: float32 [2048], replicated
- d_norm1_shift: float32 [2048], replicated
- d_w_qkv: float32 [3, 2048, 2048], P(None, ('dp', 'col'), 'row')
- d_b_qv: float32 [2, 2048], P(None, 'row')
- d_w_out: float32 [2048, 2048], P('row', ('dp', 'col'))
- d_b_out: float32 [2048], replicated
- d_norm2_gain: float32 [2048], replicated
- d_norm2_shift: float32 [2048], replicated
- d_w_in: float32 [2048, 8192], P(('dp', 'col'), 'row')
- d_b_in: float32 [8192], P('row')
- d_w_down: float32 [8192, 2048], P('row', ('dp', 'col'))
- d_b_down: float32 [2048], replicated
All inputs are finite; a program needn't handle non-finite values.
Results may differ from a plain program's by a relative error of at most 0.012.
The roundings to bfloat16 on the way count: a program that leaves them out, or rounds other values in their place, can miss the bound.
Values may be sent and summed in bfloat16 or wider, within the bound.
A program may use at most 256 MiB of HBM per device.

v0:
```python
from functools import partial

import jax
import jax.numpy as jnp
from jax import lax
from jax.sharding import PartitionSpec as P

HEAD_DIM = 128


eps_norm = 1e-05


def norm_forward(values, norm_gain, norm_shift):
    average = jnp.mean(values, axis=-1, keepdims=True)
    centered = values - average
    variance = jnp.mean(centered * centered, axis=-1, keepdims=True)
    inverse = lax.rsqrt(variance + eps_norm)
    scaled = centered * inverse
    return (scaled * norm_gain + norm_shift, scaled, inverse)


def norm_backward(grad, scaled, inverse, norm_gain):
    grad_scaled = grad * norm_gain
    return inverse * (
        grad_scaled
        - jnp.mean(grad_scaled, axis=-1, keepdims=True)
        - scaled * jnp.mean(grad_scaled * scaled, axis=-1, keepdims=True)
    )


def block_scores(queries, keys_low, block_start, block_rows, prefix):
    length, width = keys_low.shape
    heads = width // HEAD_DIM
    score_scale = HEAD_DIM ** (-0.5)
    query_block = lax.dynamic_slice_in_dim(queries, block_start, block_rows, 0).reshape(
        block_rows, heads, HEAD_DIM
    )
    key_heads = keys_low.reshape(length, heads, HEAD_DIM)
    scores = (
        jnp.einsum("qhd,khd->hqk", query_block, key_heads, preferred_element_type=jnp.float32)
        * score_scale
    )
    rows_here = block_start + lax.iota(jnp.int32, block_rows)
    columns = lax.iota(jnp.int32, length)
    allowed = (columns[None, :] <= rows_here[:, None]) | (columns[None, :] < prefix)
    return (jnp.where(allowed[None], scores, -1000000000.0), query_block, key_heads)


def attend_forward(queries, keys_low, values_low, prefix, block_rows):
    length, width = queries.shape
    heads = width // HEAD_DIM
    value_heads = values_low.reshape(length, heads, HEAD_DIM)

    def one_block(block_index):
        block_start = block_index * block_rows
        scores, _, _ = block_scores(queries, keys_low, block_start, block_rows, prefix)
        row_max = jnp.max(scores, axis=-1)
        expo = jnp.exp(scores - row_max[..., None])
        row_total = jnp.sum(expo, axis=-1)
        probs_low = (expo / row_total[..., None]).astype(jnp.bfloat16)
        context = jnp.einsum(
            "hqk,khd->qhd", probs_low, value_heads, preferred_element_type=jnp.float32
        )
        return (context.reshape(block_rows, width), row_max, row_total)

    contexts, maxima, totals = lax.map(one_block, jnp.arange(length // block_rows, dtype=jnp.int32))
    return (contexts.reshape(length, width), maxima, totals)


def attend_backward(queries, keys_low, values_low, prefix, block_rows, maxima, totals, d_context):
    length, width = queries.shape
    heads = width // HEAD_DIM
    score_scale = HEAD_DIM ** (-0.5)
    value_heads = values_low.reshape(length, heads, HEAD_DIM)

    def one_block(sums, entries):
        block_index, row_max, row_total = entries
        block_start = block_index * block_rows
        scores, query_block, key_heads = block_scores(
            queries, keys_low, block_start, block_rows, prefix
        )
        probs = jnp.exp(scores - row_max[..., None]) / row_total[..., None]
        probs_low = probs.astype(jnp.bfloat16)
        grad_block = lax.dynamic_slice_in_dim(d_context, block_start, block_rows, 0).reshape(
            block_rows, heads, HEAD_DIM
        )
        d_probs = jnp.einsum(
            "qhd,khd->hqk", grad_block, value_heads, preferred_element_type=jnp.float32
        )
        inner = jnp.sum(d_probs * probs, axis=-1, keepdims=True)
        d_scores = (probs * (d_probs - inner)).astype(jnp.bfloat16)
        d_query = (
            jnp.einsum("hqk,khd->qhd", d_scores, key_heads, preferred_element_type=jnp.float32)
            * score_scale
        )
        d_keys = (
            sums[0]
            + jnp.einsum("hqk,qhd->khd", d_scores, query_block, preferred_element_type=jnp.float32)
            * score_scale
        )
        d_values = sums[1] + jnp.einsum(
            "hqk,qhd->khd", probs_low, grad_block, preferred_element_type=jnp.float32
        )
        return ((d_keys, d_values), d_query.reshape(block_rows, width).astype(jnp.bfloat16))

    zeros = jnp.zeros((length, heads, HEAD_DIM), jnp.float32)
    count = length // block_rows
    (d_keys, d_values), d_queries = lax.scan(
        one_block, (zeros, zeros), (jnp.arange(count, dtype=jnp.int32), maxima, totals)
    )
    return (
        d_queries.reshape(length, width),
        d_keys.reshape(length, width).astype(jnp.bfloat16),
        d_values.reshape(length, width).astype(jnp.bfloat16),
    )


def local(
    inputs,
    prefix_len,
    norm1_gain,
    norm1_shift,
    w_qkv,
    b_qv,
    w_out,
    b_out,
    norm2_gain,
    norm2_shift,
    w_in,
    b_in,
    w_down,
    b_down,
    d_output,
):
    low_mats = (
        w_qkv.astype(jnp.bfloat16),
        w_out.astype(jnp.bfloat16),
        w_in.astype(jnp.bfloat16),
        w_down.astype(jnp.bfloat16),
    )
    full_qkv, full_out, full_in, full_down = (
        lax.all_gather(low_mats[0], ("dp", "col"), axis=1, tiled=True),
        lax.all_gather(low_mats[1], ("dp", "col"), axis=1, tiled=True),
        lax.all_gather(low_mats[2], ("dp", "col"), axis=0, tiled=True),
        lax.all_gather(low_mats[3], ("dp", "col"), axis=1, tiled=True),
    )
    length = inputs.shape[0]
    block_rows = 512
    prefix = prefix_len[0]
    source = inputs.astype(jnp.float32)
    normed1, scaled1, inverse1 = norm_forward(source, norm1_gain, norm1_shift)
    normed1_low = normed1.astype(jnp.bfloat16)
    projected = jnp.einsum("td,cdn->ctn", normed1_low, full_qkv, preferred_element_type=jnp.float32)
    bias_rows = jnp.stack([b_qv[0], jnp.zeros_like(b_qv[0]), b_qv[1]])
    projected = (projected + bias_rows[:, None, :]).astype(jnp.bfloat16)
    queries, keys_low, values_low = (projected[0], projected[1], projected[2])
    context, maxima, totals = attend_forward(queries, keys_low, values_low, prefix, block_rows)
    context_low = context.astype(jnp.bfloat16)
    attn_partial = jnp.dot(context_low, full_out, preferred_element_type=jnp.float32)
    hidden = source + lax.psum(attn_partial, "row") + b_out
    normed2, scaled2, inverse2 = norm_forward(hidden, norm2_gain, norm2_shift)
    normed2_low = normed2.astype(jnp.bfloat16)
    pre_act = jnp.dot(normed2_low, full_in, preferred_element_type=jnp.float32) + b_in
    activated, gelu_pull = jax.vjp(partial(jax.nn.gelu, approximate=False), pre_act)
    activated_low = activated.astype(jnp.bfloat16)
    mlp_partial = jnp.dot(activated_low, full_down, preferred_element_type=jnp.float32)
    result = hidden + lax.psum(mlp_partial.astype(jnp.bfloat16), "row").astype(jnp.float32) + b_down
    output = result.astype(jnp.bfloat16)
    grad_top = d_output.astype(jnp.float32)
    grad_bdown = jnp.sum(grad_top, axis=0)
    grad_wdown = jnp.einsum(
        "tf,td->fd", activated_low, d_output, preferred_element_type=jnp.float32
    )
    grad_act = jnp.einsum("td,fd->tf", d_output, full_down, preferred_element_type=jnp.float32)
    grad_pre = gelu_pull(grad_act)[0].astype(jnp.bfloat16)
    grad_bin = jnp.sum(grad_pre.astype(jnp.float32), axis=0)
    grad_win = jnp.einsum("td,tf->df", normed2_low, grad_pre, preferred_element_type=jnp.float32)
    norm2_partial = jnp.einsum("tf,df->td", grad_pre, full_in, preferred_element_type=jnp.float32)
    grad_normed2 = lax.psum(norm2_partial, "row")
    grad_gain2 = jnp.sum(grad_normed2 * scaled2, axis=0)
    grad_shift2 = jnp.sum(grad_normed2, axis=0)
    grad_hidden = grad_top + norm_backward(grad_normed2, scaled2, inverse2, norm2_gain)
    grad_branch = grad_hidden.astype(jnp.bfloat16)
    grad_bout = jnp.sum(grad_branch.astype(jnp.float32), axis=0)
    grad_wout = jnp.einsum(
        "tr,td->rd", context_low, grad_branch, preferred_element_type=jnp.float32
    )
    grad_context = jnp.einsum(
        "td,rd->tr", grad_branch, full_out, preferred_element_type=jnp.float32
    ).astype(jnp.bfloat16)
    grad_queries, grad_keys, grad_values = attend_backward(
        queries, keys_low, values_low, prefix, block_rows, maxima, totals, grad_context
    )
    grad_projected = jnp.stack([grad_queries, grad_keys, grad_values])
    grad_bqv = jnp.stack(
        [
            jnp.sum(grad_queries.astype(jnp.float32), axis=0),
            jnp.sum(grad_values.astype(jnp.float32), axis=0),
        ]
    )
    grad_wqkv = jnp.einsum(
        "td,ctn->cdn", normed1_low, grad_projected, preferred_element_type=jnp.float32
    )
    norm1_partial = jnp.einsum(
        "ctn,cdn->td", grad_projected, full_qkv, preferred_element_type=jnp.float32
    )
    grad_normed1 = lax.psum(norm1_partial, "row")
    grad_gain1 = jnp.sum(grad_normed1 * scaled1, axis=0)
    grad_shift1 = jnp.sum(grad_normed1, axis=0)
    d_inputs = grad_hidden + norm_backward(grad_normed1, scaled1, inverse1, norm1_gain)
    sent_wqkv, sent_wout, sent_win, sent_wdown = (
        lax.psum_scatter(grad_wqkv, ("dp", "col"), scatter_dimension=1, tiled=True),
        lax.psum_scatter(grad_wout, ("dp", "col"), scatter_dimension=1, tiled=True),
        lax.psum_scatter(grad_win, ("dp", "col"), scatter_dimension=0, tiled=True),
        lax.psum_scatter(grad_wdown, ("dp", "col"), scatter_dimension=1, tiled=True),
    )
    small = lax.psum(
        (
            grad_gain1,
            grad_shift1,
            grad_bqv,
            grad_bout,
            grad_gain2,
            grad_shift2,
            grad_bin,
            grad_bdown,
        ),
        ("dp", "col"),
    )
    return (
        output,
        d_inputs,
        small[0],
        small[1],
        sent_wqkv,
        small[2],
        sent_wout,
        small[3],
        small[4],
        small[5],
        sent_win,
        small[6],
        sent_wdown,
        small[7],
    )


def solution(mesh):
    return jax.shard_map(
        local,
        mesh=mesh,
        in_specs=(
            P(("dp", "col"), None),
            P(("dp", "col")),
            P(),
            P(),
            P(None, ("dp", "col"), "row"),
            P(None, "row"),
            P("row", ("dp", "col")),
            P(),
            P(),
            P(),
            P(("dp", "col"), "row"),
            P("row"),
            P("row", ("dp", "col")),
            P(),
            P(("dp", "col"), None),
        ),
        out_specs=(
            P(("dp", "col"), None),
            P(("dp", "col"), None),
            P(),
            P(),
            P(None, ("dp", "col"), "row"),
            P(None, "row"),
            P("row", ("dp", "col")),
            P(),
            P(),
            P(),
            P(("dp", "col"), "row"),
            P("row"),
            P("row", ("dp", "col")),
            P(),
        ),
        check_vma=False,
    )
```

profile of v0, /device:TPU:0, one launch (start us, length us, event | category | flops | bytes accessed | tf_op | source)
XLA Modules:
  0.0 1795.9 jit_solution(17203102358258843139)
XLA Ops:
  18.9 40.9 %all-gather.5.cloned.1.call-done = bf16[3,2048,512]{1,2,0:T(8,128)(2,1)} async-done(((bf16[3,256,512]{1,2,0:T(8,128)(2,1)}), bf16[3,2048,512]{1,2,0:T(8,128)(2,1)}) %all-gather.5.cloned.1.call-update) | async-done | bytes 6291472 | tf_op jit(solution)/shard_map/all_gather | solution.py:143
  59.9 11.3 fusion.36
  76.2 22.5 %while.31 = (s32[]{:T(128)}, bf16[2,512,512]{2,1,0:T(8,128)(2,1)}, f32[2,4,512]{2,1,0:T(4,128)S(1)}, f32[2,4,512]{2,1,0:T(4,128)S(1)}, s32[2]{0:T(128)S(1)}, /*i...) while((s32[]{:T(128)}, bf16[2,512,512]{2,1,0:T(8,128)(2,1)}, ...), condition=%wide.wide.region_5.6_spmd, body=%wide.wide.region_2.5_spmd.sunk | while | flops 1099953664 | bytes 37828856 | solution.py:67
  98.7 8.0 fusion.51
  112.8 285.0 %all-reduce.6.cloned.1.call-done = f32[1024,2048]{1,0:T(8,128)} async-done(((f32[1024,2048]{1,0:T(8,128)}), f32[1024,2048]{1,0:T(8,128)}) %all-reduce.6.cloned.1.call-update) | async-done | bytes 8388624 | tf_op jit(solution)/shard_map/psum | solution.py:161
  408.0 45.5 %all-gather.9.cloned.1.call-done = bf16[2048,2048]{1,0:T(8,128)(2,1)} async-done(((bf16[256,2048]{1,0:T(8,128)(2,1)}), bf16[2048,2048]{1,0:T(8,128)(2,1)}) %all-gather.9.cloned.1.call-update) | async-done | bytes 8388624 | tf_op jit(solution)/shard_map/all_gather | solution.py:145
  453.5 15.9 fusion.45
  469.4 42.4 %all-gather.11.cloned.1.call-done = bf16[2048,2048]{1,0:T(8,128)(2,1)} async-done(((bf16[2048,256]{1,0:T(8,128)(2,1)}), bf16[2048,2048]{1,0:T(8,128)(2,1)}) %all-gather.11.cloned.1.call-update) | async-done | bytes 8388624 | tf_op jit(solution)/shard_map/all_gather | solution.py:146
  511.8 33.7 %convert_reduce_fusion.2 = (f32[2048]{0:T(1024)}, bf16[1024,2048]{1,0:T(8,128)(2,1)S(1)}, f32[1024,2048]{1,0:T(8,128)}) fusion(f32[1024,2048]{1,0:T(8,128)} %fusion.45, f32[2048]{0:T(1024)S(1)} %copy-done.41, bf16[1024,2048]{1,0:T(8,128)(2,1)} %param.33, bf16[2048,2048]{1,0:T(8,128)(2,1)} %all-gather.11.cloned.1.call-done), kind=kOutput, calls=%fused_computation.58 | convolution fusion | flops 8747218944 | bytes 33570816 | tf_op jit(solution)/shard_map/td,fd->tf/dot_general | solution.py:175
  547.5 11.3 fusion.52
  558.9 8.3 multiply_convert_fusion.1
  569.2 12.6 convolution_convert_fusion
  583.2 266.6 %all-reduce.10.cloned.1.call-done = f32[1024,2048]{1,0:T(8,128)} async-done(((f32[1024,2048]{1,0:T(8,128)}), f32[1024,2048]{1,0:T(8,128)}) %all-reduce.10.cloned.1.call-update) | async-done | bytes 8388624 | tf_op jit(solution)/shard_map/psum | solution.py:180
  849.8 8.2 multiply_reduce_fusion.1
  858.0 148.7 %all-reduce.8.cloned.1.call-done = bf16[1024,2048]{1,0:T(8,128)(2,1)} async-done(((bf16[1024,2048]{1,0:T(8,128)(2,1)}), bf16[1024,2048]{1,0:T(8,128)(2,1)}) %all-reduce.8.cloned.1.call-update) | async-done | bytes 4194320 | tf_op jit(solution)/shard_map/psum | solution.py:168
  1006.8 13.8 convert_reduce_fusion.3
  1024.3 67.0 %while.30 = (s32[]{:T(128)}, f32[1024,4,128]{0,2,1:T(8,128)S(1)}, f32[1024,4,128]{0,2,1:T(8,128)}, bf16[2,512,512]{1,2,0:T(8,128)(2,1)}, s32[2]{0:T(128)S(1)}, /...) while((s32[]{:T(128)}, f32[1024,4,128]{0,2,1:T(8,128)S(1)}, ...), condition=%wide.region_15.16_spmd.clone, body=%wide.region_13.15_spmd.clone.sunk | while | flops 2709519872 | bytes 132717008 | solution.py:109
  1028.1 6.3 exponential_divide_fusion.2
  1061.4 6.3 exponential_divide_fusion.2
  1096.6 11.2 convolution_bitcast_fusion.1
  1109.0 12.7 convolution_bitcast_fusion
  1123.0 7.8 fusion.41
  1130.9 16.4 fusion.44
  1147.3 15.6 fusion.53
  1164.3 233.5 %all-reduce.12.cloned.1.call-done = f32[1024,2048]{1,0:T(8,128)} async-done(((f32[1024,2048]{1,0:T(8,128)}), f32[1024,2048]{1,0:T(8,128)}) %all-reduce.12.cloned.1.call-update) | async-done | bytes 8388624 | tf_op jit(solution)/shard_map/psum | solution.py:208
  1397.8 6.5 fusion.26
  1404.4 25.1 %all-reduce = (f32[2048]{0:T(1024)}, f32[2048]{0:T(1024)}, f32[2,512]{1,0:T(2,128)}, f32[2048]{0:T(1024)}, f32[2048]{0:T(1024)}, /*index=5*/f32[2048]{0:T(1024)}, f32[2048]{0:T(1024)}, f32[2048]{0:T(1024)}) all-reduce(f32[2048]{0:T(1024)S(1)} %get-tuple-element.244, ...), channel_id=1, replica_groups=mesh['dp'=2,'row'=4,'col'=4] {'dp','col'}, use_global_device_ids=true, to_apply=%region_20.21 | all-reduce | flops 15360 | bytes 122880 | tf_op jit(solution)/shard_map/psum | solution.py:218
  1429.6 12.2 fusion.25
  1441.8 51.4 %reduce-scatter.5.cloned.1.call-done = f32[3,256,512]{1,2,0:T(8,128)} async-done(((f32[3,2048,512]{1,2,0:T(8,128)}), f32[3,256,512]{1,2,0:T(8,128)}) %reduce-scatter.5.cloned.1.call-update) | async-done | bytes 1572880 | tf_op jit(solution)/shard_map/reduce_scatter | solution.py:213
  1496.2 52.5 %reduce-scatter.7.cloned.1.call-done = f32[512,256]{1,0:T(8,128)} async-done(((f32[512,2048]{1,0:T(8,128)}), f32[512,256]{1,0:T(8,128)}) %reduce-scatter.7.cloned.1.call-update) | async-done | bytes 524304 | tf_op jit(solution)/shard_map/reduce_scatter | solution.py:214
  1548.7 120.2 %reduce-scatter.9.cloned.1.call-done = f32[256,2048]{1,0:T(8,128)} async-done(((f32[2048,2048]{1,0:T(8,128)}), f32[256,2048]{1,0:T(8,128)}) %reduce-scatter.9.cloned.1.call-update) | async-done | bytes 2097168 | tf_op jit(solution)/shard_map/reduce_scatter | solution.py:215
  1668.8 120.0 %reduce-scatter.11.cloned.1.call-done = f32[2048,256]{1,0:T(8,128)} async-done(((f32[2048,2048]{1,0:T(8,128)}), f32[2048,256]{1,0:T(8,128)}) %reduce-scatter.11.cloned.1.call-update) | async-done | bytes 2097168 | tf_op jit(solution)/shard_map/reduce_scatter | solution.py:216
  (232 shorter events, 127.6 us)
Async XLA Ops:
  7.2 52.7 %copy-start.46 = (f32[2048]{0:T(1024)S(1)}, f32[2048]{0:T(1024)}, u32[]{:S(2)}) copy-start(f32[2048]{0:T(1024)} %param.22) | copy-start | bytes 24580
  7.2 52.7 %copy-start.38 = (f32[2048]{0:T(1024)S(1)}, f32[2048]{0:T(1024)}, u32[]{:S(2)}) copy-start(f32[2048]{0:T(1024)} %param.21) | copy-start | bytes 24580
  7.2 52.7 %all-gather.5.cloned.1.call-start = ((), (), s32[]{:S(2)}) async-start(), calls=%async_computation.4 | async-start | bytes 7077888 | tf_op jit(solution)/shard_map/all_gather | solution.py:143
  9.8 88.9 %all-gather.7.cloned.1.call-start = ((), (), s32[]{:S(2)}) async-start(), calls=%async_computation.5 | async-start | bytes 2359296 | tf_op jit(solution)/shard_map/all_gather | solution.py:144
  11.7 386.1 %all-reduce.6.cloned.1.call-start = ((), (), s32[]{:S(2)}) async-start(), calls=%async_computation.6 | async-start | bytes 16777216 | tf_op jit(solution)/shard_map/psum | solution.py:161
  15.3 44.5 %copy-start.24 = (f32[1024]{0:T(1024)}, f32[1024]{0:T(1024)S(1)}, u32[]{:S(2)}) copy-start(f32[1024]{0:T(1024)S(1)} %broadcast_multiply_fusion.5) | copy-start | bytes 12292
  18.8 41.1 %copy-start.29 = (f32[1024]{0:T(1024)}, f32[1024]{0:T(1024)S(1)}, u32[]{:S(2)}) copy-start(f32[1024]{0:T(1024)S(1)} %add_rsqrt_fusion.1) | copy-start | bytes 12292
  106.8 291.0 %copy-start.40 = (f32[2048]{0:T(1024)S(1)}, f32[2048]{0:T(1024)}, u32[]{:S(2)}) copy-start(f32[2048]{0:T(1024)} %param.26) | copy-start | bytes 24580
  106.8 346.7 %all-gather.9.cloned.1.call-start = ((), (), s32[]{:S(2)}) async-start(), calls=%async_computation.7 | async-start | bytes 9437184 | tf_op jit(solution)/shard_map/all_gather | solution.py:145
  109.6 402.2 %all-gather.11.cloned.1.call-start = ((), (), s32[]{:S(2)}) async-start(), calls=%async_computation.8 | async-start | bytes 9437184 | tf_op jit(solution)/shard_map/all_gather | solution.py:146
  112.3 737.5 %all-reduce.10.cloned.1.call-start = ((), (), s32[]{:S(2)}) async-start(), calls=%async_computation.10 | async-start | bytes 16777216 | tf_op jit(solution)/shard_map/psum | solution.py:180
  403.5 50.0 %copy-start.31 = (f32[2048]{0:T(1024)S(1)}, f32[2048]{0:T(1024)}, u32[]{:S(2)}) copy-start(f32[2048]{0:T(1024)} %param.27) | copy-start | bytes 24580
  403.5 50.0 %copy-start.48 = (f32[2048]{0:T(1024)S(1)}, f32[2048]{0:T(1024)}, u32[]{:S(2)}) copy-start(f32[2048]{0:T(1024)} %param.28) | copy-start | bytes 24580
  403.5 65.9 %copy-start.21 = (f32[1024]{0:T(1024)}, f32[1024]{0:T(1024)S(1)}, u32[]{:S(2)}) copy-start(f32[1024]{0:T(1024)S(1)} %broadcast_multiply_fusion.4) | copy-start | bytes 12292
  408.0 61.4 %copy-start.26 = (f32[1024]{0:T(1024)}, f32[1024]{0:T(1024)S(1)}, u32[]{:S(2)}) copy-start(f32[1024]{0:T(1024)S(1)} %add_rsqrt_fusion) | copy-start | bytes 12292
  408.0 103.8 %copy-start.41 = (f32[2048]{0:T(1024)S(1)}, f32[2048]{0:T(1024)}, u32[]{:S(2)}) copy-start(f32[2048]{0:T(1024)} %param.30) | copy-start | bytes 24580
  511.8 35.7 %copy-start.44 = (bf16[2048,2048]{1,0:T(8,128)(2,1)S(1)}, bf16[2048,2048]{1,0:T(8,128)(2,1)}, u32[]{:S(2)}) copy-start(bf16[2048,2048]{1,0:T(8,128)(2,1)} %all-gather.9.cloned.1.call-done) | copy-start | bytes 25165828
  558.8 447.9 %all-reduce.8.cloned.1.call-start = ((), (), s32[]{:S(2)}) async-start(), calls=%async_computation.9 | async-start | bytes 8388608 | tf_op jit(solution)/shard_map/psum | solution.py:168
  569.1 280.7 %copy-start.22 = (f32[1024]{0:T(1024)S(1)}, f32[1024]{0:T(1024)}, u32[]{:S(2)}) copy-start(f32[1024]{0:T(1024)} %copy-done.21) | copy-start | bytes 12292
  569.1 280.7 %copy-start.27 = (f32[1024]{0:T(1024)S(1)}, f32[1024]{0:T(1024)}, u32[]{:S(2)}) copy-start(f32[1024]{0:T(1024)} %copy-done.26) | copy-start | bytes 12292
  569.2 280.7 %copy-start.32 = (f32[2048]{0:T(1024)S(1)}, f32[2048]{0:T(1024)}, u32[]{:S(2)}) copy-start(f32[2048]{0:T(1024)} %param.27) | copy-start | bytes 24580
  581.8 816.0 %all-reduce.12.cloned.1.call-start = ((), (), s32[]{:S(2)}) async-start(), calls=%async_computation.11 | async-start | bytes 16777216 | tf_op jit(solution)/shard_map/psum | solution.py:208
  583.2 423.6 %copy-start.42 = (f32[2048]{0:T(1024)S(1)}, f32[2048]{0:T(1024)}, u32[]{:S(2)}) copy-start(f32[2048]{0:T(1024)} %param.32) | copy-start | bytes 24580
  1107.8 385.3 %reduce-scatter.5.cloned.1.call-start = ((), (), s32[]{:S(2)}) async-start(), calls=%async_computation.12 | async-start | bytes 14155776 | tf_op jit(solution)/shard_map/reduce_scatter | solution.py:213
  1121.8 426.8 %reduce-scatter.7.cloned.1.call-start = ((), (), s32[]{:S(2)}) async-start(), calls=%async_computation.13 | async-start | bytes 4718592 | tf_op jit(solution)/shard_map/reduce_scatter | solution.py:214
  1130.8 538.0 %reduce-scatter.9.cloned.1.call-start = ((), (), s32[]{:S(2)}) async-start(), calls=%async_computation.14 | async-start | bytes 18874368 | tf_op jit(solution)/shard_map/reduce_scatter | solution.py:215
  1147.3 641.5 %reduce-scatter.11.cloned.1.call-start = ((), (), s32[]{:S(2)}) async-start(), calls=%async_computation.15 | async-start | bytes 18874368 | tf_op jit(solution)/shard_map/reduce_scatter | solution.py:216
  1164.1 240.3 %copy-start.34 = (f32[2048]{0:T(1024)S(1)}, f32[2048]{0:T(1024)}, u32[]{:S(2)}) copy-start(f32[2048]{0:T(1024)} %get-tuple-element.242) | copy-start | bytes 24580
  1164.1 240.3 %copy-start.35 = (f32[2048]{0:T(1024)S(1)}, f32[2048]{0:T(1024)}, u32[]{:S(2)}) copy-start(f32[2048]{0:T(1024)} %get-tuple-element.248) | copy-start | bytes 24580
  1164.1 240.3 %copy-start.36 = (f32[2048]{0:T(1024)S(1)}, f32[2048]{0:T(1024)}, u32[]{:S(2)}) copy-start(f32[2048]{0:T(1024)} %get-tuple-element.303) | copy-start | bytes 24580
  1164.1 240.3 %copy-start.37 = (f32[2048]{0:T(1024)S(1)}, f32[2048]{0:T(1024)}, u32[]{:S(2)}) copy-start(f32[2048]{0:T(1024)} %get-tuple-element.318) | copy-start | bytes 24580
  1164.1 240.3 %copy-start.43 = (f32[2048]{0:T(1024)S(1)}, f32[2048]{0:T(1024)}, u32[]{:S(2)}) copy-start(f32[2048]{0:T(1024)} %get-tuple-element.300) | copy-start | bytes 24580
  (39 other events, 181.3 us)
Sparse Core Ops, SparseCore 0:
  10.5 49.3 all-gather.4
  62.3 28.1 all-gather.6
  106.9 290.8 all-reduce.5
  400.1 53.3 all-gather.8
  455.8 55.9 all-gather.10
  559.0 290.8 all-reduce.9
  852.8 153.9 all-reduce.7
  1108.0 289.8 all-reduce.11
  1401.7 91.3 reduce-scatter.4
  1497.3 51.2 reduce-scatter.6
  1552.8 115.9 reduce-scatter.8
  1672.8 115.9 reduce-scatter.10
where the time goes:
time: 1800 us
  waiting for transfers between devices  1410 us (78%)
  matrix products  213 us (12%)
  other arithmetic  91 us (5%)
  local copies, waits for them, and re-layouts  40.2 us (2%)
  blocking collectives  25.1 us (1%)
    psum x1, waiting for transfers between devices, local(): hidden = source + lax.psum(attn_partial, 'row') + b_out  285 us
    psum x1, waiting for transfers between devices, local(): grad_normed2 = lax.psum(norm2_partial, 'row')  267 us
    psum x1, waiting for transfers between devices, local(): grad_normed1 = lax.psum(norm1_partial, 'row')  233 us
    psum x1, waiting for transfers between devices, local(): lax.psum(mlp_partial.astype(jnp.bfloat16), 'row').astype(jnp.float32)  149 us
    reduce_scatter x1, waiting for transfers between devices, local(): lax.psum_scatter(grad_win, ('dp', 'col'), scatter_dimension=0, tiled=True)  120 us
    reduce_scatter x1, waiting for transfers between devices, local(): lax.psum_scatter(grad_wdown, ('dp', 'col'), scatter_dimension=1, tiled=True)  120 us
    reduce_scatter x1, waiting for transfers between devices, local(): lax.psum_scatter(grad_wout, ('dp', 'col'), scatter_dimension=1, tiled=True)  52.5 us
    reduce_scatter x1, waiting for transfers between devices, local(): lax.psum_scatter(grad_wqkv, ('dp', 'col'), scatter_dimension=1, tiled=True)  51.4 us
  transfers between devices with their start and end apart: 12, of which 11 were waited for; matrix products, arithmetic and copies ran while one was open for 10% of the time, Pallas kernels for 0%

commit v1 on v0

--- a/solution.py
+++ b/solution.py
@@ -114,6 +114,12 @@
         d_keys.reshape(length, width).astype(jnp.bfloat16),
         d_values.reshape(length, width).astype(jnp.bfloat16),
     )
+
+
+def scatter_low(grad, dim):
+    low = grad.astype(jnp.bfloat16)
+    summed = lax.psum_scatter(low, ("dp", "col"), scatter_dimension=dim, tiled=True)
+    return summed.astype(jnp.float32)
 
 
 def local(
@@ -158,7 +164,7 @@
     context, maxima, totals = attend_forward(queries, keys_low, values_low, prefix, block_rows)
     context_low = context.astype(jnp.bfloat16)
     attn_partial = jnp.dot(context_low, full_out, preferred_element_type=jnp.float32)
-    hidden = source + lax.psum(attn_partial, "row") + b_out
+    hidden = source + lax.psum(attn_partial.astype(jnp.bfloat16), "row").astype(jnp.float32) + b_out
     normed2, scaled2, inverse2 = norm_forward(hidden, norm2_gain, norm2_shift)
     normed2_low = normed2.astype(jnp.bfloat16)
     pre_act = jnp.dot(normed2_low, full_in, preferred_element_type=jnp.float32) + b_in
@@ -177,7 +183,7 @@
     grad_bin = jnp.sum(grad_pre.astype(jnp.float32), axis=0)
     grad_win = jnp.einsum("td,tf->df", normed2_low, grad_pre, preferred_element_type=jnp.float32)
     norm2_partial = jnp.einsum("tf,df->td", grad_pre, full_in, preferred_element_type=jnp.float32)
-    grad_normed2 = lax.psum(norm2_partial, "row")
+    grad_normed2 = lax.psum(norm2_partial.astype(jnp.bfloat16), "row").astype(jnp.float32)
     grad_gain2 = jnp.sum(grad_normed2 * scaled2, axis=0)
     grad_shift2 = jnp.sum(grad_normed2, axis=0)
     grad_hidden = grad_top + norm_backward(grad_normed2, scaled2, inverse2, norm2_gain)
@@ -205,15 +211,15 @@
     norm1_partial = jnp.einsum(
         "ctn,cdn->td", grad_projected, full_qkv, preferred_element_type=jnp.float32
     )
-    grad_normed1 = lax.psum(norm1_partial, "row")
+    grad_normed1 = lax.psum(norm1_partial.astype(jnp.bfloat16), "row").astype(jnp.float32)
     grad_gain1 = jnp.sum(grad_normed1 * scaled1, axis=0)
     grad_shift1 = jnp.sum(grad_normed1, axis=0)
     d_inputs = grad_hidden + norm_backward(grad_normed1, scaled1, inverse1, norm1_gain)
     sent_wqkv, sent_wout, sent_win, sent_wdown = (
-        lax.psum_scatter(grad_wqkv, ("dp", "col"), scatter_dimension=1, tiled=True),
-        lax.psum_scatter(grad_wout, ("dp", "col"), scatter_dimension=1, tiled=True),
-        lax.psum_scatter(grad_win, ("dp", "col"), scatter_dimension=0, tiled=True),
-        lax.psum_scatter(grad_wdown, ("dp", "col"), scatter_dimension=1, tiled=True),
+        scatter_low(grad_wqkv, 1),
+        scatter_low(grad_wout, 1),
+        scatter_low(grad_win, 0),
+        scatter_low(grad_wdown, 1),
     )
     small = lax.psum(
         (

time: 1800 us -> 1170 us (0.65)
  waiting for transfers between devices: 1410 us -> 803 us
  matrix products: 213 us -> 188 us
    psum x3 -> x2, waiting for transfers between devices: 785 us -> 305 us  [the longest x1 155 us: local(): lax.psum(norm2_partial.astype(jnp.bfloat16), 'row').astype(jnp.float32)]
    reduce_scatter x4, waiting for transfers between devices: 344 us -> 75.1 us  [scatter_low(): lax.psum_scatter(low, ('dp', 'col'), scatter_dimension=dim, tiled=True)]
    psum x1, waiting for transfers between devices: 149 us -> 292 us  [local(): lax.psum(mlp_partial.astype(jnp.bfloat16), 'row').astype(jnp.float32)]
  transfers between devices with their start and end apart: 12 -> 11, of which waited for: 11 -> 8; matrix products, arithmetic and copies ran while one was open for 10% -> 19% of each run, Pallas kernels for 0% -> 0%
where the time goes in v1:
time: 1170 us; the launch traced here: 1160 us
  waiting for transfers between devices  803 us (69%)
  matrix products  188 us (16%)
  other arithmetic  92.7 us (8%)
  local copies, waits for them, and re-layouts  35 us (3%)
  blocking collectives  25.3 us (2%)
  between operations  14.5 us (1%)
    psum x1, waiting for transfers between devices, local(): lax.psum(mlp_partial.astype(jnp.bfloat16), 'row').astype(jnp.float32)  292 us
    psum x1, waiting for transfers between devices, local(): lax.psum(norm2_partial.astype(jnp.bfloat16), 'row').astype(jnp.float32)  155 us
    psum x1, waiting for transfers between devices, local(): lax.psum(attn_partial.astype(jnp.bfloat16), 'row').astype(jnp.float32)  150 us
    reduce_scatter x4, waiting for transfers between devices, scatter_low(): lax.psum_scatter(low, ('dp', 'col'), scatter_dimension=dim, tiled=True)  75.1 us
    all_gather x1, waiting for transfers between devices, local(): lax.all_gather(low_mats[2], ('dp', 'col'), axis=0, tiled=True)  47.3 us
    all_gather x1, waiting for transfers between devices, local(): lax.all_gather(low_mats[3], ('dp', 'col'), axis=1, tiled=True)  42.2 us
    all_gather x1, waiting for transfers between devices, local(): lax.all_gather(low_mats[0], ('dp', 'col'), axis=1, tiled=True)  41.7 us
    dot_general x1, matrix products, local(): jnp.einsum('td,fd->tf', d_output, full_down, preferred_element_type=jnp.f...  33.7 us
  transfers between devices with their start and end apart: 11, of which 8 were waited for; matrix products, arithmetic and copies ran while one was open for 19% of the time, Pallas kernels for 0%

profile of v1, /device:TPU:0, one launch (start us, length us, event | category | flops | bytes accessed | tf_op | source)
XLA Modules:
  0.0 1162.4 jit_solution(7180135684275567967)
XLA Ops:
  14.6 3.4 fusion.29
  18.2 41.7 %all-gather.5.cloned.1.call-done = bf16[3,2048,512]{1,2,0:T(8,128)(2,1)} async-done(((bf16[3,256,512]{1,2,0:T(8,128)(2,1)}), bf16[3,2048,512]{1,2,0:T(8,128)(2,1)}) %all-gather.5.cloned.1.call-update) | async-done | bytes 6291472 | tf_op jit(solution)/shard_map/all_gather | solution.py:149
  59.9 11.6 fusion.44
  76.5 22.6 %while.31 = (s32[]{:T(128)}, bf16[2,512,512]{2,1,0:T(8,128)(2,1)}, f32[2,4,512]{2,1,0:T(4,128)S(1)}, f32[2,4,512]{2,1,0:T(4,128)S(1)}, s32[2]{0:T(128)S(1)}, /*i...) while((s32[]{:T(128)}, bf16[2,512,512]{2,1,0:T(8,128)(2,1)}, ...), condition=%wide.wide.region_5.6_spmd, body=%wide.wide.region_2.5_spmd.sunk | while | flops 1099953664 | bytes 37828856 | solution.py:67
  99.1 6.6 convolution_convert_fusion.4
  111.4 149.5 %all-reduce.6.cloned.1.call-done = bf16[1024,2048]{1,0:T(8,128)(2,1)} async-done(((bf16[1024,2048]{1,0:T(8,128)(2,1)}), bf16[1024,2048]{1,0:T(8,128)(2,1)}) %all-reduce.6.cloned.1.call-update) | async-done | bytes 4194320 | tf_op jit(solution)/shard_map/psum | solution.py:167
  260.9 5.0 fusion.45
  269.4 47.3 %all-gather.9.cloned.1.call-done = bf16[2048,2048]{1,0:T(8,128)(2,1)} async-done(((bf16[256,2048]{1,0:T(8,128)(2,1)}), bf16[2048,2048]{1,0:T(8,128)(2,1)}) %all-gather.9.cloned.1.call-update) | async-done | bytes 8388624 | tf_op jit(solution)/shard_map/all_gather | solution.py:151
  316.8 16.2 %fusion.52 = f32[1024,2048]{1,0:T(8,128)} fusion(bf16[2048,2048]{1,0:T(8,128)(2,1)} %all-gather.9.cloned.1.call-done, f32[2048]{0:T(1024)S(1)} %copy-done.42, f32[2048]{0:T(1024)S(1)} %copy-done.29, f32[1024]{0:T(1024)S(1)} %add_rsqrt_fusion, f32[1024]{0:T(1024)S(1)} %broadcast_multiply_fusion.4, f32[2048]{0:T(1024)S(1)} %copy-done.19, ...), kind=kOutput, calls=%fused_computation.124 | convolution fusion | flops 8608808960 | bytes 25198592 | tf_op jit(solution)/shard_map/dot_general | solution.py:170
  333.0 42.2 %all-gather.11.cloned.1.call-done = bf16[2048,2048]{1,0:T(8,128)(2,1)} async-done(((bf16[2048,256]{1,0:T(8,128)(2,1)}), bf16[2048,2048]{1,0:T(8,128)(2,1)}) %all-gather.11.cloned.1.call-update) | async-done | bytes 8388624 | tf_op jit(solution)/shard_map/all_gather | solution.py:152
  375.2 33.7 %convert_reduce_fusion.4 = (f32[2048]{0:T(1024)}, bf16[1024,2048]{1,0:T(8,128)(2,1)S(1)}, f32[1024,2048]{1,0:T(8,128)}) fusion(f32[1024,2048]{1,0:T(8,128)} %fusion.52, f32[2048]{0:T(1024)S(1)} %copy-done.36, bf16[1024,2048]{1,0:T(8,128)(2,1)} %param.33, bf16[2048,2048]{1,0:T(8,128)(2,1)} %all-gather.11.cloned.1.call-done), kind=kOutput, calls=%fused_computation.73 | convolution fusion | flops 8747218944 | bytes 33570816 | tf_op jit(solution)/shard_map/td,fd->tf/dot_general | solution.py:181
  411.0 10.8 convolution_convert_fusion.2
  421.9 155.1 %all-reduce.8.cloned.1.call-done = bf16[1024,2048]{1,0:T(8,128)(2,1)} async-done(((bf16[1024,2048]{1,0:T(8,128)(2,1)}), bf16[1024,2048]{1,0:T(8,128)(2,1)}) %all-reduce.8.cloned.1.call-update) | async-done | bytes 4194320 | tf_op jit(solution)/shard_map/psum | solution.py:186
  577.0 10.3 fusion.36
  587.3 8.6 convert_reduce_fusion.5
  599.1 3.8 convolution_convert_fusion.5
  603.0 15.6 %convolution_convert_fusion.1 = bf16[2048,2048]{1,0:T(8,128)(2,1)} fusion(bf16[1024,2048]{1,0:T(8,128)(2,1)} %copy-done.45, f32[2048]{0:T(1024)S(1)} %copy-done.42, f32[2048]{0:T(1024)S(1)} %copy-done.29, f32[1024]{0:T(1024)S(1)} %add_rsqrt_fusion, f32[1024]{0:T(1024)S(1)} %broadcast_multiply_fusion.4, f32[2048]{0:T(1024)S(1)} %copy-done.19, ...), kind=kOutput, calls=%fused_computation.95 | convolution fusion | flops 8613003264 | bytes 21004288 | tf_op jit(solution)/shard_map/td,tf->df/dot_general | solution.py:184
  621.1 10.3 multiply_convert_fusion.1
  631.4 14.0 %convolution_convert_fusion = bf16[2048,2048]{1,0:T(8,128)(2,1)} fusion(bf16[1024,2048]{1,0:T(8,128)(2,1)} %multiply_convert_fusion.1, bf16[1024,2048]{1,0:T(8,128)(2,1)} %param.33), kind=kOutput, calls=%fused_computation.94 | convolution fusion | flops 8594128896 | bytes 16777216 | tf_op jit(solution)/shard_map/tf,td->fd/dot_general | solution.py:178
  645.6 14.0 %convolution_convert_fusion.3 = bf16[1024,2048]{1,0:T(8,128)(2,1)} fusion(bf16[1024,2048]{1,0:T(8,128)(2,1)} %multiply_convert_fusion.1, bf16[2048,2048]{1,0:T(8,128)(2,1)} %all-gather.11.cloned.1.call-done), kind=kOutput, calls=%fused_computation.100 | convolution fusion | flops 8592031744 | bytes 16777216 | tf_op jit(solution)/shard_map/dot_general | solution.py:173
  659.5 7.9 convolution_convert_fusion.6
  667.5 35.6 %while.30 = (s32[]{:T(128)}, f32[1024,4,128]{0,2,1:T(8,128)S(1)}, f32[1024,4,128]{0,2,1:T(8,128)}, bf16[2,512,512]{1,2,0:T(8,128)(2,1)}, s32[2]{0:T(128)S(1)}, /...) while((s32[]{:T(128)}, f32[1024,4,128]{0,2,1:T(8,128)S(1)}, ...), condition=%wide.region_15.16_spmd.clone, body=%wide.region_13.15_spmd.clone.sunk | while | flops 2709519872 | bytes 115939768 | solution.py:109
  673.5 4.2 exponential_divide_fusion.2
  691.1 4.2 exponential_divide_fusion.2
  708.5 11.4 bitcast_convert_fusion
  720.6 12.0 %convert_bitcast_fusion = bf16[3,2048,512]{1,2,0:T(8,128)(2,1)} fusion(bf16[1,1024,512]{2,1,0:T(8,128)(2,1)} %copy.67, bf16[1,1024,512]{2,1,0:T(8,128)(2,1)S(1)} %copy.66, bf16[1,1024,512]{2,1,0:T(8,128)(2,1)S(1)} %bitcast.139, bf16[1024,2048]{1,0:T(8,128)(2,1)} %param.19, f32[2048]{0:T(1024)S(1)} %copy-done.44, f32[2048]{0:T(1024)S(1)} %copy-done.31, ...), kind=kOutput, calls=%fused_computation.96 | convolution fusion | flops 6461325312 | bytes 13656064 | tf_op jit(solution)/shard_map/td,ctn->cdn/dot_general | solution.py:208
  737.8 56.0 %reduce-scatter.11.cloned.1.call-done = bf16[2048,256]{1,0:T(8,128)(2,1)} async-done(((bf16[2048,2048]{1,0:T(8,128)(2,1)}), bf16[2048,256]{1,0:T(8,128)(2,1)}) %reduce-scatter.11.cloned.1.call-update) | async-done | bytes 1048592 | tf_op jit(solution)/shard_map/reduce_scatter | solution.py:121
  796.5 292.0 %all-reduce.10.cloned.1.call-done = (bf16[1024,2048]{1,0:T(8,128)(2,1)}, bf16[1024,2048]{1,0:T(8,128)(2,1)}) async-done(((bf16[1024,2048]{1,0:T(8,128)(2,1)}, bf16[1024,2048]{1,0:T(8,128)(2,1)}), (bf16[1024,2048]{1,0:T(8,128)(2,1)}, bf16[1024,2048]{1,0:T(8,128)(2,1)})) %all-reduce.10.cloned.1.call-update) | async-done | bytes 8388624 | tf_op jit(solution)/shard_map/psum | solution.py:174
  1088.6 6.2 fusion.37
  1094.9 25.3 %all-reduce = (f32[2048]{0:T(1024)}, f32[2048]{0:T(1024)}, f32[2,512]{1,0:T(2,128)}, f32[2048]{0:T(1024)}, f32[2048]{0:T(1024)}, /*index=5*/f32[2048]{0:T(1024)}, f32[2048]{0:T(1024)}, f32[2048]{0:T(1024)}) all-reduce(f32[2048]{0:T(1024)S(1)} %get-tuple-element.244, ...), channel_id=1, replica_groups=mesh['dp'=2,'row'=4,'col'=4] {'dp','col'}, use_global_device_ids=true, to_apply=%region_20.21 | all-reduce | flops 15360 | bytes 122880 | tf_op jit(solution)/shard_map/psum | solution.py:224
  1120.2 14.0 %fusion.28 = (f32[1024,2048]{1,0:T(8,128)}, bf16[1024,2048]{1,0:T(8,128)(2,1)}) fusion(f32[1024,2048]{1,0:T(8,128)} %copy-done.6, bf16[1024,2048]{1,0:T(8,128)(2,1)} %param.19, bf16[1024,2048]{1,0:T(8,128)(2,1)} %get-tuple-element.301, f32[1024]{0:T(1024)S(1)} %broadcast_multiply_fusion, f32[1024]{0:T(1024)S(1)} %broadcast_multiply_fusion.1, ...), kind=kLoop, calls=%fused_computation.62 | loop fusion | flops 35651584 | bytes 37789696 | tf_op jit(solution)/shard_map/add | solution.py:217
  1134.1 19.1 %reduce-scatter.5.cloned.1.call-done = bf16[3,256,512]{1,2,0:T(8,128)(2,1)} async-done(((bf16[3,2048,512]{1,2,0:T(8,128)(2,1)}), bf16[3,256,512]{1,2,0:T(8,128)(2,1)}) %reduce-scatter.5.cloned.1.call-update) | async-done | bytes 786448 | tf_op jit(solution)/shard_map/reduce_scatter | solution.py:121
  (220 shorter events, 92.4 us)
Async XLA Ops:
  7.2 10.8 copy-start.39
  7.2 52.7 %copy-start.30 = (f32[2048]{0:T(1024)S(1)}, f32[2048]{0:T(1024)}, u32[]{:S(2)}) copy-start(f32[2048]{0:T(1024)} %param.21) | copy-start | bytes 24580
  7.2 52.7 %copy-start.43 = (f32[2048]{0:T(1024)S(1)}, f32[2048]{0:T(1024)}, u32[]{:S(2)}) copy-start(f32[2048]{0:T(1024)} %param.22) | copy-start | bytes 24580
  7.2 52.7 %all-gather.5.cloned.1.call-start = ((), (), s32[]{:S(2)}) async-start(), calls=%async_computation.4 | async-start | bytes 7077888 | tf_op jit(solution)/shard_map/all_gather | solution.py:149
  9.8 89.2 %all-gather.7.cloned.1.call-start = ((), (), s32[]{:S(2)}) async-start(), calls=%async_computation.5 | async-start | bytes 2359296 | tf_op jit(solution)/shard_map/all_gather | solution.py:150
  11.7 249.2 %all-reduce.6.cloned.1.call-start = ((), (), s32[]{:S(2)}) async-start(), calls=%async_computation.6 | async-start | bytes 8388608 | tf_op jit(solution)/shard_map/psum | solution.py:167
  14.6 45.3 %copy-start.25 = (f32[1024]{0:T(1024)}, f32[1024]{0:T(1024)S(1)}, u32[]{:S(2)}) copy-start(f32[1024]{0:T(1024)S(1)} %broadcast_multiply_fusion.5) | copy-start | bytes 12292
  18.0 41.9 %copy-start.27 = (f32[1024]{0:T(1024)}, f32[1024]{0:T(1024)S(1)}, u32[]{:S(2)}) copy-start(f32[1024]{0:T(1024)S(1)} %add_rsqrt_fusion.1) | copy-start | bytes 12292
  105.7 155.2 %copy-start.19 = (f32[2048]{0:T(1024)S(1)}, f32[2048]{0:T(1024)}, u32[]{:S(2)}) copy-start(f32[2048]{0:T(1024)} %param.26) | copy-start | bytes 24580
  105.7 211.0 %all-gather.9.cloned.1.call-start = ((), (), s32[]{:S(2)}) async-start(), calls=%async_computation.7 | async-start | bytes 9437184 | tf_op jit(solution)/shard_map/all_gather | solution.py:151
  108.5 266.7 %all-gather.11.cloned.1.call-start = ((), (), s32[]{:S(2)}) async-start(), calls=%async_computation.8 | async-start | bytes 9437184 | tf_op jit(solution)/shard_map/all_gather | solution.py:152
  111.3 205.5 %copy-start.29 = (f32[2048]{0:T(1024)S(1)}, f32[2048]{0:T(1024)}, u32[]{:S(2)}) copy-start(f32[2048]{0:T(1024)} %param.27) | copy-start | bytes 24580
  111.3 205.5 %copy-start.42 = (f32[2048]{0:T(1024)S(1)}, f32[2048]{0:T(1024)}, u32[]{:S(2)}) copy-start(f32[2048]{0:T(1024)} %param.28) | copy-start | bytes 24580
  111.3 465.6 %all-reduce.8.cloned.1.call-start = ((), (), s32[]{:S(2)}) async-start(), calls=%async_computation.9 | async-start | bytes 8388608 | tf_op jit(solution)/shard_map/psum | solution.py:186
  269.4 105.8 %copy-start.36 = (f32[2048]{0:T(1024)S(1)}, f32[2048]{0:T(1024)}, u32[]{:S(2)}) copy-start(f32[2048]{0:T(1024)} %param.30) | copy-start | bytes 24580
  375.2 35.8 %copy-start.40 = (bf16[2048,2048]{1,0:T(8,128)(2,1)S(1)}, bf16[2048,2048]{1,0:T(8,128)(2,1)}, u32[]{:S(2)}) copy-start(bf16[2048,2048]{1,0:T(8,128)(2,1)} %all-gather.9.cloned.1.call-done) | copy-start | bytes 25165828
  421.8 311.2 %reduce-scatter.7.cloned.1.call-start = ((), (), s32[]{:S(2)}) async-start(), calls=%async_computation.11 | async-start | bytes 2359296 | tf_op jit(solution)/shard_map/reduce_scatter | solution.py:121
  577.0 10.3 copy-start.9
  587.3 11.8 %copy-start.18 = (bf16[2,512,512]{2,1,0:T(8,128)(2,1)S(1)}, bf16[2,512,512]{2,1,0:T(8,128)(2,1)}, u32[]{:S(2)}) copy-start(bf16[2,512,512]{2,1,0:T(8,128)(2,1)} %get-tuple-element.127) | copy-start | bytes 3145732
  602.9 131.9 %reduce-scatter.9.cloned.1.call-start = ((), (), s32[]{:S(2)}) async-start(), calls=%async_computation.12 | async-start | bytes 9437184 | tf_op jit(solution)/shard_map/reduce_scatter | solution.py:121
  618.6 175.3 %reduce-scatter.11.cloned.1.call-start = ((), (), s32[]{:S(2)}) async-start(), calls=%async_computation.13 | async-start | bytes 9437184 | tf_op jit(solution)/shard_map/reduce_scatter | solution.py:121
  645.5 443.1 %all-reduce.10.cloned.1.call-start = ((), (), s32[]{:S(2)}) async-start(), calls=%async_computation.14 | async-start | bytes 16777216 | tf_op jit(solution)/shard_map/psum | solution.py:174
  645.5 14.0 %copy-start.41 = (bf16[512,2048]{1,0:T(8,128)(2,1)S(1)}, bf16[512,2048]{1,0:T(8,128)(2,1)}, u32[]{:S(2)}) copy-start(bf16[512,2048]{1,0:T(8,128)(2,1)} %all-gather.7.cloned.1.call-done) | copy-start | bytes 6291460
  719.9 12.7 %copy-start.12 = (bf16[2,512,512]{1,2,0:T(8,128)(2,1)S(1)}, bf16[2,512,512]{1,2,0:T(8,128)(2,1)}, u32[]{:S(2)}) copy-start(bf16[2,512,512]{1,2,0:T(8,128)(2,1)} %get-tuple-element.649) | copy-start | bytes 3145732
  720.0 433.2 %reduce-scatter.5.cloned.1.call-start = ((), (), s32[]{:S(2)}) async-start(), calls=%async_computation.10 | async-start | bytes 7077888 | tf_op jit(solution)/shard_map/reduce_scatter | solution.py:121
  732.7 362.1 %copy-start.32 = (f32[2048]{0:T(1024)S(1)}, f32[2048]{0:T(1024)}, u32[]{:S(2)}) copy-start(f32[2048]{0:T(1024)} %get-tuple-element.242) | copy-start | bytes 24580
  732.7 362.1 %copy-start.33 = (f32[2048]{0:T(1024)S(1)}, f32[2048]{0:T(1024)}, u32[]{:S(2)}) copy-start(f32[2048]{0:T(1024)} %get-tuple-element.248) | copy-start | bytes 24580
  732.7 362.1 %copy-start.34 = (f32[2048]{0:T(1024)S(1)}, f32[2048]{0:T(1024)}, u32[]{:S(2)}) copy-start(f32[2048]{0:T(1024)} %get-tuple-element.305) | copy-start | bytes 24580
  732.7 362.1 %copy-start.35 = (f32[2048]{0:T(1024)S(1)}, f32[2048]{0:T(1024)}, u32[]{:S(2)}) copy-start(f32[2048]{0:T(1024)} %get-tuple-element.317) | copy-start | bytes 24580
  732.7 362.1 %copy-start.38 = (f32[2048]{0:T(1024)S(1)}, f32[2048]{0:T(1024)}, u32[]{:S(2)}) copy-start(f32[2048]{0:T(1024)} %get-tuple-element.302) | copy-start | bytes 24580
  732.7 387.4 %copy-start.20 = (f32[2048]{0:T(1024)S(1)}, f32[2048]{0:T(1024)}, u32[]{:S(2)}) copy-start(f32[2048]{0:T(1024)} %param.26) | copy-start | bytes 24580
  732.8 387.4 %copy-start.37 = (f32[2048]{0:T(1024)S(1)}, f32[2048]{0:T(1024)}, u32[]{:S(2)}) copy-start(f32[2048]{0:T(1024)} %param.32) | copy-start | bytes 24580
  (32 other events, 127.4 us)
Sparse Core Ops, SparseCore 0:
  10.5 49.3 all-gather.4
  62.3 28.2 all-gather.6
  105.9 154.9 all-reduce.5
  263.3 53.3 all-gather.8
  319.2 55.9 all-gather.10
  422.0 154.9 all-reduce.7
  603.0 40.2 reduce-scatter.6
  647.2 71.2 reduce-scatter.8
  722.6 71.2 reduce-scatter.10
  797.0 291.5 all-reduce.9
  1092.4 60.7 reduce-scatter.4

commit v2 on v1

--- a/solution.py
+++ b/solution.py
@@ -3,9 +3,14 @@
 import jax
 import jax.numpy as jnp
 from jax import lax
+from jax.experimental import pallas as pl
+from jax.experimental.pallas import tpu as pltpu
 from jax.sharding import PartitionSpec as P
 
 HEAD_DIM = 128
+MESH_IDS = pl.DeviceIdType.MESH
+CHUNK = 32
+LAG = 2
 
 
 eps_norm = 1e-05
@@ -114,6 +119,142 @@
         d_keys.reshape(length, width).astype(jnp.bfloat16),
         d_values.reshape(length, width).astype(jnp.bfloat16),
     )
+
+
+def sum_row_kernel(n, p_ref, o_ref, held, rs_s, rs_r, ag_s, ag_r, loc):
+    half = p_ref.shape[0] // 2
+    chunks = half // CHUNK
+    r = lax.axis_index("row")
+    last = n - 1
+    bar = pltpu.get_barrier_semaphore()
+    for cond, dev in ((r > 0, r - 1), (r < last, r + 1)):
+
+        @pl.when(cond)
+        def _():
+            pl.semaphore_signal(bar, inc=1, device_id={"row": dev}, device_id_type=MESH_IDS)
+
+    inside = (r > 0) & (r < last)
+
+    @pl.when(inside)
+    def _():
+        pl.semaphore_wait(bar, 2)
+
+    @pl.when(jnp.logical_not(inside))
+    def _():
+        pl.semaphore_wait(bar, 1)
+
+    place = (r, last - r)
+    after = (jnp.minimum(r + 1, last), jnp.maximum(r - 1, 0))
+    before = (jnp.maximum(r - 1, 0), jnp.minimum(r + 1, last))
+
+    def rows(d, c):
+        return pl.ds(pl.multiple_of((half if d == 0 else 0) + c * CHUNK, CHUNK), CHUNK)
+
+    def onward(d, c, src):
+        return pltpu.make_async_remote_copy(
+            src_ref=src.at[rows(d, c)],
+            dst_ref=held.at[rows(d, c)],
+            send_sem=rs_s.at[d, c],
+            recv_sem=rs_r.at[d, c],
+            device_id={"row": after[d]},
+            device_id_type=MESH_IDS,
+        )
+
+    def back(d, c, src):
+        return pltpu.make_async_remote_copy(
+            src_ref=src.at[rows(d, c)],
+            dst_ref=o_ref.at[rows(d, c)],
+            send_sem=ag_s.at[d, c],
+            recv_sem=ag_r.at[d, c],
+            device_id={"row": before[d]},
+            device_id_type=MESH_IDS,
+        )
+
+    def keep(d, c):
+        return pltpu.make_async_copy(held.at[rows(d, c)], o_ref.at[rows(d, c)], loc.at[c])
+
+    def step(t, carry):
+        for d in (0, 1):
+
+            @pl.when((place[d] == 0) & (t < chunks))
+            def _():
+                onward(d, t, p_ref).start()
+
+            c = t - LAG * place[d]
+
+            @pl.when((place[d] > 0) & (c >= 0) & (c < chunks))
+            def _():
+                onward(d, c, p_ref).wait_recv()
+                here = rows(d, c)
+                held[here] = (
+                    held[here].astype(jnp.float32) + p_ref[here].astype(jnp.float32)
+                ).astype(jnp.bfloat16)
+
+                @pl.when(place[d] < last)
+                def _():
+                    onward(d, c, held).start()
+
+                @pl.when(place[d] == last)
+                def _():
+                    back(d, c, held).start()
+                    keep(d, c).start()
+
+        for d in (0, 1):
+            c = t - LAG * (2 * last - place[d])
+
+            @pl.when((place[d] < last) & (c >= 0) & (c < chunks))
+            def _():
+                back(d, c, o_ref).wait_recv()
+
+                @pl.when(place[d] > 0)
+                def _():
+                    back(d, c, o_ref).start()
+
+        return carry
+
+    lax.fori_loop(0, chunks + LAG * 2 * last, step, 0)
+
+    def drain(c, carry):
+        for d in (0, 1):
+
+            @pl.when(place[d] < last)
+            def _():
+                onward(d, c, p_ref).wait_send()
+
+            @pl.when(place[d] > 0)
+            def _():
+                back(d, c, o_ref).wait_send()
+
+            @pl.when(place[d] == last)
+            def _():
+                keep(d, c).wait()
+
+        return carry
+
+    lax.fori_loop(0, chunks, drain, 0)
+
+
+def sum_row(partial_low, collective_id):
+    n = lax.axis_size("row")
+    chunks = partial_low.shape[0] // 2 // CHUNK
+    dma = pltpu.SemaphoreType.DMA
+    return pl.pallas_call(
+        partial(sum_row_kernel, n),
+        out_shape=jax.ShapeDtypeStruct(partial_low.shape, partial_low.dtype),
+        in_specs=[pl.BlockSpec(memory_space=pltpu.VMEM)],
+        out_specs=pl.BlockSpec(memory_space=pl.ANY),
+        scratch_shapes=[
+            pltpu.VMEM(partial_low.shape, partial_low.dtype),
+            dma((2, chunks)),
+            dma((2, chunks)),
+            dma((2, chunks)),
+            dma((2, chunks)),
+            dma((chunks,)),
+        ],
+        compiler_params=pltpu.CompilerParams(
+            collective_id=collective_id, has_side_effects=True, vmem_limit_bytes=16 * 2**20
+        ),
+    )(partial_low)
 
 
 def scatter_low(grad, dim):
@@ -164,14 +305,14 @@
     context, maxima, totals = attend_forward(queries, keys_low, values_low, prefix, block_rows)
     context_low = context.astype(jnp.bfloat16)
     attn_partial = jnp.dot(context_low, full_out, preferred_element_type=jnp.float32)
-    hidden = source + lax.psum(attn_partial.astype(jnp.bfloat16), "row").astype(jnp.float32) + b_out
+    hidden = source + sum_row(attn_partial.astype(jnp.bfloat16), 0).astype(jnp.float32) + b_out
     normed2, scaled2, inverse2 = norm_forward(hidden, norm2_gain, norm2_shift)
     normed2_low = normed2.astype(jnp.bfloat16)
     pre_act = jnp.dot(normed2_low, full_in, preferred_element_type=jnp.float32) + b_in
     activated, gelu_pull = jax.vjp(partial(jax.nn.gelu, approximate=False), pre_act)
     activated_low = activated.astype(jnp.bfloat16)
     mlp_partial = jnp.dot(activated_low, full_down, preferred_element_type=jnp.float32)
-    result = hidden + lax.psum(mlp_partial.astype(jnp.bfloat16), "row").astype(jnp.float32) + b_down
+    result = hidden + sum_row(mlp_partial.astype(jnp.bfloat16), 1).astype(jnp.float32) + b_down
     output = result.astype(jnp.bfloat16)
     grad_top = d_output.astype(jnp.float32)
     grad_bdown = jnp.sum(grad_top, axis=0)
@@ -183,7 +324,7 @@
     grad_bin = jnp.sum(grad_pre.astype(jnp.float32), axis=0)
     grad_win = jnp.einsum("td,tf->df", normed2_low, grad_pre, preferred_element_type=jnp.float32)
     norm2_partial = jnp.einsum("tf,df->td", grad_pre, full_in, preferred_element_type=jnp.float32)
-    grad_normed2 = lax.psum(norm2_partial.astype(jnp.bfloat16), "row").astype(jnp.float32)
+    grad_normed2 = sum_row(norm2_partial.astype(jnp.bfloat16), 2).astype(jnp.float32)
     grad_gain2 = jnp.sum(grad_normed2 * scaled2, axis=0)
     grad_shift2 = jnp.sum(grad_normed2, axis=0)
     grad_hidden = grad_top + norm_backward(grad_normed2, scaled2, inverse2, norm2_gain)
@@ -211,7 +352,7 @@
     norm1_partial = jnp.einsum(
         "ctn,cdn->td", grad_projected, full_qkv, preferred_element_type=jnp.float32
     )
-    grad_normed1 = lax.psum(norm1_partial.astype(jnp.bfloat16), "row").astype(jnp.float32)
+    grad_normed1 = sum_row(norm1_partial.astype(jnp.bfloat16), 3).astype(jnp.float32)
     grad_gain1 = jnp.sum(grad_normed1 * scaled1, axis=0)
     grad_shift1 = jnp.sum(grad_normed1, axis=0)
     d_inputs = grad_hidden + norm_backward(grad_normed1, scaled1, inverse1, norm1_gain)

time: 1170 us -> 825 us (0.71)
  waiting for transfers between devices: 803 us -> 55.5 us
  Pallas kernels: 0 us -> 430 us
  other arithmetic: 92.7 us -> 78.4 us
    psum x3 -> x0, waiting for transfers between devices: 597 us -> none  [the longest x1 292 us: local(): lax.psum(mlp_partial.astype(jnp.bfloat16), 'row').astype(jnp.float32)]
    pallas_call x0 -> x4, Pallas kernels: none -> 430 us  [sum_row(): pl.pallas_call(partial(sum_row_kernel, n), out_shape=jax.ShapeDtypeStruct...]
    reduce_scatter x4, waiting for transfers between devices: 75.1 us -> 18.2 us  [scatter_low(): lax.psum_scatter(low, ('dp', 'col'), scatter_dimension=dim, tiled=True)]
    all_gather x1, waiting for transfers between devices: 47.3 us -> 0.02 us  [local(): lax.all_gather(low_mats[2], ('dp', 'col'), axis=0, tiled=True)]
    all_gather x1, waiting for transfers between devices: 42.2 us -> 0.02 us  [local(): lax.all_gather(low_mats[3], ('dp', 'col'), axis=1, tiled=True)]
  transfers between devices with their start and end apart: 11 -> 8, of which waited for: 8 -> 2; matrix products, arithmetic and copies ran while one was open for 19% -> 23% of each run, Pallas kernels for 0% -> 26%
where the time goes in v2:
time: 825 us; the launch traced here: 821 us
  Pallas kernels  430 us (52%)
  matrix products  180 us (22%)
  other arithmetic  78.4 us (10%)
  waiting for transfers between devices  55.5 us (7%)
  local copies, waits for them, and re-layouts  34.7 us (4%)
  blocking collectives  24.2 us (3%)
  between operations  15.2 us (2%)
    pallas_call x4, Pallas kernels, sum_row(): pl.pallas_call(partial(sum_row_kernel, n), out_shape=jax.ShapeDtypeStruct...  430 us
    all_gather x1, waiting for transfers between devices, local(): lax.all_gather(low_mats[0], ('dp', 'col'), axis=1, tiled=True)  37.1 us
    dot_general x1, matrix products, local(): jnp.einsum('td,fd->tf', d_output, full_down, preferred_element_type=jnp.f...  34.1 us
    psum x1, blocking collectives, local(): lax.psum((grad_gain1, grad_shift1, grad_bqv, grad_bout, grad_gain2, grad_...  24.2 us
    reduce_scatter x4, waiting for transfers between devices, scatter_low(): lax.psum_scatter(low, ('dp', 'col'), scatter_dimension=dim, tiled=True)  18.2 us
  transfers between devices with their start and end apart: 8, of which 2 were waited for; matrix products, arithmetic and copies ran while one was open for 23% of the time, Pallas kernels for 26%

profile of v2, /device:TPU:0, one launch (start us, length us, event | category | flops | bytes accessed | tf_op | source)
XLA Modules:
  0.0 821.4 jit_solution(16508797327300174572)
XLA Ops:
  18.8 3.8 fusion.29
  22.8 37.1 %all-gather.5.cloned.1.call-done = bf16[3,2048,512]{1,2,0:T(8,128)(2,1)} async-done(((bf16[3,256,512]{1,2,0:T(8,128)(2,1)}), bf16[3,2048,512]{1,2,0:T(8,128)(2,1)}) %all-gather.5.cloned.1.call-update) | async-done | bytes 6291472 | tf_op jit(solution)/shard_map/all_gather | solution.py:290
  59.9 11.3 %fusion.44 = bf16[3,1024,512]{1,2,0:T(8,128)(2,1)S(1)} fusion(f32[3,512]{1,0:T(4,128)S(1)} %pad_maximum_fusion.3, bf16[3,2048,512]{1,2,0:T(8,128)(2,1)} %all-gather.5.cloned.1.call-done, bf16[1024,2048]{1,0:T(8,128)(2,1)} %param.19, f32[2048]{0:T(1024)S(1)} %copy-done.54, f32[2048]{0:T(1024)S(1)} %copy-done.40, f32[1024]{0:T(1024)S(1)} %add_rsqrt_fusion.1, ...), kind=kOutput, calls=%fused_computation.102 | convolution fusion | flops 6458179584 | bytes 13662208 | tf_op jit(solution)/shard_map/td,cdn->ctn/dot_general | solution.py:301
  78.4 22.5 %while.31 = (s32[]{:T(128)}, bf16[2,512,512]{2,1,0:T(8,128)(2,1)}, f32[2,4,512]{2,1,0:T(4,128)S(1)}, f32[2,4,512]{2,1,0:T(4,128)S(1)}, s32[2]{0:T(128)S(1)}, /*i...) while((s32[]{:T(128)}, bf16[2,512,512]{2,1,0:T(8,128)(2,1)}, ...), condition=%wide.wide.region_5.6_spmd, body=%wide.wide.region_2.5_spmd.sunk | while | flops 1099953664 | bytes 37828856 | solution.py:72
  85.3 3.2 fusion.124
  96.6 3.2 fusion.124
  101.0 5.0 convolution_convert_fusion.4.p_ref
  106.0 110.5 %shard_map.254 = bf16[1024,2048]{1,0:T(8,128)(2,1)S(1)} custom-call(bf16[1024,2048]{1,0:T(8,128)(2,1)S(1)} %convolution_convert_fusion.4.p_ref), custom_call_target="tpu_custom_call" | custom-call | tf_op jit(solution)/shard_map/pallas_call | solution.py:241
  220.6 16.2 %fusion.52 = f32[1024,2048]{1,0:T(8,128)} fusion(bf16[2048,2048]{1,0:T(8,128)(2,1)} %all-gather.9.cloned.1.call-done, f32[2048]{0:T(1024)S(1)} %copy-done.56, f32[2048]{0:T(1024)S(1)} %copy-done.42, f32[1024]{0:T(1024)S(1)} %add_rsqrt_fusion, f32[1024]{0:T(1024)S(1)} %broadcast_multiply_fusion.4, f32[2048]{0:T(1024)S(1)} %copy-done.23, ...), kind=kOutput, calls=%fused_computation.124 | convolution fusion | flops 8608808960 | bytes 25198592 | tf_op jit(solution)/shard_map/dot_general | solution.py:311
  236.8 34.1 %convert_reduce_fusion.4 = (f32[2048]{0:T(1024)}, bf16[1024,2048]{1,0:T(8,128)(2,1)S(1)}, f32[1024,2048]{1,0:T(8,128)}) fusion(f32[1024,2048]{1,0:T(8,128)} %fusion.52, f32[2048]{0:T(1024)S(1)} %copy-done.49, bf16[1024,2048]{1,0:T(8,128)(2,1)} %param.33, bf16[2048,2048]{1,0:T(8,128)(2,1)} %all-gather.11.cloned.1.call-done), kind=kOutput, calls=%fused_computation.73 | convolution fusion | flops 8747218944 | bytes 33570816 | tf_op jit(solution)/shard_map/td,fd->tf/dot_general | solution.py:322
  271.0 9.1 %convolution_convert_fusion.2.p_ref = bf16[1024,2048]{1,0:T(8,128)(2,1)S(1)} fusion(bf16[1024,2048]{1,0:T(8,128)(2,1)S(1)} %get-tuple-element.301, bf16[2048,2048]{1,0:T(8,128)(2,1)S(1)} %copy-done.53), kind=kOutput, calls=%fused_computation.99 | convolution fusion | flops 8592031744 | bytes 16777216 | tf_op jit(solution)/shard_map/tf,df->td/dot_general | solution.py:326
  280.1 108.1 %shard_map.256 = bf16[1024,2048]{1,0:T(8,128)(2,1)S(1)} custom-call(bf16[1024,2048]{1,0:T(8,128)(2,1)S(1)} %convolution_convert_fusion.2.p_ref), custom_call_target="tpu_custom_call" | custom-call | tf_op jit(solution)/shard_map/pallas_call | solution.py:241
  388.1 10.0 %multiply_convert_fusion.1 = bf16[1024,2048]{1,0:T(8,128)(2,1)} fusion(f32[1024,2048]{1,0:T(8,128)} %get-tuple-element.302, f32[1024,2048]{1,0:T(8,128)} %fusion.52, f32[2048]{0:T(1024)S(1)} %copy-done.49), kind=kLoop, calls=%fused_computation.77 | loop fusion | flops 8388608 | bytes 20979712 | tf_op jit(solution)/shard_map/convert_element_type | solution.py:313
  398.1 12.5 %convolution_convert_fusion.3.p_ref = bf16[1024,2048]{1,0:T(8,128)(2,1)S(1)} fusion(bf16[1024,2048]{1,0:T(8,128)(2,1)} %multiply_convert_fusion.1, bf16[2048,2048]{1,0:T(8,128)(2,1)} %all-gather.11.cloned.1.call-done), kind=kOutput, calls=%fused_computation.100 | convolution fusion | flops 8592031744 | bytes 16777216 | tf_op jit(solution)/shard_map/dot_general | solution.py:314
  410.7 105.9 %shard_map.255 = bf16[1024,2048]{1,0:T(8,128)(2,1)S(1)} custom-call(bf16[1024,2048]{1,0:T(8,128)(2,1)S(1)} %convolution_convert_fusion.3.p_ref), custom_call_target="tpu_custom_call" | custom-call | tf_op jit(solution)/shard_map/pallas_call | solution.py:241
  516.7 6.1 fusion.36
  522.8 9.6 %convert_reduce_fusion.5 = (f32[2048]{0:T(1024)}, f32[1024,2048]{1,0:T(8,128)S(1)}, bf16[1024,2048]{1,0:T(8,128)(2,1)}, f32[2048]{0:T(1024)}) fusion(f32[1024]{0:T(1024)S(1)} %get-tuple-element.322, f32[1024]{0:T(1024)S(1)} %copy-done.33, f32[2048]{0:T(1024)S(1)} %copy-done.24, bf16[1024,2048]{1,0:T(8,128)(2,1)S(1)} %copy-done.1, ...), kind=kLoop, calls=%fused_computation.74 | loop fusion | flops 46133248 | bytes 33611776 | tf_op jit(solution)/shard_map/reduce_sum | solution.py:332
  532.5 3.4 copy-done.9
  535.9 3.7 convolution_convert_fusion.5
  539.7 7.5 convolution_convert_fusion.6
  547.2 35.5 %while.30 = (s32[]{:T(128)}, f32[1024,4,128]{0,2,1:T(8,128)S(1)}, f32[1024,4,128]{0,2,1:T(8,128)}, bf16[2,512,512]{1,2,0:T(8,128)(2,1)}, s32[2]{0:T(128)S(1)}, /...) while((s32[]{:T(128)}, f32[1024,4,128]{0,2,1:T(8,128)S(1)}, ...), condition=%wide.region_12.13_spmd.clone, body=%wide.region_10.12_spmd.clone.sunk | while | flops 2709519872 | bytes 115939768 | solution.py:114
  553.0 4.2 exponential_divide_fusion.2
  570.6 4.2 exponential_divide_fusion.2
  588.1 12.3 %convert_bitcast_fusion = bf16[3,2048,512]{1,2,0:T(8,128)(2,1)} fusion(bf16[1,1024,512]{2,1,0:T(8,128)(2,1)} %copy.67, bf16[1,1024,512]{2,1,0:T(8,128)(2,1)S(1)} %copy.66, bf16[1,1024,512]{2,1,0:T(8,128)(2,1)S(1)} %bitcast.139, bf16[1024,2048]{1,0:T(8,128)(2,1)} %param.19, f32[2048]{0:T(1024)S(1)} %copy-done.55, f32[2048]{0:T(1024)S(1)} %copy-done.41, ...), kind=kOutput, calls=%fused_computation.96 | convolution fusion | flops 6461325312 | bytes 13656064 | tf_op jit(solution)/shard_map/td,ctn->cdn/dot_general | solution.py:349
  600.5 15.4 %convolution_convert_fusion.1 = bf16[2048,2048]{1,0:T(8,128)(2,1)} fusion(bf16[1024,2048]{1,0:T(8,128)(2,1)} %copy-done.58, f32[2048]{0:T(1024)S(1)} %copy-done.57, f32[2048]{0:T(1024)S(1)} %copy-done.44, f32[1024]{0:T(1024)S(1)} %copy-done.39, f32[1024]{0:T(1024)S(1)} %copy-done.34, f32[2048]{0:T(1024)S(1)} %copy-done.25, bf16[1024,2048]{1,0:T(8,128)(2,1)} %copy-done, ...), kind=kOutput, calls=%fused_computation.95 | convolution fusion | flops 8613003264 | bytes 21004288 | tf_op jit(solution)/shard_map/td,tf->df/dot_general | solution.py:325
  616.0 14.2 %convolution_convert_fusion = bf16[2048,2048]{1,0:T(8,128)(2,1)} fusion(bf16[1024,2048]{1,0:T(8,128)(2,1)} %multiply_convert_fusion.1, bf16[1024,2048]{1,0:T(8,128)(2,1)} %param.33), kind=kOutput, calls=%fused_computation.94 | convolution fusion | flops 8594128896 | bytes 16777216 | tf_op jit(solution)/shard_map/tf,td->fd/dot_general | solution.py:319
  631.4 8.8 %bitcast_convert_fusion.p_ref = bf16[1024,2048]{1,0:T(8,128)(2,1)S(1)} fusion(bf16[3,2048,512]{1,2,0:T(8,128)(2,1)} %all-gather.5.cloned.1.call-done, bf16[1,1024,512]{2,1,0:T(8,128)(2,1)S(1)} %copy-done.21, bf16[1,1024,512]{2,1,0:T(8,128)(2,1)S(1)} %copy.66, bf16[1,1024,512]{2,1,0:T(8,128)(2,1)S(1)} %bitcast.140), kind=kOutput, calls=%fused_computation.72 | convolution fusion | flops 6447693824 | bytes 13631488 | tf_op jit(solution)/shard_map/ctn,cdn->td/dot_general | solution.py:352
  640.2 105.1 %shard_map.257 = bf16[1024,2048]{1,0:T(8,128)(2,1)S(1)} custom-call(bf16[1024,2048]{1,0:T(8,128)(2,1)S(1)} %bitcast_convert_fusion.p_ref), custom_call_target="tpu_custom_call" | custom-call | tf_op jit(solution)/shard_map/pallas_call | solution.py:241
  747.4 4.3 fusion.37
  751.7 24.2 %all-reduce = (f32[2048]{0:T(1024)}, f32[2048]{0:T(1024)}, f32[2,512]{1,0:T(2,128)}, f32[2048]{0:T(1024)}, f32[2048]{0:T(1024)}, /*index=5*/f32[2048]{0:T(1024)}, f32[2048]{0:T(1024)}, f32[2048]{0:T(1024)}) all-reduce(f32[2048]{0:T(1024)S(1)} %get-tuple-element.244, ...), channel_id=1, replica_groups=mesh['dp'=2,'row'=4,'col'=4] {'dp','col'}, use_global_device_ids=true, to_apply=%region_16.17 | all-reduce | flops 15360 | bytes 122880 | tf_op jit(solution)/shard_map/psum | solution.py:365
  775.9 10.2 %fusion.28 = f32[1024,2048]{1,0:T(8,128)} fusion(f32[1024,2048]{1,0:T(8,128)} %copy-done.9, bf16[1024,2048]{1,0:T(8,128)(2,1)} %param.19, bf16[1024,2048]{1,0:T(8,128)(2,1)} %copy-done.2, f32[1024]{0:T(1024)S(1)} %broadcast_multiply_fusion, f32[1024]{0:T(1024)S(1)} %broadcast_multiply_fusion.1, f32[2048]{0:T(1024)S(1)} %copy-done.41, ...), kind=kLoop, calls=%fused_computation.62 | loop fusion | flops 20971520 | bytes 25190400 | tf_op jit(solution)/shard_map/add | solution.py:358
  793.4 18.2 %reduce-scatter.11.cloned.1.call-done = bf16[2048,256]{1,0:T(8,128)(2,1)} async-done(((bf16[2048,2048]{1,0:T(8,128)(2,1)}), bf16[2048,256]{1,0:T(8,128)(2,1)}) %reduce-scatter.11.cloned.1.call-update) | async-done | bytes 1048592 | tf_op jit(solution)/shard_map/reduce_scatter | solution.py:262
  (241 shorter events, 81.5 us)
Async XLA Ops:
  7.2 52.7 %all-gather.5.cloned.1.call-start = ((), (), s32[]{:S(2)}) async-start(), calls=%async_computation.4 | async-start | bytes 7077888 | tf_op jit(solution)/shard_map/all_gather | solution.py:290
  10.0 91.0 %all-gather.7.cloned.1.call-start = ((), (), s32[]{:S(2)}) async-start(), calls=%async_computation.5 | async-start | bytes 2359296 | tf_op jit(solution)/shard_map/all_gather | solution.py:291
  11.8 48.1 %copy-start.40 = (f32[2048]{0:T(1024)S(1)}, f32[2048]{0:T(1024)}, u32[]{:S(2)}) copy-start(f32[2048]{0:T(1024)} %param.21) | copy-start | bytes 24580
  11.8 48.1 %copy-start.54 = (f32[2048]{0:T(1024)S(1)}, f32[2048]{0:T(1024)}, u32[]{:S(2)}) copy-start(f32[2048]{0:T(1024)} %param.22) | copy-start | bytes 24580
  11.8 208.7 %all-gather.9.cloned.1.call-start = ((), (), s32[]{:S(2)}) async-start(), calls=%async_computation.6 | async-start | bytes 9437184 | tf_op jit(solution)/shard_map/all_gather | solution.py:292
  14.6 222.2 %all-gather.11.cloned.1.call-start = ((), (), s32[]{:S(2)}) async-start(), calls=%async_computation.7 | async-start | bytes 9437184 | tf_op jit(solution)/shard_map/all_gather | solution.py:293
  15.8 770.4 %reduce-scatter.7.cloned.1.call-start = ((), (), s32[]{:S(2)}) async-start(), calls=%async_computation.9 | async-start | bytes 2359296 | tf_op jit(solution)/shard_map/reduce_scatter | solution.py:262
  18.7 41.1 %copy-start.30 = (f32[1024]{0:T(1024)}, f32[1024]{0:T(1024)S(1)}, u32[]{:S(2)}) copy-start(f32[1024]{0:T(1024)S(1)} %broadcast_multiply_fusion.5) | copy-start | bytes 12292
  22.6 37.3 %copy-start.35 = (f32[1024]{0:T(1024)}, f32[1024]{0:T(1024)S(1)}, u32[]{:S(2)}) copy-start(f32[1024]{0:T(1024)S(1)} %add_rsqrt_fusion.1) | copy-start | bytes 12292
  100.9 115.5 %copy-start.11 = (bf16[1024,512]{0,1:T(8,128)(2,1)}, bf16[1024,512]{0,1:T(8,128)(2,1)S(1)}, u32[]{:S(2)}) copy-start(bf16[1024,512]{0,1:T(8,128)(2,1)S(1)} %get-tuple-element.612) | copy-start | bytes 3145732
  100.9 115.5 %copy-start.26 = (f32[2,4,512]{2,1,0:T(4,128)}, f32[2,4,512]{2,1,0:T(4,128)S(1)}, u32[]{:S(2)}) copy-start(f32[2,4,512]{2,1,0:T(4,128)S(1)} %get-tuple-element.565) | copy-start | bytes 49156
  100.9 115.5 %copy-start.28 = (f32[2,4,512]{2,1,0:T(4,128)}, f32[2,4,512]{2,1,0:T(4,128)S(1)}, u32[]{:S(2)}) copy-start(f32[2,4,512]{2,1,0:T(4,128)S(1)} %get-tuple-element.564) | copy-start | bytes 49156
  100.9 115.5 %copy-start.3 = (bf16[1024,2048]{1,0:T(8,128)(2,1)S(1)}, bf16[1024,2048]{1,0:T(8,128)(2,1)}, u32[]{:S(2)}) copy-start(bf16[1024,2048]{1,0:T(8,128)(2,1)} %param.19) | copy-start | bytes 12582916
  101.0 115.5 %copy-start.23 = (f32[2048]{0:T(1024)S(1)}, f32[2048]{0:T(1024)}, u32[]{:S(2)}) copy-start(f32[2048]{0:T(1024)} %param.26) | copy-start | bytes 24580
  218.0 18.8 %copy-start.32 = (f32[1024]{0:T(1024)}, f32[1024]{0:T(1024)S(1)}, u32[]{:S(2)}) copy-start(f32[1024]{0:T(1024)S(1)} %broadcast_multiply_fusion.4) | copy-start | bytes 12292
  236.8 34.2 %copy-start.53 = (bf16[2048,2048]{1,0:T(8,128)(2,1)S(1)}, bf16[2048,2048]{1,0:T(8,128)(2,1)}, u32[]{:S(2)}) copy-start(bf16[2048,2048]{1,0:T(8,128)(2,1)} %all-gather.9.cloned.1.call-done) | copy-start | bytes 25165828
  398.1 118.5 %copy-start.24 = (f32[2048]{0:T(1024)S(1)}, f32[2048]{0:T(1024)}, u32[]{:S(2)}) copy-start(f32[2048]{0:T(1024)} %param.26) | copy-start | bytes 24580
  398.1 118.5 %copy-start.33 = (f32[1024]{0:T(1024)S(1)}, f32[1024]{0:T(1024)}, u32[]{:S(2)}) copy-start(f32[1024]{0:T(1024)} %copy-done.32) | copy-start | bytes 12292
  398.1 118.5 %copy-start.38 = (f32[1024]{0:T(1024)S(1)}, f32[1024]{0:T(1024)}, u32[]{:S(2)}) copy-start(f32[1024]{0:T(1024)} %copy-done.37) | copy-start | bytes 12292
  398.1 118.5 %copy-start.43 = (f32[2048]{0:T(1024)S(1)}, f32[2048]{0:T(1024)}, u32[]{:S(2)}) copy-start(f32[2048]{0:T(1024)} %param.27) | copy-start | bytes 24580
  410.7 106.0 %copy-start.1 = (bf16[1024,2048]{1,0:T(8,128)(2,1)S(1)}, bf16[1024,2048]{1,0:T(8,128)(2,1)}, u32[]{:S(2)}) copy-start(bf16[1024,2048]{1,0:T(8,128)(2,1)} %copy-done) | copy-start | bytes 12582916
  410.7 106.0 %copy-start.4 = (bf16[1024,2048]{1,0:T(8,128)(2,1)S(1)}, bf16[1024,2048]{1,0:T(8,128)(2,1)}, u32[]{:S(2)}) copy-start(bf16[1024,2048]{1,0:T(8,128)(2,1)} %param.19) | copy-start | bytes 12582916
  539.7 248.3 %reduce-scatter.5.cloned.1.call-start = ((), (), s32[]{:S(2)}) async-start(), calls=%async_computation.8 | async-start | bytes 7077888 | tf_op jit(solution)/shard_map/reduce_scatter | solution.py:262
  600.4 190.2 %reduce-scatter.9.cloned.1.call-start = ((), (), s32[]{:S(2)}) async-start(), calls=%async_computation.10 | async-start | bytes 9437184 | tf_op jit(solution)/shard_map/reduce_scatter | solution.py:262
  616.0 195.7 %reduce-scatter.11.cloned.1.call-start = ((), (), s32[]{:S(2)}) async-start(), calls=%async_computation.11 | async-start | bytes 9437184 | tf_op jit(solution)/shard_map/reduce_scatter | solution.py:262
  640.2 105.2 %copy-start.15 = (bf16[2,512,512]{1,2,0:T(8,128)(2,1)S(1)}, bf16[2,512,512]{1,2,0:T(8,128)(2,1)}, u32[]{:S(2)}) copy-start(bf16[2,512,512]{1,2,0:T(8,128)(2,1)} %get-tuple-element.628) | copy-start | bytes 3145732
  640.2 107.3 %copy-start.5 = (bf16[1024,2048]{1,0:T(8,128)(2,1)S(1)}, bf16[1024,2048]{1,0:T(8,128)(2,1)}, u32[]{:S(2)}) copy-start(bf16[1024,2048]{1,0:T(8,128)(2,1)} %param.19) | copy-start | bytes 12582916
  640.2 111.5 %copy-start.45 = (f32[2048]{0:T(1024)S(1)}, f32[2048]{0:T(1024)}, u32[]{:S(2)}) copy-start(f32[2048]{0:T(1024)} %get-tuple-element.242) | copy-start | bytes 24580
  640.2 111.5 %copy-start.46 = (f32[2048]{0:T(1024)S(1)}, f32[2048]{0:T(1024)}, u32[]{:S(2)}) copy-start(f32[2048]{0:T(1024)} %get-tuple-element.248) | copy-start | bytes 24580
  640.2 111.5 %copy-start.47 = (f32[2048]{0:T(1024)S(1)}, f32[2048]{0:T(1024)}, u32[]{:S(2)}) copy-start(f32[2048]{0:T(1024)} %get-tuple-element.303) | copy-start | bytes 24580
  640.2 111.5 %copy-start.48 = (f32[2048]{0:T(1024)S(1)}, f32[2048]{0:T(1024)}, u32[]{:S(2)}) copy-start(f32[2048]{0:T(1024)} %get-tuple-element.316) | copy-start | bytes 24580
  640.2 111.5 %copy-start.51 = (f32[2048]{0:T(1024)S(1)}, f32[2048]{0:T(1024)}, u32[]{:S(2)}) copy-start(f32[2048]{0:T(1024)} %get-tuple-element.300) | copy-start | bytes 24580
  (42 other events, 251.9 us)
Sparse Core Ops, SparseCore 0:
  10.5 49.3 all-gather.4
  62.3 28.1 all-gather.6
  93.0 54.3 all-gather.8
  149.2 55.9 all-gather.10
  539.7 40.2 reduce-scatter.6
  600.5 60.8 reduce-scatter.4
  664.9 71.2 reduce-scatter.8
  740.0 71.5 reduce-scatter.10

commit v3 on v2

--- a/solution.py
+++ b/solution.py
@@ -73,55 +73,13 @@
     return (contexts.reshape(length, width), maxima, totals)
 
 
-def attend_backward(queries, keys_low, values_low, prefix, block_rows, maxima, totals, d_context):
-    length, width = queries.shape
-    heads = width // HEAD_DIM
-    score_scale = HEAD_DIM ** (-0.5)
-    value_heads = values_low.reshape(length, heads, HEAD_DIM)
-
-    def one_block(sums, entries):
-        block_index, row_max, row_total = entries
-        block_start = block_index * block_rows
-        scores, query_block, key_heads = block_scores(
-            queries, keys_low, block_start, block_rows, prefix
-        )
-        probs = jnp.exp(scores - row_max[..., None]) / row_total[..., None]
-        probs_low = probs.astype(jnp.bfloat16)
-        grad_block = lax.dynamic_slice_in_dim(d_context, block_start, block_rows, 0).reshape(
-            block_rows, heads, HEAD_DIM
-        )
-        d_probs = jnp.einsum(
-            "qhd,khd->hqk", grad_block, value_heads, preferred_element_type=jnp.float32
-        )
-        inner = jnp.sum(d_probs * probs, axis=-1, keepdims=True)
-        d_scores = (probs * (d_probs - inner)).astype(jnp.bfloat16)
-        d_query = (
-            jnp.einsum("hqk,khd->qhd", d_scores, key_heads, preferred_element_type=jnp.float32)
-            * score_scale
-        )
-        d_keys = (
-            sums[0]
-            + jnp.einsum("hqk,qhd->khd", d_scores, query_block, preferred_element_type=jnp.float32)
-            * score_scale
-        )
-        d_values = sums[1] + jnp.einsum(
-            "hqk,qhd->khd", probs_low, grad_block, preferred_element_type=jnp.float32
-        )
-        return ((d_keys, d_values), d_query.reshape(block_rows, width).astype(jnp.bfloat16))
-
-    zeros = jnp.zeros((length, heads, HEAD_DIM), jnp.float32)
-    count = length // block_rows
-    (d_keys, d_values), d_queries = lax.scan(
-        one_block, (zeros, zeros), (jnp.arange(count, dtype=jnp.int32), maxima, totals)
-    )
-    return (
-        d_queries.reshape(length, width),
-        d_keys.reshape(length, width).astype(jnp.bfloat16),
-        d_values.reshape(length, width).astype(jnp.bfloat16),
-    )
-
-
-def sum_row_kernel(n, p_ref, o_ref, held, rs_s, rs_r, ag_s, ag_r, loc):
+def dot(left, right, left_dim, right_dim):
+    return lax.dot_general(
+        left, right, (((left_dim,), (right_dim,)), ((), ())), preferred_element_type=jnp.float32
+    )
+
+
+def line_sum(n, p_ref, o_ref, held, rs_s, rs_r, ag_s, ag_r, loc):
     half = p_ref.shape[0] // 2
     chunks = half // CHUNK
     r = lax.axis_index("row")
@@ -173,7 +131,7 @@
     def keep(d, c):
         return pltpu.make_async_copy(held.at[rows(d, c)], o_ref.at[rows(d, c)], loc.at[c])
 
-    def step(t, carry):
+    def step(t):
         for d in (0, 1):
 
             @pl.when((place[d] == 0) & (t < chunks))
@@ -210,56 +168,279 @@
                 def _():
                     back(d, c, o_ref).start()
 
+    def drain():
+        def one(c, carry):
+            for d in (0, 1):
+
+                @pl.when(place[d] < last)
+                def _():
+                    onward(d, c, p_ref).wait_send()
+
+                @pl.when(place[d] > 0)
+                def _():
+                    back(d, c, o_ref).wait_send()
+
+                @pl.when(place[d] == last)
+                def _():
+                    keep(d, c).wait()
+
+            return carry
+
+        lax.fori_loop(0, chunks, one, 0)
+
+    return step, drain
+
+
+def line_steps(n, total_rows):
+    return total_rows // 2 // CHUNK + LAG * 2 * (n - 1)
+
+
+def line_scratch(shape):
+    chunks = shape[0] // 2 // CHUNK
+    dma = pltpu.SemaphoreType.DMA
+    return [
+        pltpu.VMEM(shape, jnp.bfloat16),
+        dma((2, chunks)),
+        dma((2, chunks)),
+        dma((2, chunks)),
+        dma((2, chunks)),
+        dma((chunks,)),
+    ]
+
+
+def loop(start, stop, body):
+    def one(t, carry):
+        body(t)
         return carry
 
-    lax.fori_loop(0, chunks + LAG * 2 * last, step, 0)
-
-    def drain(c, carry):
-        for d in (0, 1):
-
-            @pl.when(place[d] < last)
-            def _():
-                onward(d, c, p_ref).wait_send()
-
-            @pl.when(place[d] > 0)
-            def _():
-                back(d, c, o_ref).wait_send()
-
-            @pl.when(place[d] == last)
-            def _():
-                keep(d, c).wait()
-
-        return carry
-
-    lax.fori_loop(0, chunks, drain, 0)
-
-
-def sum_row(partial_low, collective_id):
-    n = lax.axis_size("row")
-    chunks = partial_low.shape[0] // 2 // CHUNK
+    lax.fori_loop(start, stop, one, 0)
+
+
+IN_VMEM = pl.BlockSpec(memory_space=pltpu.VMEM)
+IN_HBM = pl.BlockSpec(memory_space=pl.ANY)
+
+
+def low_shape(*shape):
+    return jax.ShapeDtypeStruct(shape, jnp.bfloat16)
+
+
+def kernel_params(collective_id, mib):
+    return pltpu.CompilerParams(
+        collective_id=collective_id, has_side_effects=True, vmem_limit_bytes=mib * 2**20
+    )
+
+
+COST = pl.CostEstimate(flops=1000, bytes_accessed=1000, transcendentals=0)
+
+
+def sum_row_kernel(n, p_ref, o_ref, *line):
+    step, drain = line_sum(n, p_ref, o_ref, *line)
+    loop(0, line_steps(n, p_ref.shape[0]), step)
+    drain()
+
+
+def sum_row(partial_low):
+    return pl.pallas_call(
+        partial(sum_row_kernel, lax.axis_size("row")),
+        out_shape=low_shape(*partial_low.shape),
+        in_specs=[IN_VMEM],
+        out_specs=IN_HBM,
+        scratch_shapes=line_scratch(partial_low.shape),
+        compiler_params=kernel_params(0, 16),
+        cost_estimate=COST,
+    )(partial_low)
+
+
+TILE_M = 512
+TILE_N = 1024
+
+
+def products_sum_kernel(n, p_ref, *refs):
+    pairs = 2
+    sources = refs[: 2 * pairs]
+    o_ref = refs[2 * pairs]
+    outs = refs[2 * pairs + 1 : 3 * pairs + 1]
+    held = refs[3 * pairs + 1 : 5 * pairs + 1]
+    stage, load_sem, store_sem = refs[5 * pairs + 1 : 5 * pairs + 4]
+    line = refs[5 * pairs + 4 :]
+    loads = [
+        pltpu.make_async_copy(src, dst, load_sem.at[i])
+        for i, (src, dst) in enumerate(zip(sources, held))
+    ]
+    for load in loads:
+        load.start()
+    step, drain = line_sum(n, p_ref, o_ref, *line)
+    steps = line_steps(n, p_ref.shape[0])
+    across = outs[0].shape[1] // TILE_N
+    tiles = (outs[0].shape[0] // TILE_M) * across
+    begin = 3
+
+    def store(k, tile):
+        m = pl.ds(pl.multiple_of((tile // across) * TILE_M, TILE_M), TILE_M)
+        c = pl.ds(pl.multiple_of(lax.rem(tile, across) * TILE_N, TILE_N), TILE_N)
+        slot = lax.rem(tile, 2)
+        return m, c, slot, pltpu.make_async_copy(
+            stage.at[slot], outs[k].at[m, c], store_sem.at[slot]
+        )
+
+    loop(0, begin, step)
+    for k in range(pairs):
+        loads[2 * k].wait()
+        loads[2 * k + 1].wait()
+
+        def body(t):
+            step(t)
+            tile = t - begin - k * tiles
+            m, c, slot, copy = store(k, tile)
+
+            if k == 0:
+
+                @pl.when(tile >= 2)
+                def _():
+                    store(k, tile - 2)[3].wait()
+            else:
+                copy.wait()
+
+            stage[slot] = dot(held[2 * k][:, m], held[2 * k + 1][:, c], 0, 0).astype(jnp.bfloat16)
+            copy.start()
+
+        loop(begin + k * tiles, begin + (k + 1) * tiles, body)
+    loop(begin + pairs * tiles, steps, step)
+    for slot in range(2):
+        store(pairs - 1, slot)[3].wait()
+    drain()
+
+
+def products_sum(partial_low, pairs):
+    sources = [array for pair in pairs for array in pair]
+    out = [low_shape(left.shape[1], right.shape[1]) for left, right in pairs]
     dma = pltpu.SemaphoreType.DMA
     return pl.pallas_call(
-        partial(sum_row_kernel, n),
-        out_shape=jax.ShapeDtypeStruct(partial_low.shape, partial_low.dtype),
-        in_specs=[pl.BlockSpec(memory_space=pltpu.VMEM)],
-        out_specs=pl.BlockSpec(memory_space=pl.ANY),
+        partial(products_sum_kernel, lax.axis_size("row")),
+        out_shape=[low_shape(*partial_low.shape)] + out,
+        in_specs=[IN_VMEM] + [IN_HBM] * len(sources),
+        out_specs=[IN_HBM] * (1 + len(out)),
+        scratch_shapes=[pltpu.VMEM(array.shape, jnp.bfloat16) for array in sources]
+        + [pltpu.VMEM((2, TILE_M, TILE_N), jnp.bfloat16), dma((len(sources),)), dma((2,))]
+        + line_scratch(partial_low.shape),
+        compiler_params=kernel_params(1, 48),
+        cost_estimate=COST,
+    )(partial_low, *sources)
+
+
+QUERY_ROWS = 256
+
+
+def attend_piece(i, prefix, cols, q, k, v, k_t, d_context, d_proj, d_key, d_value, first):
+    start = i * QUERY_ROWS
+    width = max(start + QUERY_ROWS, q.shape[0] // 2)
+    here = slice(start, start + QUERY_ROWS)
+    score_scale = HEAD_DIM ** (-0.5)
+    q_block, g_block = q[here, cols], d_context[here, cols]
+    scores = dot(k[:width, cols], q_block, 1, 1) * score_scale
+    key = lax.broadcasted_iota(jnp.int32, scores.shape, 0)
+    query = lax.broadcasted_iota(jnp.int32, scores.shape, 1) + start
+    scores = jnp.where((key <= query) | (key < prefix), scores, -1000000000.0)
+    expo = jnp.exp(scores - jnp.max(scores, axis=0, keepdims=True))
+    probs = expo * (1.0 / jnp.sum(expo, axis=0, keepdims=True))
+    d_probs = dot(v[:width, cols], g_block, 1, 1)
+    inner = jnp.sum(d_probs * probs, axis=0, keepdims=True)
+    d_scores = (probs * (d_probs - inner)).astype(jnp.bfloat16)
+    d_query = dot(k_t[cols, :width], d_scores, 1, 0) * score_scale
+    d_proj[0, here, cols] = d_query.T.astype(jnp.bfloat16)
+    for total, term in (
+        (d_key, dot(d_scores, q_block, 1, 0)),
+        (d_value, dot(probs.astype(jnp.bfloat16), g_block, 1, 0)),
+    ):
+        if first:
+            total[...] = term
+        else:
+            total[:width] += term
+
+
+def attend_sum_kernel(
+    n, prefix_ref, p_ref, q, k, v, k_t, d_context, n1_hbm, ctx_hbm, branch_hbm,
+    o_ref, d_proj, d_bias, d_wqkv, d_wout,
+    n1, ctx, branch, d_key, d_value, load_sem, *line,
+):
+    loads = [
+        pltpu.make_async_copy(src, dst, load_sem.at[i])
+        for i, (src, dst) in enumerate(((n1_hbm, n1), (ctx_hbm, ctx), (branch_hbm, branch)))
+    ]
+    for load in loads:
+        load.start()
+    step, drain = line_sum(n, p_ref, o_ref, *line)
+    steps = line_steps(n, p_ref.shape[0])
+    prefix = prefix_ref[0]
+    blocks = q.shape[0] // QUERY_ROWS
+    heads = q.shape[1] // HEAD_DIM
+
+    def head(h):
+        cols = pl.ds(pl.multiple_of(h * HEAD_DIM, HEAD_DIM), HEAD_DIM)
+        for j in range(blocks):
+            step(h * blocks + j)
+            attend_piece(
+                blocks - 1 - j, prefix, cols, q, k, v, k_t, d_context, d_proj, d_key, d_value,
+                j == 0,
+            )
+        d_proj[1, :, cols] = (d_key[...] * HEAD_DIM ** (-0.5)).astype(jnp.bfloat16)
+        d_proj[2, :, cols] = d_value[...].astype(jnp.bfloat16)
+        for b, c in ((0, 0), (1, 2)):
+            d_bias[b : b + 1, cols] = jnp.sum(
+                d_proj[c, :, cols].astype(jnp.float32), axis=0, keepdims=True
+            )
+
+    loop(0, heads, head)
+    for load in loads:
+        load.wait()
+    begin = heads * blocks
+    tiles = n1.shape[1] // TILE_M
+
+    for c in range(3):
+
+        def body(t):
+            step(t)
+            m = pl.ds(pl.multiple_of((t - begin - c * tiles) * TILE_M, TILE_M), TILE_M)
+            d_wqkv[c, m] = dot(n1[:, m], d_proj[c], 0, 0).astype(jnp.bfloat16)
+            if c == 0:
+                d_wout[:, m] = dot(ctx[...], branch[:, m], 0, 0).astype(jnp.bfloat16)
+
+        loop(begin + c * tiles, begin + (c + 1) * tiles, body)
+    loop(begin + 3 * tiles, steps, step)
+    drain()
+
+
+def attend_sum(prefix_len, partial_low, q, k, v, d_context, normed1, context, d_branch):
+    tokens, width = q.shape
+    depth = normed1.shape[1]
+    dma = pltpu.SemaphoreType.DMA
+    return pl.pallas_call(
+        partial(attend_sum_kernel, lax.axis_size("row")),
+        out_shape=[
+            low_shape(*partial_low.shape),
+            low_shape(3, tokens, width),
+            jax.ShapeDtypeStruct((2, width), jnp.float32),
+            low_shape(3, depth, width),
+            low_shape(width, depth),
+        ],
+        in_specs=[pl.BlockSpec(memory_space=pltpu.SMEM)] + [IN_VMEM] * 6 + [IN_HBM] * 3,
+        out_specs=[IN_HBM] + [IN_VMEM] * 4,
         scratch_shapes=[
-            pltpu.VMEM(partial_low.shape, partial_low.dtype),
-            dma((2, chunks)),
-            dma((2, chunks)),
-            dma((2, chunks)),
-            dma((2, chunks)),
-            dma((chunks,)),
-        ],
-        compiler_params=pltpu.CompilerParams(
-            collective_id=collective_id, has_side_effects=True, vmem_limit_bytes=16 * 2**20
-        ),
-    )(partial_low)
+            pltpu.VMEM((tokens, depth), jnp.bfloat16),
+            pltpu.VMEM((tokens, width), jnp.bfloat16),
+            pltpu.VMEM((tokens, depth), jnp.bfloat16),
+            pltpu.VMEM((tokens, HEAD_DIM), jnp.float32),
+            pltpu.VMEM((tokens, HEAD_DIM), jnp.float32),
+            dma((3,)),
+        ]
+        + line_scratch(partial_low.shape),
+        compiler_params=kernel_params(2, 56),
+        cost_estimate=COST,
+    )(prefix_len, partial_low, q, k, v, k.T, d_context, normed1, context, d_branch)
 
 
 def scatter_low(grad, dim):
-    low = grad.astype(jnp.bfloat16)
-    summed = lax.psum_scatter(low, ("dp", "col"), scatter_dimension=dim, tiled=True)
+    summed = lax.psum_scatter(grad, ("dp", "col"), scatter_dimension=dim, tiled=True)
     return summed.astype(jnp.float32)
 
 
@@ -305,63 +486,50 @@
     context, maxima, totals = attend_forward(queries, keys_low, values_low, prefix, block_rows)
     context_low = context.astype(jnp.bfloat16)
     attn_partial = jnp.dot(context_low, full_out, preferred_element_type=jnp.float32)
-    hidden = source + sum_row(attn_partial.astype(jnp.bfloat16), 0).astype(jnp.float32) + b_out
+    hidden = source + sum_row(attn_partial.astype(jnp.bfloat16)).astype(jnp.float32) + b_out
     normed2, scaled2, inverse2 = norm_forward(hidden, norm2_gain, norm2_shift)
     normed2_low = normed2.astype(jnp.bfloat16)
     pre_act = jnp.dot(normed2_low, full_in, preferred_element_type=jnp.float32) + b_in
     activated, gelu_pull = jax.vjp(partial(jax.nn.gelu, approximate=False), pre_act)
     activated_low = activated.astype(jnp.bfloat16)
     mlp_partial = jnp.dot(activated_low, full_down, preferred_element_type=jnp.float32)
-    result = hidden + sum_row(mlp_partial.astype(jnp.bfloat16), 1).astype(jnp.float32) + b_down
-    output = result.astype(jnp.bfloat16)
     grad_top = d_output.astype(jnp.float32)
     grad_bdown = jnp.sum(grad_top, axis=0)
-    grad_wdown = jnp.einsum(
-        "tf,td->fd", activated_low, d_output, preferred_element_type=jnp.float32
-    )
     grad_act = jnp.einsum("td,fd->tf", d_output, full_down, preferred_element_type=jnp.float32)
     grad_pre = gelu_pull(grad_act)[0].astype(jnp.bfloat16)
     grad_bin = jnp.sum(grad_pre.astype(jnp.float32), axis=0)
-    grad_win = jnp.einsum("td,tf->df", normed2_low, grad_pre, preferred_element_type=jnp.float32)
     norm2_partial = jnp.einsum("tf,df->td", grad_pre, full_in, preferred_element_type=jnp.float32)
-    grad_normed2 = sum_row(norm2_partial.astype(jnp.bfloat16), 2).astype(jnp.float32)
+    summed2, grad_wdown, grad_win = products_sum(
+        norm2_partial.astype(jnp.bfloat16), ((activated_low, d_output), (normed2_low, grad_pre))
+    )
+    grad_normed2 = summed2.astype(jnp.float32)
     grad_gain2 = jnp.sum(grad_normed2 * scaled2, axis=0)
     grad_shift2 = jnp.sum(grad_normed2, axis=0)
     grad_hidden = grad_top + norm_backward(grad_normed2, scaled2, inverse2, norm2_gain)
     grad_branch = grad_hidden.astype(jnp.bfloat16)
     grad_bout = jnp.sum(grad_branch.astype(jnp.float32), axis=0)
-    grad_wout = jnp.einsum(
-        "tr,td->rd", context_low, grad_branch, preferred_element_type=jnp.float32
-    )
     grad_context = jnp.einsum(
         "td,rd->tr", grad_branch, full_out, preferred_element_type=jnp.float32
     ).astype(jnp.bfloat16)
-    grad_queries, grad_keys, grad_values = attend_backward(
-        queries, keys_low, values_low, prefix, block_rows, maxima, totals, grad_context
-    )
-    grad_projected = jnp.stack([grad_queries, grad_keys, grad_values])
-    grad_bqv = jnp.stack(
-        [
-            jnp.sum(grad_queries.astype(jnp.float32), axis=0),
-            jnp.sum(grad_values.astype(jnp.float32), axis=0),
-        ]
-    )
-    grad_wqkv = jnp.einsum(
-        "td,ctn->cdn", normed1_low, grad_projected, preferred_element_type=jnp.float32
-    )
+    mlp_sum, grad_projected, grad_bqv, grad_wqkv, grad_wout = attend_sum(
+        prefix_len, mlp_partial.astype(jnp.bfloat16), queries, keys_low, values_low,
+        grad_context, normed1_low, context_low, grad_branch,
+    )
+    output = (hidden + mlp_sum.astype(jnp.float32) + b_down).astype(jnp.bfloat16)
     norm1_partial = jnp.einsum(
         "ctn,cdn->td", grad_projected, full_qkv, preferred_element_type=jnp.float32
     )
-    grad_normed1 = sum_row(norm1_partial.astype(jnp.bfloat16), 3).astype(jnp.float32)
+    sent_win = scatter_low(grad_win, 0)
+    sent_wdown = scatter_low(grad_wdown, 1)
+    norm1_low = norm1_partial.astype(jnp.bfloat16)
+    grad_wqkv, grad_wout, sent_win, sent_wdown = lax.optimization_barrier(
+        (grad_wqkv, grad_wout, sent_win, sent_wdown)
+    )
+    sent_wout, sent_wqkv = scatter_low(grad_wout, 1), scatter_low(grad_wqkv, 1)
+    grad_normed1 = sum_row(norm1_low).astype(jnp.float32)
     grad_gain1 = jnp.sum(grad_normed1 * scaled1, axis=0)
     grad_shift1 = jnp.sum(grad_normed1, axis=0)
     d_inputs = grad_hidden + norm_backward(grad_normed1, scaled1, inverse1, norm1_gain)
-    sent_wqkv, sent_wout, sent_win, sent_wdown = (
-        scatter_low(grad_wqkv, 1),
-        scatter_low(grad_wout, 1),
-        scatter_low(grad_win, 0),
-        scatter_low(grad_wdown, 1),
-    )
     small = lax.psum(
         (
             grad_gain1,

time: 825 us -> 752 us (0.912)
  matrix products: 180 us -> 110 us
  waiting for transfers between devices: 55.5 us -> 33.7 us
  other arithmetic: 78.4 us -> 96.9 us
  Pallas kernels: 430 us -> 444 us
  local copies, waits for them, and re-layouts: 34.7 us -> 23.6 us
    dot_general x12 -> x0, matrix products: 56.6 us -> none  [the longest x1 15.4 us: local(): jnp.einsum('td,tf->df', normed2_low, grad_pre, preferred_element_type=jnp...]
    reduce_scatter x4, waiting for transfers between devices: 18.2 us -> 0.03 us  [scatter_low(): lax.psum_scatter(grad, ('dp', 'col'), scatter_dimension=dim, tiled=True)]
    pallas_call x4, Pallas kernels: 430 us -> 444 us  [the longest x2 217 us: sum_row(): pl.pallas_call(partial(sum_row_kernel, lax.axis_size('row')), out_shape=l...]
    sub x0 -> x2, other arithmetic: none -> 12 us  [one_block(): expo = jnp.exp(scores - row_max[..., None])]
    dot_general x4 -> x2, matrix products: 12.7 us -> 2.59 us  [block_scores(): jnp.einsum('qhd,khd->hqk', query_block, key_heads, preferred_element_type...]
  transfers between devices with their start and end apart: 8 -> 8, of which waited for: 2 -> 1; matrix products, arithmetic and copies ran while one was open for 23% -> 21% of each run, Pallas kernels for 26% -> 45%
where the time goes in v3:
time: 752 us; the launch traced here: 749 us
  Pallas kernels  444 us (59%)
  matrix products  110 us (15%)
  other arithmetic  96.9 us (13%)
  waiting for transfers between devices  33.7 us (4%)
  local copies, waits for them, and re-layouts  23.6 us (3%)
  blocking collectives  23.5 us (3%)
  between operations  15.9 us (2%)
    pallas_call x2, Pallas kernels, sum_row(): pl.pallas_call(partial(sum_row_kernel, lax.axis_size('row')), out_shape=l...  217 us
    pallas_call x1, Pallas kernels, attend_sum(): pl.pallas_call(partial(attend_sum_kernel, lax.axis_size('row')), out_shap...  117 us
    pallas_call x1, Pallas kernels, products_sum(): pl.pallas_call(partial(products_sum_kernel, lax.axis_size('row')), out_sh...  110 us
    dot_general x1, matrix products, local(): jnp.einsum('td,fd->tf', d_output, full_down, preferred_element_type=jnp.f...  33.5 us
    all_gather x1, waiting for transfers between devices, local(): lax.all_gather(low_mats[0], ('dp', 'col'), axis=1, tiled=True)  32.3 us
    psum x1, blocking collectives, local(): lax.psum((grad_gain1, grad_shift1, grad_bqv, grad_bout, grad_gain2, grad_...  23.5 us
  transfers between devices with their start and end apart: 8, of which 1 were waited for; matrix products, arithmetic and copies ran while one was open for 21% of the time, Pallas kernels for 45%

profile of v3, /device:TPU:0, one launch (start us, length us, event | category | flops | bytes accessed | tf_op | source)
XLA Modules:
  0.0 748.9 jit_solution(11718335703456404291)
XLA Ops:
  7.2 2.7 copy.40
  11.9 2.7 convert_element_type.106
  15.9 2.8 convert_reduce_fusion.2
  18.7 3.8 fusion.26
  22.7 4.8 fusion.22.n1_hbm
  27.5 32.3 %all-gather.5.cloned.1.call-done = bf16[3,2048,512]{1,2,0:T(8,128)(2,1)} async-done(((bf16[3,256,512]{1,2,0:T(8,128)(2,1)}), bf16[3,2048,512]{1,2,0:T(8,128)(2,1)}) %all-gather.5.cloned.1.call-update) | async-done | bytes 6291472 | tf_op jit(solution)/shard_map/all_gather | solution.py:471
  59.9 10.1 %fusion.42 = bf16[3,1024,512]{1,2,0:T(8,128)(2,1)S(1)} fusion(f32[3,512]{1,0:T(4,128)S(1)} %pad_maximum_fusion, bf16[3,2048,512]{1,2,0:T(8,128)(2,1)} %all-gather.5.cloned.1.call-done, bf16[1024,2048]{1,0:T(8,128)(2,1)} %fusion.22.n1_hbm), kind=kOutput, calls=%fused_computation.83 | convolution fusion | flops 6445596672 | bytes 13637632 | tf_op jit(solution)/shard_map/td,cdn->ctn/dot_general | solution.py:482
  74.0 32.3 %while.11 = (s32[]{:T(128)}, bf16[2,512,512]{1,2,0:T(8,128)(2,1)}, s32[2]{0:T(128)S(1)}, s32[]{:T(128)}, bf16[1024,512]{0,1:T(8,128)(2,1)S(1)}, /*index=5*/bf16[...) while((s32[]{:T(128)}, bf16[2,512,512]{1,2,0:T(8,128)(2,1)}, ...), condition=%wide.wide.region_5.6_spmd, body=%wide.wide.region_2.5_spmd.sunk | while | flops 1091570176 | bytes 52451608 | solution.py:72
  77.7 6.0 fusion.86
  83.7 5.1 fusion.87
  93.6 6.0 fusion.86
  99.6 5.7 fusion.87
  108.2 4.3 convolution_convert_fusion.2.p_ref
  112.5 110.6 %shard_map.254 = bf16[1024,2048]{1,0:T(8,128)(2,1)S(1)} custom-call(bf16[1024,2048]{1,0:T(8,128)(2,1)S(1)} %convolution_convert_fusion.2.p_ref), custom_call_target="tpu_custom_call" | custom-call | flops 1000 | bytes 1000 | tf_op jit(solution)/shard_map/pallas_call | solution.py:243
  227.8 4.1 add_convert_fusion.2.refs_2_
  231.9 14.5 %fusion.49 = f32[1024,2048]{1,0:T(8,128)} fusion(bf16[1024,2048]{1,0:T(8,128)(2,1)} %add_convert_fusion.2.refs_2_, bf16[2048,2048]{1,0:T(8,128)(2,1)} %all-gather.9.cloned.1.call-done), kind=kOutput, calls=%fused_computation.101 | convolution fusion | flops 8589934592 | bytes 20971520 | tf_op jit(solution)/shard_map/dot_general | solution.py:492
  246.4 33.5 %convert_reduce_fusion.4 = (f32[2048]{0:T(1024)S(1)}, bf16[1024,2048]{1,0:T(8,128)(2,1)S(1)}, f32[1024,2048]{1,0:T(8,128)}) fusion(f32[1024,2048]{1,0:T(8,128)} %fusion.49, f32[2048]{0:T(1024)S(1)} %copy-done.37, bf16[1024,2048]{1,0:T(8,128)(2,1)} %refs_1_.1, bf16[2048,2048]{1,0:T(8,128)(2,1)} %all-gather.11.cloned.1.call-done), kind=kOutput, calls=%fused_computation.56 | convolution fusion | flops 8747218944 | bytes 33570816 | tf_op jit(solution)/shard_map/td,fd->tf/dot_general | solution.py:498
  279.9 10.6 %convolution_convert_fusion.p_ref = bf16[1024,2048]{1,0:T(8,128)(2,1)} fusion(bf16[1024,2048]{1,0:T(8,128)(2,1)S(1)} %get-tuple-element.121.refs_3_, bf16[2048,2048]{1,0:T(8,128)(2,1)S(1)} %copy-done.41), kind=kOutput, calls=%fused_computation.80 | convolution fusion | flops 8592031744 | bytes 16777216 | tf_op jit(solution)/shard_map/tf,df->td/dot_general | solution.py:501
  290.5 9.9 %multiply_convert_fusion.refs_0_ = bf16[1024,2048]{1,0:T(8,128)(2,1)} fusion(f32[1024,2048]{1,0:T(8,128)} %get-tuple-element.122, f32[1024,2048]{1,0:T(8,128)} %fusion.49, f32[2048]{0:T(1024)S(1)} %copy-done.37), kind=kLoop, calls=%fused_computation.60 | loop fusion | flops 8388608 | bytes 20979712 | tf_op jit(solution)/shard_map/convert_element_type | solution.py:494
  300.4 110.1 %shard_map.255 = (bf16[1024,2048]{1,0:T(8,128)(2,1)S(1)}, bf16[2048,2048]{1,0:T(8,128)(2,1)}, bf16[2048,2048]{1,0:T(8,128)(2,1)}) custom-call(bf16[1024,2048]{1,0:T(8,128)(2,1)} %convolution_convert_fusion.p_ref, bf16[1024,2048]{1,0:T(8,128)(2,1)} %multiply_convert_fusion.refs_0_, bf16[1024,2048]{1,0:T(8,128)(2,1)} %refs_1_.1, ...), custom_call_target="tpu_custom_call" | custom-call | flops 1000 | bytes 1000 | tf_op jit(solution)/shard_map/pallas_call | solution.py:318
  418.2 9.7 %fusion.33 = (f32[2048]{0:T(1024)S(1)}, f32[1024]{0:T(1024)S(1)}, f32[1024]{0:T(1024)S(1)}, f32[2048]{0:T(1024)S(1)}) fusion(bf16[1024,2048]{1,0:T(8,128)(2,1)} %copy-done.3, f32[1024]{0:T(1024)S(1)} %copy-done.34, f32[1024]{0:T(1024)S(1)} %copy-done.26, f32[2048]{0:T(1024)S(1)} %copy-done.22, bf16[1024,2048]{1,0:T(8,128)(2,1)} %copy-done, ...), kind=kLoop, calls=%fused_computation.53 | loop fusion | flops 29353984 | bytes 12632064 | tf_op jit(solution)/shard_map/reduce_sum | solution.py:506
  430.0 10.2 %convert_reduce_fusion.5 = (f32[2048]{0:T(1024)S(1)}, bf16[1024,2048]{1,0:T(8,128)(2,1)S(1)}, f32[1024,2048]{1,0:T(8,128)}, f32[2048]{0:T(1024)S(1)}) fusion(f32[1024]{0:T(1024)S(1)} %get-tuple-element.139, f32[1024]{0:T(1024)S(1)} %copy-done.26, f32[2048]{0:T(1024)S(1)} %copy-done.22, bf16[1024,2048]{1,0:T(8,128)(2,1)S(1)} %copy-done.1, ...), kind=kLoop, calls=%fused_computation.57 | loop fusion | flops 37744640 | bytes 29409280 | tf_op jit(solution)/shard_map/reduce_sum | solution.py:510
  440.2 3.3 convolution_convert_fusion.3.d_context
  444.4 10.5 %convolution_convert_fusion.1.p_ref = bf16[1024,2048]{1,0:T(8,128)(2,1)} fusion(bf16[1024,2048]{1,0:T(8,128)(2,1)S(1)} %copy-done.10, bf16[2048,2048]{1,0:T(8,128)(2,1)S(1)} %bitcast.67), kind=kOutput, calls=%fused_computation.81 | convolution fusion | flops 8592031744 | bytes 16777216 | tf_op jit(solution)/shard_map/dot_general | solution.py:495
  454.9 116.8 %shard_map.256 = (bf16[1024,2048]{1,0:T(8,128)(2,1)}, bf16[3,1024,512]{2,1,0:T(8,128)(2,1)}, f32[2,512]{1,0:T(2,128)}, bf16[3,2048,512]{2,1,0:T(8,128)(2,1)}, bf16[512,2048]{1,0:T(8,128)(2,1)}) custom-call(s32[1]{0:T(128)S(6)} %copy.61.prefix_ref, bf16[1024,2048]{1,0:T(8,128)(2,1)} %convolution_convert_fusion.1.p_ref, bf16[1024,512]{1,0:T(8,128)(2,1)} %copy.43.q, ...), custom_call_target="tpu_custom_call" | custom-call | flops 1000 | bytes 1000 | tf_op jit(solution)/shard_map/pallas_call | solution.py:417
  571.8 2.7 convert_element_type.121
  574.5 2.8 convert_element_type.120
  578.1 9.7 %bitcast_convert_fusion.p_ref = bf16[1024,2048]{1,0:T(8,128)(2,1)S(1)} fusion(bf16[3,1024,512]{2,1,0:T(8,128)(2,1)} %get-tuple-element.66, bf16[3,2048,512]{1,2,0:T(8,128)(2,1)} %all-gather.5.cloned.1.call-done), kind=kOutput, calls=%fused_computation.55 | convolution fusion | flops 6444548096 | bytes 13631488 | tf_op jit(solution)/shard_map/ctn,cdn->td/dot_general | solution.py:519
  587.9 106.2 %shard_map.257 = bf16[1024,2048]{1,0:T(8,128)(2,1)S(1)} custom-call(bf16[1024,2048]{1,0:T(8,128)(2,1)S(1)} %bitcast_convert_fusion.p_ref), custom_call_target="tpu_custom_call" | custom-call | flops 1000 | bytes 1000 | tf_op jit(solution)/shard_map/pallas_call | solution.py:243
  696.0 4.3 fusion.34
  700.4 23.5 %all-reduce = (f32[2048]{0:T(1024)}, f32[2048]{0:T(1024)}, f32[2,512]{1,0:T(2,128)}, f32[2048]{0:T(1024)}, f32[2048]{0:T(1024)}, /*index=5*/f32[2048]{0:T(1024)}, f32[2048]{0:T(1024)}, f32[2048]{0:T(1024)}) all-reduce(f32[2048]{0:T(1024)S(1)} %get-tuple-element.92, ...), channel_id=1, replica_groups=mesh['dp'=2,'row'=4,'col'=4] {'dp','col'}, use_global_device_ids=true, to_apply=%region_13.14 | all-reduce | flops 15360 | bytes 122880 | tf_op jit(solution)/shard_map/psum | solution.py:533
  723.9 13.7 %fusion.25 = (f32[1024,2048]{1,0:T(8,128)}, bf16[1024,2048]{1,0:T(8,128)(2,1)}) fusion(f32[1024,2048]{1,0:T(8,128)} %get-tuple-element.125, bf16[1024,2048]{1,0:T(8,128)(2,1)} %param.17, bf16[1024,2048]{1,0:T(8,128)(2,1)} %copy-done.2, f32[1024]{0:T(1024)S(1)} %broadcast_multiply_fusion, f32[1024]{0:T(1024)S(1)} %broadcast_multiply_fusion.1, ...), kind=kLoop, calls=%fused_computation.45 | loop fusion | flops 35651584 | bytes 37789696 | tf_op jit(solution)/shard_map/add | solution.py:532
  (159 shorter events, 38.4 us)
Async XLA Ops:
  7.2 52.7 %all-gather.5.cloned.1.call-start = ((), (), s32[]{:S(2)}) async-start(), calls=%async_computation.4 | async-start | bytes 7077888 | tf_op jit(solution)/shard_map/all_gather | solution.py:471
  10.0 98.2 %all-gather.7.cloned.1.call-start = ((), (), s32[]{:S(2)}) async-start(), calls=%async_computation.5 | async-start | bytes 2359296 | tf_op jit(solution)/shard_map/all_gather | solution.py:472
  11.8 10.8 %copy-start.39 = (f32[2,512]{1,0:T(2,128)S(1)}, f32[2,512]{1,0:T(2,128)}, u32[]{:S(2)}) copy-start(f32[2,512]{1,0:T(2,128)} %param.22) | copy-start | bytes 12292
  11.8 10.9 %copy-start.27 = (f32[2048]{0:T(1024)S(1)}, f32[2048]{0:T(1024)}, u32[]{:S(2)}) copy-start(f32[2048]{0:T(1024)} %param.19) | copy-start | bytes 24580
  11.8 10.9 %copy-start.35 = (f32[2048]{0:T(1024)S(1)}, f32[2048]{0:T(1024)}, u32[]{:S(2)}) copy-start(f32[2048]{0:T(1024)} %param.20) | copy-start | bytes 24580
  11.8 220.1 %all-gather.9.cloned.1.call-start = ((), (), s32[]{:S(2)}) async-start(), calls=%async_computation.6 | async-start | bytes 9437184 | tf_op jit(solution)/shard_map/all_gather | solution.py:473
  14.6 231.7 %all-gather.11.cloned.1.call-start = ((), (), s32[]{:S(2)}) async-start(), calls=%async_computation.7 | async-start | bytes 9437184 | tf_op jit(solution)/shard_map/all_gather | solution.py:474
  15.8 556.0 %reduce-scatter.7.cloned.1.call-start = ((), (), s32[]{:S(2)}) async-start(), calls=%async_computation.9 | async-start | bytes 9437184 | tf_op jit(solution)/shard_map/reduce_scatter | solution.py:443
  18.7 41.2 %copy-start.23 = (f32[1024]{0:T(1024)}, f32[1024]{0:T(1024)S(1)}, u32[]{:S(2)}) copy-start(f32[1024]{0:T(1024)S(1)} %broadcast_multiply_fusion.5) | copy-start | bytes 12292
  22.5 37.4 %copy-start.31 = (f32[1024]{0:T(1024)}, f32[1024]{0:T(1024)S(1)}, u32[]{:S(2)}) copy-start(f32[1024]{0:T(1024)S(1)} %add_rsqrt_fusion.1) | copy-start | bytes 12292
  106.3 116.8 %copy-start.8 = (bf16[1024,512]{0,1:T(8,128)(2,1)}, bf16[1024,512]{0,1:T(8,128)(2,1)S(1)}, u32[]{:S(2)}) copy-start(bf16[1024,512]{0,1:T(8,128)(2,1)S(1)} %get-tuple-element.268) | copy-start | bytes 3145732
  108.2 115.0 %copy-start.16 = (bf16[2,512,512]{2,1,0:T(8,128)(2,1)}, bf16[2,512,512]{2,1,0:T(8,128)(2,1)S(1)}, u32[]{:S(2)}) copy-start(bf16[2,512,512]{2,1,0:T(8,128)(2,1)S(1)} %copy.42) | copy-start | bytes 3145732
  108.2 115.0 %copy-start.5 = (bf16[1024,2048]{1,0:T(8,128)(2,1)S(1)}, bf16[1024,2048]{1,0:T(8,128)(2,1)}, u32[]{:S(2)}) copy-start(bf16[1024,2048]{1,0:T(8,128)(2,1)} %param.17) | copy-start | bytes 12582916
  108.2 115.0 %copy-start.21 = (f32[2048]{0:T(1024)S(1)}, f32[2048]{0:T(1024)}, u32[]{:S(2)}) copy-start(f32[2048]{0:T(1024)} %param.24) | copy-start | bytes 24580
  231.9 14.5 %copy-start.37 = (f32[2048]{0:T(1024)S(1)}, f32[2048]{0:T(1024)}, u32[]{:S(2)}) copy-start(f32[2048]{0:T(1024)} %param.28) | copy-start | bytes 24580
  246.4 33.5 %copy-start.41 = (bf16[2048,2048]{1,0:T(8,128)(2,1)S(1)}, bf16[2048,2048]{1,0:T(8,128)(2,1)}, u32[]{:S(2)}) copy-start(bf16[2048,2048]{1,0:T(8,128)(2,1)} %all-gather.9.cloned.1.call-done) | copy-start | bytes 25165828
  279.9 10.6 %copy-start.12 = (bf16[1024,2048]{1,0:T(8,128)(2,1)}, bf16[1024,2048]{1,0:T(8,128)(2,1)S(1)}, u32[]{:S(2)}) copy-start(bf16[1024,2048]{1,0:T(8,128)(2,1)S(1)} %get-tuple-element.121.refs_3_) | copy-start | bytes 12582916
  412.6 161.9 %reduce-scatter.5.cloned.1.call-start = ((), (), s32[]{:S(2)}) async-start(), calls=%async_computation.8 | async-start | bytes 9437184 | tf_op jit(solution)/shard_map/reduce_scatter | solution.py:443
  413.2 324.3 %reduce-scatter.11.cloned.1.call-start = ((), (), s32[]{:S(2)}) async-start(), calls=%async_computation.11 | async-start | bytes 2359296 | tf_op jit(solution)/shard_map/reduce_scatter | solution.py:443
  418.1 10.4 %copy-start.4 = (bf16[1024,2048]{1,0:T(8,128)(2,1)S(1)}, bf16[1024,2048]{1,0:T(8,128)(2,1)}, u32[]{:S(2)}) copy-start(bf16[1024,2048]{1,0:T(8,128)(2,1)} %copy-done.3) | copy-start | bytes 12582916
  418.1 11.8 %copy-start.6 = (bf16[1024,2048]{1,0:T(8,128)(2,1)S(1)}, bf16[1024,2048]{1,0:T(8,128)(2,1)}, u32[]{:S(2)}) copy-start(bf16[1024,2048]{1,0:T(8,128)(2,1)} %param.17) | copy-start | bytes 12582916
  418.2 25.3 %slice-start = ((s8[8388608]{0:T(1024)(128)(4,1)}), s8[4194304]{0:T(1024)(128)(4,1)S(1)}, s32[]{:S(2)}) async-start(s8[8388608]{0:T(1024)(128)(4,1)} %bitcast.66), calls=%async_computation.12 | async-start | bytes 8388608
  430.0 10.2 %copy-start.42 = (bf16[512,2048]{1,0:T(8,128)(2,1)S(1)}, bf16[512,2048]{1,0:T(8,128)(2,1)}, u32[]{:S(2)}) copy-start(bf16[512,2048]{1,0:T(8,128)(2,1)} %all-gather.7.cloned.1.call-done) | copy-start | bytes 6291460
  430.0 13.5 %slice-start.1 = ((s8[8388608]{0:T(1024)(128)(4,1)}), s8[4194304]{0:T(1024)(128)(4,1)S(1)}, s32[]{:S(2)}) async-start(s8[8388608]{0:T(1024)(128)(4,1)} %bitcast.66), calls=%async_computation.13 | async-start | bytes 8388608
  440.1 14.8 %copy-start.11 = (bf16[1024,2048]{1,0:T(8,128)(2,1)}, bf16[1024,2048]{1,0:T(8,128)(2,1)S(1)}, u32[]{:S(2)}) copy-start(bf16[1024,2048]{1,0:T(8,128)(2,1)S(1)} %get-tuple-element.124.branch_hbm) | copy-start | bytes 12582916
  577.3 162.0 %reduce-scatter.9.cloned.1.call-start = ((), (), s32[]{:S(2)}) async-start(), calls=%async_computation.10 | async-start | bytes 7077888 | tf_op jit(solution)/shard_map/reduce_scatter | solution.py:443
  587.8 108.2 %copy-start.7 = (bf16[1024,2048]{1,0:T(8,128)(2,1)S(1)}, bf16[1024,2048]{1,0:T(8,128)(2,1)}, u32[]{:S(2)}) copy-start(bf16[1024,2048]{1,0:T(8,128)(2,1)} %param.17) | copy-start | bytes 12582916
  587.8 108.2 %copy-start.24 = (f32[1024]{0:T(1024)S(1)}, f32[1024]{0:T(1024)}, u32[]{:S(2)}) copy-start(f32[1024]{0:T(1024)} %copy-done.23) | copy-start | bytes 12292
  587.8 108.2 %copy-start.28 = (f32[2048]{0:T(1024)S(1)}, f32[2048]{0:T(1024)}, u32[]{:S(2)}) copy-start(f32[2048]{0:T(1024)} %param.19) | copy-start | bytes 24580
  587.8 108.2 %copy-start.32 = (f32[1024]{0:T(1024)S(1)}, f32[1024]{0:T(1024)}, u32[]{:S(2)}) copy-start(f32[1024]{0:T(1024)} %copy-done.31) | copy-start | bytes 12292
  587.8 112.5 %copy-start.40 = (f32[2,512]{1,0:T(2,128)S(1)}, f32[2,512]{1,0:T(2,128)}, u32[]{:S(2)}) copy-start(f32[2,512]{1,0:T(2,128)} %get-tuple-element.72) | copy-start | bytes 12292
  587.8 136.0 %copy-start.38 = (f32[2048]{0:T(1024)S(1)}, f32[2048]{0:T(1024)}, u32[]{:S(2)}) copy-start(f32[2048]{0:T(1024)} %param.30) | copy-start | bytes 24580
  (24 other events, 98.9 us)
Sparse Core Ops, SparseCore 0:
  10.5 49.3 all-gather.4
  62.3 28.2 all-gather.6
  92.5 54.3 all-gather.8
  148.7 55.9 all-gather.10
  412.7 70.6 reduce-scatter.6
  487.0 71.2 reduce-scatter.4
  577.4 39.9 reduce-scatter.10
  621.1 61.7 reduce-scatter.8

commit v4 on v3

v4 whole, which is shorter than its diff:
```python
from functools import partial

import jax
import jax.numpy as jnp
from jax import lax
from jax.experimental import pallas as pl
from jax.experimental.pallas import tpu as pltpu
from jax.sharding import PartitionSpec as P

HEAD_DIM = 128
MESH_IDS = pl.DeviceIdType.MESH
CHUNK = 32
LAG = 2


eps_norm = 1e-05


def norm_forward(values, norm_gain, norm_shift):
    average = jnp.mean(values, axis=-1, keepdims=True)
    centered = values - average
    variance = jnp.mean(centered * centered, axis=-1, keepdims=True)
    inverse = lax.rsqrt(variance + eps_norm)
    scaled = centered * inverse
    return (scaled * norm_gain + norm_shift, scaled, inverse)


def norm_backward(grad, scaled, inverse, norm_gain):
    grad_scaled = grad * norm_gain
    return inverse * (
        grad_scaled
        - jnp.mean(grad_scaled, axis=-1, keepdims=True)
        - scaled * jnp.mean(grad_scaled * scaled, axis=-1, keepdims=True)
    )


def dot(left, right, left_dim, right_dim):
    return lax.dot_general(
        left, right, (((left_dim,), (right_dim,)), ((), ())), preferred_element_type=jnp.float32
    )


def greet_row(n, others=()):
    r = lax.axis_index("row")
    last = n - 1
    bar = pltpu.get_barrier_semaphore()
    for cond, dev in ((r > 0, r - 1), (r < last, r + 1)):

        @pl.when(cond)
        def _():
            pl.semaphore_signal(bar, inc=1, device_id={"row": dev}, device_id_type=MESH_IDS)

    for other in others:
        pl.semaphore_signal(bar, inc=1, device_id=other, device_id_type=MESH_IDS)
    inside = (r > 0) & (r < last)

    @pl.when(inside)
    def _():
        pl.semaphore_wait(bar, 2 + len(others))

    @pl.when(jnp.logical_not(inside))
    def _():
        pl.semaphore_wait(bar, 1 + len(others))


def plane_partners():
    y, x = lax.axis_index("dp"), lax.axis_index("col")
    far_x, near = lax.rem(x + 2, 4), x + 1 - 2 * lax.rem(x, 2)
    far_near = lax.rem(near + 2, 4)
    ids = {"x": {"col": far_x}, "y": {"dp": 1 - y}, "near": {"col": near}}
    mine = {"own": y * 4 + x, "x": y * 4 + far_x, "y": (1 - y) * 4 + x, "xy": (1 - y) * 4 + far_x}
    theirs = {
        "own": y * 4 + near,
        "x": y * 4 + far_near,
        "y": (1 - y) * 4 + near,
        "xy": (1 - y) * 4 + far_near,
    }
    return ids, mine, theirs


KINDS = ("own", "x", "y", "xy")


def plane_gather(pieces, send_sem, recv_sem, near_send, near_recv, local_sem):
    ids, mine, theirs = plane_partners()
    count = len(pieces)

    def remote(kind, k, to, src, dst):
        row = KINDS.index(kind)
        near = to == "near"
        return pltpu.make_async_remote_copy(
            src_ref=src,
            dst_ref=dst,
            send_sem=(near_send if near else send_sem).at[row, k],
            recv_sem=(near_recv if near else recv_sem).at[row, k],
            device_id=ids[to],
            device_id_type=MESH_IDS,
        )

    def outgoing(k):
        own, place = pieces[k](mine["own"])
        return [remote("x", k, "x", own, place), remote("y", k, "y", own, place)]

    def local(k):
        own, place = pieces[k](mine["own"])
        return pltpu.make_async_copy(own, place, local_sem.at[k])

    def onward(k):
        kind, to = ("x", "y") if k % 2 == 0 else ("y", "x")
        place = pieces[k](mine[kind])[1]
        return remote("xy", k, to, place, place)

    def share(kind, k):
        own, place = pieces[k](mine[kind])
        return remote(kind, k, "near", own if kind == "own" else place, place)

    def start():
        for k in range(count):
            for copy in outgoing(k):
                copy.start()
        for k in range(count):
            share("own", k).start()
            local(k).start()

    def arrive(k):
        for copy in outgoing(k):
            copy.wait_recv()
        onward(k).start()
        share("x", k).start()
        share("y", k).start()

    def arrive_far(k):
        onward(k).wait_recv()
        share("xy", k).start()

    def finish():
        for k in range(count):
            local(k).wait()
            for copy in outgoing(k):
                copy.wait_send()
            onward(k).wait_send()
            for kind in KINDS:
                place = pieces[k](theirs[kind])[1]
                share(kind, k).wait_send()
                remote(kind, k, "near", place, place).wait_recv()

    return list(ids.values()), start, arrive, arrive_far, finish


def line_sum(n, p_ref, o_ref, held, rs_s, rs_r, ag_s, ag_r, loc):
    half = p_ref.shape[0] // 2
    chunks = half // CHUNK
    r = lax.axis_index("row")
    last = n - 1
    place = (r, last - r)
    after = (jnp.minimum(r + 1, last), jnp.maximum(r - 1, 0))
    before = (jnp.maximum(r - 1, 0), jnp.minimum(r + 1, last))

    def rows(d, c):
        return pl.ds(pl.multiple_of((half if d == 0 else 0) + c * CHUNK, CHUNK), CHUNK)

    def onward(d, c, src):
        return pltpu.make_async_remote_copy(
            src_ref=src.at[rows(d, c)],
            dst_ref=held.at[rows(d, c)],
            send_sem=rs_s.at[d, c],
            recv_sem=rs_r.at[d, c],
            device_id={"row": after[d]},
            device_id_type=MESH_IDS,
        )

    def back(d, c, src):
        return pltpu.make_async_remote_copy(
            src_ref=src.at[rows(d, c)],
            dst_ref=o_ref.at[rows(d, c)],
            send_sem=ag_s.at[d, c],
            recv_sem=ag_r.at[d, c],
            device_id={"row": before[d]},
            device_id_type=MESH_IDS,
        )

    def keep(d, c):
        return pltpu.make_async_copy(held.at[rows(d, c)], o_ref.at[rows(d, c)], loc.at[c])

    def step(t):
        for d in (0, 1):

            @pl.when((place[d] == 0) & (t >= 0) & (t < chunks))
            def _():
                onward(d, t, p_ref).start()

            c = t - LAG * place[d]

            @pl.when((place[d] > 0) & (c >= 0) & (c < chunks))
            def _():
                onward(d, c, p_ref).wait_recv()
                here = rows(d, c)
                held[here] = (
                    held[here].astype(jnp.float32) + p_ref[here].astype(jnp.float32)
                ).astype(jnp.bfloat16)

                @pl.when(place[d] < last)
                def _():
                    onward(d, c, held).start()

                @pl.when(place[d] == last)
                def _():
                    back(d, c, held).start()
                    keep(d, c).start()

        for d in (0, 1):
            c = t - LAG * (2 * last - place[d])

            @pl.when((place[d] < last) & (c >= 0) & (c < chunks))
            def _():
                back(d, c, o_ref).wait_recv()

                @pl.when(place[d] > 0)
                def _():
                    back(d, c, o_ref).start()

    def settle(c):
        for d in (0, 1):

            @pl.when(place[d] < last)
            def _():
                onward(d, c, p_ref).wait_send()

            @pl.when(place[d] == last)
            def _():
                keep(d, c).wait()

    def finish(c):
        for d in (0, 1):

            @pl.when(place[d] > 0)
            def _():
                back(d, c, o_ref).wait_send()

    def drain():
        def both(c):
            settle(c)
            finish(c)

        loop(0, chunks, both)

    return step, drain, settle, lambda: loop(0, chunks, finish)


def line_steps(n, total_rows):
    return total_rows // 2 // CHUNK + LAG * 2 * (n - 1)


def line_scratch(shape):
    chunks = shape[0] // 2 // CHUNK
    dma = pltpu.SemaphoreType.DMA
    return [
        pltpu.VMEM(shape, jnp.bfloat16),
        dma((2, chunks)),
        dma((2, chunks)),
        dma((2, chunks)),
        dma((2, chunks)),
        dma((chunks,)),
    ]


def loop(start, stop, body):
    def one(t, carry):
        body(t)
        return carry

    lax.fori_loop(start, stop, one, 0)


COST = pl.CostEstimate(flops=1000, bytes_accessed=1000, transcendentals=0)
IN_VMEM = pl.BlockSpec(memory_space=pltpu.VMEM)
IN_HBM = pl.BlockSpec(memory_space=pl.ANY)


def low_shape(*shape):
    return jax.ShapeDtypeStruct(shape, jnp.bfloat16)


def kernel_params(collective_id, mib):
    return pltpu.CompilerParams(
        collective_id=collective_id, has_side_effects=True, vmem_limit_bytes=mib * 2**20
    )


def sum_row_kernel(n, p_ref, o_ref, *line):
    greet_row(n)
    step, drain = line_sum(n, p_ref, o_ref, *line)[:2]
    loop(0, line_steps(n, p_ref.shape[0]), step)
    drain()


def sum_row(partial_low):
    return pl.pallas_call(
        partial(sum_row_kernel, lax.axis_size("row")),
        out_shape=low_shape(*partial_low.shape),
        in_specs=[IN_VMEM],
        out_specs=IN_HBM,
        scratch_shapes=line_scratch(partial_low.shape),
        compiler_params=kernel_params(0, 16),
        cost_estimate=COST,
    )(partial_low)


TILE = 512
BLOCK = 256


def mlp_sums_kernel(
    n, spread, ctx, w_out, b_out, gain, shift, b_in, src_hbm, w_in_hbm, w_down_hbm, g_hbm,
    branch, d_normed, mlp, d_wdown, d_win, d_bin,
    p, w_in, w_down, g, normed, act, d_pre, mlp_acc, d_acc, rows_a, rows_b, stage, w_stage,
    load_sem, block_sem, mlp_sem, store_sem, *more,
):
    tokens, depth = p.shape
    units = act.shape[1]
    half = tokens // 2
    part = BLOCK // 2
    blocks = tokens // BLOCK
    per_block = part // CHUNK
    quarters = units // TILE

    def sides(j):
        low_rows = pl.ds(pl.multiple_of(j * part, part), part)
        high_rows = pl.ds(pl.multiple_of(half + j * part, part), part)
        return low_rows, high_rows

    def own(j, side=None):
        if side is None:
            return pl.ds(pl.multiple_of(j * BLOCK, BLOCK), BLOCK)
        return pl.ds(pl.multiple_of(j * BLOCK + side * part, part), part)

    lines, gather_sems = more[:12], more[12:]
    loads = []
    others = []
    if spread:
        deep, wide = w_in_hbm.shape[0], w_down_hbm.shape[1]

        def in_piece(k, place):
            size = deep // 2
            there = pl.ds(pl.multiple_of(place * deep + k * size, size), size)
            return w_in_hbm.at[pl.ds(k * size, size)], w_in.at[there]

        def down_piece(k, place):
            some = pl.ds(k * (units // 2), units // 2)
            cols = pl.ds(pl.multiple_of(place * wide, wide), wide)
            return w_down_hbm.at[some], w_down.at[some, cols]

        pieces = [partial(f, k) for f in (in_piece, down_piece) for k in range(2)]
        others, start_gather, arrive, arrive_far, finish_gather = plane_gather(
            pieces, *gather_sems
        )
    else:
        loads = [
            pltpu.make_async_copy(w_in_hbm, w_in, load_sem.at[0]),
            pltpu.make_async_copy(w_down_hbm, w_down, load_sem.at[1]),
        ]
    for j in range(blocks):
        for side, here in enumerate((j * part, half + j * part)):
            loads.append(
                pltpu.make_async_copy(
                    g_hbm.at[pl.ds(here, part)],
                    g.at[pl.ds(j * BLOCK + side * part, part)],
                    load_sem.at[2 + 2 * j + side],
                )
            )
    for load in loads:
        load.start()
    d_bin[...] = jnp.zeros_like(d_bin)
    greet_row(n, others)
    if spread:
        start_gather()
    step1, _, settle1, finish1 = line_sum(n, p, branch, *lines[:6])
    step2, drain2, _, _ = line_sum(n, p, d_normed, *lines[6:])

    def project(j):
        low_rows, high_rows = sides(j)
        both = jnp.concatenate([ctx[low_rows], ctx[high_rows]], axis=0)
        for c in range(0, depth, TILE):
            cols = slice(c, c + TILE)
            term = dot(both, w_out[:, cols], 1, 0).astype(jnp.bfloat16)
            p[low_rows, cols] = term[:part]
            p[high_rows, cols] = term[part:]
        loop(j * per_block, (j + 1) * per_block, step1)

    for j in range(blocks):
        project(j)
        if spread and j == blocks - 2:
            for k in range(len(pieces)):
                arrive(k)
    if spread:
        for k in range(len(pieces)):
            arrive_far(k)
        finish_gather()
    for load in loads:
        load.wait()

    def norm_block(j):
        loop(j * per_block, (j + 1) * per_block, settle1)
        copies = []
        for i, (src, dst) in enumerate(((branch, rows_a), (src_hbm, rows_b))):
            for side, here in enumerate(sides(j)):
                copies.append(
                    pltpu.make_async_copy(
                        src.at[here], dst.at[pl.ds(side * part, part)], block_sem.at[i, side]
                    )
                )
        for copy in copies:
            copy.start()
        for copy in copies:
            copy.wait()

        def few(k):
            here = pl.ds(pl.multiple_of(k * 64, 64), 64)
            there = pl.ds(pl.multiple_of(j * BLOCK + k * 64, 64), 64)
            source = rows_b[here].astype(jnp.float32)
            hidden = source + rows_a[here].astype(jnp.float32) + b_out[...]
            normed[there] = norm_forward(hidden, gain[...], shift[...])[0].astype(jnp.bfloat16)

        loop(0, BLOCK // 64, few)

    def mlp_out(j):
        return [
            pltpu.make_async_copy(
                stage.at[pl.ds(side * part, part)], mlp.at[here], mlp_sem.at[side]
            )
            for side, here in enumerate(sides(j))
        ]

    first = tokens // 2 // CHUNK

    def block(j):
        for q in range(quarters):
            t = first + j * per_block + q
            step1(t)
            step2(t - first - per_block)
            if q == 0:
                norm_block(j)
            units_q = slice(q * TILE, (q + 1) * TILE)
            here = own(j)
            pre = dot(normed[here], w_in[:, units_q], 1, 0) + b_in[:, units_q]
            d_act = dot(g[here], w_down[units_q], 1, 1)
            lower = 0.5 * (1.0 + lax.erf(pre * 0.5**0.5))
            act[here, units_q] = (pre * lower).astype(jnp.bfloat16)
            slope = lower + pre * (jnp.exp(-0.5 * pre * pre) * (0.5 / jnp.pi) ** 0.5)
            low_pre = (d_act * slope).astype(jnp.bfloat16)
            d_pre[here, units_q] = low_pre
            d_bin[:, units_q] += jnp.sum(low_pre.astype(jnp.float32), axis=0, keepdims=True)
            for c in range(0, depth, TILE):
                cols = slice(c, c + TILE)
                m_term = dot(act[here, units_q], w_down[units_q, cols], 1, 0)
                d_term = dot(d_pre[here, units_q], w_in[cols, units_q], 1, 1)
                if q == 0:
                    mlp_acc[:, cols] = m_term
                    d_acc[:, cols] = d_term
                elif q < quarters - 1:
                    mlp_acc[:, cols] += m_term
                    d_acc[:, cols] += d_term
                else:
                    if c == 0:

                        @pl.when(j > 0)
                        def _():
                            for copy in mlp_out(j - 1):
                                copy.wait()

                    stage[:, cols] = (mlp_acc[:, cols] + m_term).astype(jnp.bfloat16)
                    d_low = (d_acc[:, cols] + d_term).astype(jnp.bfloat16)
                    for side, rows in enumerate(sides(j)):
                        p[rows, cols] = d_low[side * part : (side + 1) * part]
        for copy in mlp_out(j):
            copy.start()

    loop(0, blocks, block)
    begin = first
    steps = line_steps(n, tokens)
    tick = tokens // 2 // CHUNK - per_block
    jobs = ((act, g, d_wdown), (normed, d_pre, d_win))
    for k, (left, right, out) in enumerate(jobs):
        across = out.shape[1] // TILE
        tiles = (out.shape[0] // TILE) * across

        def store(tile, slot):
            m = pl.ds(pl.multiple_of((tile // across) * TILE, TILE), TILE)
            c = pl.ds(pl.multiple_of(lax.rem(tile, across) * TILE, TILE), TILE)
            copy = pltpu.make_async_copy(w_stage.at[slot], out.at[m, c], store_sem.at[slot])
            return m, c, copy

        def body(u):
            step2(tick + k * (tiles // 2) + u)
            for slot in range(2):
                m, c, copy = store(2 * u + slot, slot)
                if k == 0:

                    @pl.when(u > 0)
                    def _():
                        copy.wait()
                else:
                    copy.wait()
                w_stage[slot] = dot(left[:, m], right[:, c], 0, 0).astype(jnp.bfloat16)
                copy.start()

        loop(0, tiles // 2, body)
        tick_end = tick + (k + 1) * (tiles // 2)
    if tick_end < steps:
        loop(tick_end, steps, step2)
    for slot in range(2):
        store(slot, slot)[2].wait()
    for copy in mlp_out(blocks - 1):
        copy.wait()
    finish1()
    drain2()


def mlp_sums(context, w_out, b_out, gain, shift, b_in, inputs, w_in, w_down, d_output):
    tokens, depth = inputs.shape
    units = w_in.shape[1]
    spread = w_in.shape[0] < depth
    dma = pltpu.SemaphoreType.DMA
    low_buffer = lambda *shape: pltpu.VMEM(shape, jnp.bfloat16)
    return pl.pallas_call(
        partial(mlp_sums_kernel, lax.axis_size("row"), spread),
        out_shape=[
            low_shape(tokens, depth),
            low_shape(tokens, depth),
            low_shape(tokens, depth),
            low_shape(units, depth),
            low_shape(depth, units),
            jax.ShapeDtypeStruct((1, units), jnp.float32),
        ],
        in_specs=[IN_VMEM] * 6 + [IN_HBM] * 4,
        out_specs=[IN_HBM] * 5 + [IN_VMEM],
        scratch_shapes=[
            low_buffer(tokens, depth),
            low_buffer(depth, units),
            low_buffer(units, depth),
            low_buffer(tokens, depth),
            low_buffer(tokens, depth),
            low_buffer(tokens, units),
            low_buffer(tokens, units),
            pltpu.VMEM((BLOCK, depth), jnp.float32),
            pltpu.VMEM((BLOCK, depth), jnp.float32),
            low_buffer(BLOCK, depth),
            low_buffer(BLOCK, depth),
            low_buffer(BLOCK, depth),
            low_buffer(2, TILE, TILE),
            dma((2 + 2 * (tokens // BLOCK),)),
            dma((2, 2)),
            dma((2,)),
            dma((2,)),
        ]
        + line_scratch((tokens, depth))
        + line_scratch((tokens, depth))
        + ([dma((4, 4))] * 4 + [dma((4,))] if spread else []),
        compiler_params=kernel_params(1, 61),
        cost_estimate=COST,
    )(
        context, w_out, b_out[None], gain[None], shift[None], b_in[None],
        inputs, w_in, w_down, d_output,
    )


QUERY_ROWS = 256


def block_probs(i, prefix, cols, q, k):
    start = i * QUERY_ROWS
    width = max(start + QUERY_ROWS, q.shape[0] // 2)
    here = slice(start, start + QUERY_ROWS)
    scores = dot(k[:width, cols], q[here, cols], 1, 1) * HEAD_DIM ** (-0.5)
    key = lax.broadcasted_iota(jnp.int32, scores.shape, 0)
    query = lax.broadcasted_iota(jnp.int32, scores.shape, 1) + start
    scores = jnp.where((key <= query) | (key < prefix), scores, -1000000000.0)
    expo = jnp.exp(scores - jnp.max(scores, axis=0, keepdims=True))
    return here, width, expo * (1.0 / jnp.sum(expo, axis=0, keepdims=True))


def attend_kernel(prefix_ref, projected, context):
    q, k, v = (projected.at[c] for c in range(3))
    prefix = prefix_ref[0]

    def head(h):
        cols = pl.ds(pl.multiple_of(h * HEAD_DIM, HEAD_DIM), HEAD_DIM)
        v_t = v[:, cols].T
        for i in range(q.shape[0] // QUERY_ROWS):
            here, width, probs = block_probs(i, prefix, cols, q, k)
            out = dot(v_t[:, :width], probs.astype(jnp.bfloat16), 1, 0)
            context[here, cols] = out.T.astype(jnp.bfloat16)

    loop(0, q.shape[1] // HEAD_DIM, head)


def attend(prefix_len, projected):
    return pl.pallas_call(
        attend_kernel,
        out_shape=low_shape(*projected.shape[1:]),
        in_specs=[pl.BlockSpec(memory_space=pltpu.SMEM), IN_VMEM],
        out_specs=IN_VMEM,
        compiler_params=pltpu.CompilerParams(vmem_limit_bytes=32 * 2**20),
        cost_estimate=COST,
    )(prefix_len, projected)


def attend_piece(i, prefix, cols, q, k, v, k_t, d_context, d_proj, d_key, d_value, first):
    score_scale = HEAD_DIM ** (-0.5)
    here, width, probs = block_probs(i, prefix, cols, q, k)
    q_block, g_block = q[here, cols], d_context[here, cols]
    d_probs = dot(v[:width, cols], g_block, 1, 1)
    inner = jnp.sum(d_probs * probs, axis=0, keepdims=True)
    d_scores = (probs * (d_probs - inner)).astype(jnp.bfloat16)
    d_query = dot(k_t[:, :width], d_scores, 1, 0) * score_scale
    d_proj[0, here, cols] = d_query.T.astype(jnp.bfloat16)
    for total, term in (
        (d_key, dot(d_scores, q_block, 1, 0)),
        (d_value, dot(probs.astype(jnp.bfloat16), g_block, 1, 0)),
    ):
        if first:
            total[...] = term
        else:
            total[:width] += term


def attend_sum_kernel(
    n, prefix_ref, p_ref, projected, d_context, n1_hbm, ctx_hbm, branch_hbm,
    o_ref, d_proj, d_bias, d_wqkv, d_wout,
    n1, ctx, branch, d_key, d_value, load_sem, *line,
):
    loads = [
        pltpu.make_async_copy(src, dst, load_sem.at[i])
        for i, (src, dst) in enumerate(((n1_hbm, n1), (ctx_hbm, ctx), (branch_hbm, branch)))
    ]
    for load in loads:
        load.start()
    greet_row(n)
    step, drain = line_sum(n, p_ref, o_ref, *line)[:2]
    steps = line_steps(n, p_ref.shape[0])
    prefix = prefix_ref[0]
    q, k, v = (projected.at[c] for c in range(3))
    blocks = q.shape[0] // QUERY_ROWS
    heads = q.shape[1] // HEAD_DIM

    def head(h):
        cols = pl.ds(pl.multiple_of(h * HEAD_DIM, HEAD_DIM), HEAD_DIM)
        k_t = k[:, cols].T
        for j in range(blocks):
            step(h * blocks + j)
            attend_piece(
                blocks - 1 - j, prefix, cols, q, k, v, k_t, d_context, d_proj, d_key, d_value,
                j == 0,
            )
        d_proj[1, :, cols] = (d_key[...] * HEAD_DIM ** (-0.5)).astype(jnp.bfloat16)
        d_proj[2, :, cols] = d_value[...].astype(jnp.bfloat16)
        for b, c in ((0, 0), (1, 2)):
            d_bias[b : b + 1, cols] = jnp.sum(
                d_proj[c, :, cols].astype(jnp.float32), axis=0, keepdims=True
            )

    loop(0, heads, head)
    for load in loads:
        load.wait()
    begin = heads * blocks
    tiles = n1.shape[1] // TILE

    for c in range(3):

        def body(t):
            step(t)
            m = pl.ds(pl.multiple_of((t - begin - c * tiles) * TILE, TILE), TILE)
            d_wqkv[c, m] = dot(n1[:, m], d_proj[c], 0, 0).astype(jnp.bfloat16)
            if c == 0:
                d_wout[:, m] = dot(ctx[...], branch[:, m], 0, 0).astype(jnp.bfloat16)

        loop(begin + c * tiles, begin + (c + 1) * tiles, body)
    loop(begin + 3 * tiles, steps, step)
    drain()


def attend_sum(prefix_len, partial_low, projected, d_context, normed1, context, d_branch):
    _, tokens, width = projected.shape
    depth = normed1.shape[1]
    dma = pltpu.SemaphoreType.DMA
    return pl.pallas_call(
        partial(attend_sum_kernel, lax.axis_size("row")),
        out_shape=[
            low_shape(*partial_low.shape),
            low_shape(3, tokens, width),
            jax.ShapeDtypeStruct((2, width), jnp.float32),
            low_shape(3, depth, width),
            low_shape(width, depth),
        ],
        in_specs=[pl.BlockSpec(memory_space=pltpu.SMEM)] + [IN_VMEM] * 3 + [IN_HBM] * 3,
        out_specs=[IN_HBM] + [IN_VMEM] * 4,
        scratch_shapes=[
            pltpu.VMEM((tokens, depth), jnp.bfloat16),
            pltpu.VMEM((tokens, width), jnp.bfloat16),
            pltpu.VMEM((tokens, depth), jnp.bfloat16),
            pltpu.VMEM((tokens, HEAD_DIM), jnp.float32),
            pltpu.VMEM((tokens, HEAD_DIM), jnp.float32),
            dma((3,)),
        ]
        + line_scratch(partial_low.shape),
        compiler_params=kernel_params(2, 56),
        cost_estimate=COST,
    )(prefix_len, partial_low, projected, d_context, normed1, context, d_branch)


def scatter_low(grad, dim):
    summed = lax.psum_scatter(grad, ("dp", "col"), scatter_dimension=dim, tiled=True)
    return summed.astype(jnp.float32)


def local(
    inputs,
    prefix_len,
    norm1_gain,
    norm1_shift,
    w_qkv,
    b_qv,
    w_out,
    b_out,
    norm2_gain,
    norm2_shift,
    w_in,
    b_in,
    w_down,
    b_down,
    d_output,
):
    low_mats = (
        w_qkv.astype(jnp.bfloat16),
        w_out.astype(jnp.bfloat16),
        w_in.astype(jnp.bfloat16),
        w_down.astype(jnp.bfloat16),
    )
    full_qkv, full_out, full_in, full_down = (
        lax.all_gather(low_mats[0], ("dp", "col"), axis=1, tiled=True),
        lax.all_gather(low_mats[1], ("dp", "col"), axis=1, tiled=True),
        low_mats[2],
        low_mats[3],
    )
    if (lax.axis_size("dp"), lax.axis_size("col")) != (2, 4):
        full_in = lax.all_gather(full_in, ("dp", "col"), axis=0, tiled=True)
        full_down = lax.all_gather(full_down, ("dp", "col"), axis=1, tiled=True)
    source = inputs.astype(jnp.float32)
    normed1, scaled1, inverse1 = norm_forward(source, norm1_gain, norm1_shift)
    normed1_low = normed1.astype(jnp.bfloat16)
    projected = jnp.einsum("td,cdn->ctn", normed1_low, full_qkv, preferred_element_type=jnp.float32)
    bias_rows = jnp.stack([b_qv[0], jnp.zeros_like(b_qv[0]), b_qv[1]])
    projected = (projected + bias_rows[:, None, :]).astype(jnp.bfloat16)
    context_low = attend(prefix_len, projected)
    attn_sum, summed2, mlp_partial, grad_wdown, grad_win, grad_bin = mlp_sums(
        context_low, full_out, b_out, norm2_gain, norm2_shift, b_in,
        inputs, full_in, full_down, d_output,
    )
    grad_bin = grad_bin[0]
    hidden = source + attn_sum.astype(jnp.float32) + b_out
    _, scaled2, inverse2 = norm_forward(hidden, norm2_gain, norm2_shift)
    grad_top = d_output.astype(jnp.float32)
    grad_bdown = jnp.sum(grad_top, axis=0)
    grad_normed2 = summed2.astype(jnp.float32)
    grad_gain2 = jnp.sum(grad_normed2 * scaled2, axis=0)
    grad_shift2 = jnp.sum(grad_normed2, axis=0)
    grad_hidden = grad_top + norm_backward(grad_normed2, scaled2, inverse2, norm2_gain)
    grad_branch = grad_hidden.astype(jnp.bfloat16)
    grad_bout = jnp.sum(grad_branch.astype(jnp.float32), axis=0)
    grad_context = jnp.einsum(
        "td,rd->tr", grad_branch, full_out, preferred_element_type=jnp.float32
    ).astype(jnp.bfloat16)
    mlp_sum, grad_projected, grad_bqv, grad_wqkv, grad_wout = attend_sum(
        prefix_len, mlp_partial, projected, grad_context, normed1_low, context_low, grad_branch
    )
    output = (hidden + mlp_sum.astype(jnp.float32) + b_down).astype(jnp.bfloat16)
    norm1_partial = jnp.einsum(
        "ctn,cdn->td", grad_projected, full_qkv, preferred_element_type=jnp.float32
    )
    sent_win = scatter_low(grad_win, 0)
    sent_wdown = scatter_low(grad_wdown, 1)
    norm1_low = norm1_partial.astype(jnp.bfloat16)
    grad_wqkv, grad_wout, sent_win, sent_wdown = lax.optimization_barrier(
        (grad_wqkv, grad_wout, sent_win, sent_wdown)
    )
    sent_wout, sent_wqkv = scatter_low(grad_wout, 1), scatter_low(grad_wqkv, 1)
    grad_normed1 = sum_row(norm1_low).astype(jnp.float32)
    grad_gain1 = jnp.sum(grad_normed1 * scaled1, axis=0)
    grad_shift1 = jnp.sum(grad_normed1, axis=0)
    d_inputs = grad_hidden + norm_backward(grad_normed1, scaled1, inverse1, norm1_gain)
    small = lax.psum(
        (
            grad_gain1,
            grad_shift1,
            grad_bqv,
            grad_bout,
            grad_gain2,
            grad_shift2,
            grad_bin,
            grad_bdown,
        ),
        ("dp", "col"),
    )
    return (
        output,
        d_inputs,
        small[0],
        small[1],
        sent_wqkv,
        small[2],
        sent_wout,
        small[3],
        small[4],
        small[5],
        sent_win,
        small[6],
        sent_wdown,
        small[7],
    )


def solution(mesh):
    return jax.shard_map(
        local,
        mesh=mesh,
        in_specs=(
            P(("dp", "col"), None),
            P(("dp", "col")),
            P(),
            P(),
            P(None, ("dp", "col"), "row"),
            P(None, "row"),
            P("row", ("dp", "col")),
            P(),
            P(),
            P(),
            P(("dp", "col"), "row"),
            P("row"),
            P("row", ("dp", "col")),
            P(),
            P(("dp", "col"), None),
        ),
        out_specs=(
            P(("dp", "col"), None),
            P(("dp", "col"), None),
            P(),
            P(),
            P(None, ("dp", "col"), "row"),
            P(None, "row"),
            P("row", ("dp", "col")),
            P(),
            P(),
            P(),
            P(("dp", "col"), "row"),
            P("row"),
            P("row", ("dp", "col")),
            P(),
        ),
        check_vma=False,
    )
```

time: 752 us -> 635 us (0.84)
  matrix products: 110 us -> 23.2 us
  other arithmetic: 96.9 us -> 62.9 us
  local copies, waits for them, and re-layouts: 23.6 us -> 5.46 us
  waiting for transfers between devices: 33.7 us -> 45.6 us
  Pallas kernels: 444 us -> 452 us
    pallas_call x1 -> x2, Pallas kernels: 110 us -> 225 us  [the longest x1 215 us: mlp_sums(): pl.pallas_call(partial(mlp_sums_kernel, lax.axis_size('row'), spread), ou...]
    pallas_call x2 -> x1, Pallas kernels: 217 us -> 110 us  [sum_row(): pl.pallas_call(partial(sum_row_kernel, lax.axis_size('row')), out_shape=l...]
    dot_general x9 -> x0, matrix products: 86.8 us -> none  [the longest x1 33.5 us: local(): jnp.einsum('td,fd->tf', d_output, full_down, preferred_element_type=jnp.f...]
    sub x2 -> x0, other arithmetic: 12 us -> none  [one_block(): expo = jnp.exp(scores - row_max[..., None])]
    convert_element_type x2 -> x1, other arithmetic: 14.1 us -> 2.52 us  [local(): w_qkv.astype(jnp.bfloat16)]
  transfers between devices with their start and end apart: 8 -> 6, of which waited for: 1 -> 3; matrix products, arithmetic and copies ran while one was open for 21% -> 12% of each run, Pallas kernels for 45% -> 38%
where the time goes in v4:
time: 635 us; the launch traced here: 628 us
  Pallas kernels  452 us (71%)
  other arithmetic  62.9 us (10%)
  waiting for transfers between devices  45.6 us (7%)
  blocking collectives  23.4 us (4%)
  matrix products  23.2 us (4%)
  between operations  15.7 us (2%)
    pallas_call x1, Pallas kernels, mlp_sums(): pl.pallas_call(partial(mlp_sums_kernel, lax.axis_size('row'), spread), ou...  215 us
    pallas_call x1, Pallas kernels, attend_sum(): pl.pallas_call(partial(attend_sum_kernel, lax.axis_size('row')), out_shap...  117 us
    pallas_call x1, Pallas kernels, sum_row(): pl.pallas_call(partial(sum_row_kernel, lax.axis_size('row')), out_shape=l...  110 us
    all_gather x1, waiting for transfers between devices, local(): lax.all_gather(low_mats[0], ('dp', 'col'), axis=1, tiled=True)  37.6 us
    psum x1, blocking collectives, local(): lax.psum((grad_gain1, grad_shift1, grad_bqv, grad_bout, grad_gain2, grad_...  23.4 us
    add x1, other arithmetic, local(): grad_hidden + norm_backward(grad_normed1, scaled1, inverse1, norm1_gain)  13.6 us
  transfers between devices with their start and end apart: 6, of which 3 were waited for; matrix products, arithmetic and copies ran while one was open for 12% of the time, Pallas kernels for 38%

profile of v4, /device:TPU:0, one launch (start us, length us, event | category | flops | bytes accessed | tf_op | source)
XLA Modules:
  0.0 628.1 jit_solution(10763241766231084942)
XLA Ops:
  7.3 2.5 convert_element_type.67
  9.9 1.8 convert_element_type.70
  12.5 3.0 convert_reduce_fusion.2
  15.5 1.1 convert_element_type.71.w_in_hbm
  16.7 1.2 fusion.15
  18.0 3.1 fusion.11.n1_hbm
  21.2 37.6 %all-gather.3.cloned.1.call-done = bf16[3,2048,512]{2,1,0:T(8,128)(2,1)} async-done(((bf16[3,256,512]{2,1,0:T(8,128)(2,1)}), bf16[3,2048,512]{2,1,0:T(8,128)(2,1)}) %all-gather.3.cloned.1.call-update) | async-done | bytes 6291472 | tf_op jit(solution)/shard_map/all_gather | solution.py:740
  58.8 10.1 %fusion.26.projected = bf16[3,1024,512]{2,1,0:T(8,128)(2,1)S(1)} fusion(f32[3,512]{1,0:T(4,128)S(1)} %pad_maximum_fusion, bf16[3,2048,512]{2,1,0:T(8,128)(2,1)} %all-gather.3.cloned.1.call-done, bf16[1024,2048]{1,0:T(8,128)(2,1)} %fusion.11.n1_hbm), kind=kOutput, calls=%fused_computation.43 | convolution fusion | flops 6445596672 | bytes 13637632 | tf_op jit(solution)/shard_map/td,cdn->ctn/dot_general | solution.py:751
  68.9 1.2 convert_element_type.72.w_down_hbm
  70.1 0.8 copy-done.1
  70.9 10.9 %shard_map.254.ctx.ctx_hbm = bf16[1024,512]{1,0:T(8,128)(2,1)S(1)} custom-call(s32[1]{0:T(128)S(6)} %copy.29.prefix_ref, bf16[3,1024,512]{2,1,0:T(8,128)(2,1)S(1)} %fusion.26.projected), custom_call_target="tpu_custom_call" | custom-call | flops 1000 | bytes 1000 | tf_op jit(solution)/shard_map/pallas_call | solution.py:598
  81.8 1.0 copy-done.2
  82.8 6.7 %all-gather.5.cloned.1.call-done.w_out = bf16[512,2048]{1,0:T(8,128)(2,1)} async-done(((bf16[512,256]{1,0:T(8,128)(2,1)}), bf16[512,2048]{1,0:T(8,128)(2,1)}) %all-gather.5.cloned.1.call-update) | async-done | bytes 2097168 | tf_op jit(solution)/shard_map/all_gather | solution.py:741
  89.5 214.6 %shard_map.255 = (bf16[1024,2048]{1,0:T(8,128)(2,1)}, bf16[1024,2048]{1,0:T(8,128)(2,1)}, bf16[1024,2048]{1,0:T(8,128)(2,1)}, bf16[2048,2048]{1,0:T(8,128)(2,1)}...) custom-call(bf16[1024,512]{1,0:T(8,128)(2,1)} %copy-done.2, bf16[512,2048]{1,0:T(8,128)(2,1)} %all-gather.5.cloned.1.call-done.w_out, ...), custom_call_target="tpu_custom_call" | custom-call | flops 1000 | bytes 1000 | tf_op jit(solution)/shard_map/pallas_call | solution.py:525
  304.1 0.5 reduce-scatter.5.cloned.1.call-update
  304.8 5.0 fusion.25
  309.8 1.5 copy-done.6
  311.3 2.4 multiply_reduce_fusion
  313.8 5.5 fusion.21
  319.4 8.2 %convert_reduce_fusion.4 = (f32[2048]{0:T(1024)S(1)}, bf16[1024,2048]{1,0:T(8,128)(2,1)S(1)}, f32[1024,2048]{1,0:T(8,128)}, f32[2048]{0:T(1024)S(1)}) fusion(f32[1024]{0:T(1024)S(1)} %get-tuple-element.68, f32[1024]{0:T(1024)S(1)} %broadcast_multiply_fusion.4, f32[2048]{0:T(1024)S(1)} %copy-done.13, bf16[1024,2048]{1,0:T(8,128)(2,1)S(1)} %copy-done.6, ...), kind=kLoop, calls=%fused_computation.35 | loop fusion | flops 37744640 | bytes 29409280 | tf_op jit(solution)/shard_map/reduce_sum | solution.py:769
  327.6 3.3 convolution_convert_fusion.d_context
  330.9 116.6 %shard_map.256 = (bf16[1024,2048]{1,0:T(8,128)(2,1)}, bf16[3,1024,512]{2,1,0:T(8,128)(2,1)}, f32[2,512]{1,0:T(2,128)}, bf16[3,2048,512]{2,1,0:T(8,128)(2,1)}, bf16[512,2048]{1,0:T(8,128)(2,1)}) custom-call(s32[1]{0:T(128)S(6)} %copy.29.prefix_ref, bf16[1024,2048]{1,0:T(8,128)(2,1)} %get-tuple-element.30.p_ref, bf16[3,1024,512]{2,1,0:T(8,128)(2,1)} %copy-done.1, ...), custom_call_target="tpu_custom_call" | custom-call | flops 1000 | bytes 1000 | tf_op jit(solution)/shard_map/pallas_call | solution.py:686
  447.5 2.7 convert_element_type.83
  450.5 2.8 convert_element_type.82
  453.9 9.8 %bitcast_convert_fusion.p_ref = bf16[1024,2048]{1,0:T(8,128)(2,1)S(1)} fusion(bf16[3,1024,512]{2,1,0:T(8,128)(2,1)} %get-tuple-element.33, bf16[3,2048,512]{2,1,0:T(8,128)(2,1)} %all-gather.3.cloned.1.call-done), kind=kOutput, calls=%fused_computation.34 | convolution fusion | flops 6444548096 | bytes 13631488 | tf_op jit(solution)/shard_map/ctn,cdn->td/dot_general | solution.py:777
  463.7 109.6 %shard_map.257 = bf16[1024,2048]{1,0:T(8,128)(2,1)S(1)} custom-call(bf16[1024,2048]{1,0:T(8,128)(2,1)S(1)} %bitcast_convert_fusion.p_ref), custom_call_target="tpu_custom_call" | custom-call | flops 1000 | bytes 1000 | tf_op jit(solution)/shard_map/pallas_call | solution.py:298
  573.3 2.0 copy-done
  575.3 4.2 fusion.22
  579.6 23.4 %all-reduce = (f32[2048]{0:T(1024)}, f32[2048]{0:T(1024)}, f32[2,512]{1,0:T(2,128)}, f32[2048]{0:T(1024)}, f32[2048]{0:T(1024)}, /*index=5*/f32[2048]{0:T(1024)}, f32[2048]{0:T(1024)}, f32[2048]{0:T(1024)}) all-reduce(f32[2048]{0:T(1024)S(1)} %get-tuple-element.46, ...), channel_id=1, replica_groups=mesh['dp'=2,'row'=4,'col'=4] {'dp','col'}, use_global_device_ids=true, to_apply=%region_9.0 | all-reduce | flops 15360 | bytes 122880 | tf_op jit(solution)/shard_map/psum | solution.py:791
  603.0 13.6 %fusion.14 = (f32[1024,2048]{1,0:T(8,128)}, bf16[1024,2048]{1,0:T(8,128)(2,1)}) fusion(f32[1024,2048]{1,0:T(8,128)} %get-tuple-element.62, bf16[1024,2048]{1,0:T(8,128)(2,1)} %src_hbm.1, bf16[1024,2048]{1,0:T(8,128)(2,1)} %copy-done, f32[1024]{0:T(1024)S(1)} %broadcast_multiply_fusion, f32[1024]{0:T(1024)S(1)} %broadcast_multiply_fusion.1, ...), kind=kLoop, calls=%fused_computation.25 | loop fusion | flops 35651584 | bytes 37789696 | tf_op jit(solution)/shard_map/add | solution.py:790
  616.6 1.8 convert_element_type.85
  618.4 2.5 convert_element_type.84
  (63 shorter events, 1.4 us)
Async XLA Ops:
  7.2 8.3 %copy-start.10 = (f32[256,2048]{1,0:T(8,128)S(1)}, f32[256,2048]{1,0:T(8,128)}, u32[]{:S(2)}) copy-start(f32[256,2048]{1,0:T(8,128)} %param.25) | copy-start | bytes 6291460
  7.2 10.8 %copy-start.19 = (f32[2,512]{1,0:T(2,128)S(1)}, f32[2,512]{1,0:T(2,128)}, u32[]{:S(2)}) copy-start(f32[2,512]{1,0:T(2,128)} %param.20) | copy-start | bytes 12292
  7.2 10.8 %copy-start.14 = (f32[2048]{0:T(1024)S(1)}, f32[2048]{0:T(1024)}, u32[]{:S(2)}) copy-start(f32[2048]{0:T(1024)} %param.17) | copy-start | bytes 24580
  7.2 10.8 %copy-start.16 = (f32[2048]{0:T(1024)S(1)}, f32[2048]{0:T(1024)}, u32[]{:S(2)}) copy-start(f32[2048]{0:T(1024)} %param.18) | copy-start | bytes 24580
  7.2 51.6 %all-gather.3.cloned.1.call-start = ((), (), s32[]{:S(2)}) async-start(), calls=%async_computation.4 | async-start | bytes 7077888 | tf_op jit(solution)/shard_map/all_gather | solution.py:740
  9.8 79.7 %all-gather.5.cloned.1.call-start = ((), (), s32[]{:S(2)}) async-start(), calls=%async_computation.5 | async-start | bytes 2359296 | tf_op jit(solution)/shard_map/all_gather | solution.py:741
  11.7 435.9 %reduce-scatter.7.cloned.1.call-start = ((), (), s32[]{:S(2)}) async-start(), calls=%async_computation.7 | async-start | bytes 9437184 | tf_op jit(solution)/shard_map/reduce_scatter | solution.py:712
  11.7 5.0 copy-start.3
  21.2 47.7 %copy-start.11 = (f32[2048,256]{1,0:T(8,128)S(1)}, f32[2048,256]{1,0:T(8,128)}, u32[]{:S(2)}) copy-start(f32[2048,256]{1,0:T(8,128)} %param.27) | copy-start | bytes 6291460
  68.9 2.0 copy-start.1
  81.8 1.0 copy-start.2
  304.0 0.7 copy-start.13
  304.1 146.4 %reduce-scatter.5.cloned.1.call-start = ((), (), s32[]{:S(2)}) async-start(), calls=%async_computation.6 | async-start | bytes 9437184 | tf_op jit(solution)/shard_map/reduce_scatter | solution.py:712
  304.7 311.9 %reduce-scatter.11.cloned.1.call-start = ((), (), s32[]{:S(2)}) async-start(), calls=%async_computation.9 | async-start | bytes 2359296 | tf_op jit(solution)/shard_map/reduce_scatter | solution.py:712
  304.7 5.1 copy-start.4
  304.7 6.6 %copy-start.6 = (bf16[1024,2048]{1,0:T(8,128)(2,1)S(1)}, bf16[1024,2048]{1,0:T(8,128)(2,1)}, u32[]{:S(2)}) copy-start(bf16[1024,2048]{1,0:T(8,128)(2,1)} %get-tuple-element.29) | copy-start | bytes 12582916
  304.8 9.1 %copy-start.9 = (bf16[1024,2048]{1,0:T(8,128)(2,1)S(1)}, bf16[1024,2048]{1,0:T(8,128)(2,1)}, u32[]{:S(2)}) copy-start(bf16[1024,2048]{1,0:T(8,128)(2,1)} %get-tuple-element.31) | copy-start | bytes 12582916
  304.8 9.1 %copy-start.15 = (f32[2048]{0:T(1024)S(1)}, f32[2048]{0:T(1024)}, u32[]{:S(2)}) copy-start(f32[2048]{0:T(1024)} %param.23) | copy-start | bytes 24580
  313.8 5.6 copy-start.8
  319.4 8.2 %copy-start.12 = (bf16[512,2048]{1,0:T(8,128)(2,1)S(1)}, bf16[512,2048]{1,0:T(8,128)(2,1)}, u32[]{:S(2)}) copy-start(bf16[512,2048]{1,0:T(8,128)(2,1)} %all-gather.5.cloned.1.call-done.w_out) | copy-start | bytes 6291460
  327.6 3.3 copy-start.7
  453.3 165.1 %reduce-scatter.9.cloned.1.call-start = ((), (), s32[]{:S(2)}) async-start(), calls=%async_computation.8 | async-start | bytes 7077888 | tf_op jit(solution)/shard_map/reduce_scatter | solution.py:712
  463.7 111.7 %copy-start.5 = (bf16[1024,2048]{1,0:T(8,128)(2,1)S(1)}, bf16[1024,2048]{1,0:T(8,128)(2,1)}, u32[]{:S(2)}) copy-start(bf16[1024,2048]{1,0:T(8,128)(2,1)} %src_hbm.1) | copy-start | bytes 12582916
  463.7 115.9 %copy-start.18 = (f32[1,2048]{1,0:T(1,128)S(1)}, f32[1,2048]{1,0:T(1,128)}, u32[]{:S(2)}) copy-start(f32[1,2048]{1,0:T(1,128)} %get-tuple-element.42) | copy-start | bytes 24580
  463.7 115.9 %copy-start.20 = (f32[2,512]{1,0:T(2,128)S(1)}, f32[2,512]{1,0:T(2,128)}, u32[]{:S(2)}) copy-start(f32[2,512]{1,0:T(2,128)} %get-tuple-element.39) | copy-start | bytes 12292
  463.7 139.3 %copy-start.17 = (f32[2048]{0:T(1024)S(1)}, f32[2048]{0:T(1024)}, u32[]{:S(2)}) copy-start(f32[2048]{0:T(1024)} %param.28) | copy-start | bytes 24580
  573.3 2.0 copy-start
Sparse Core Ops, SparseCore 0:
  10.5 48.2 all-gather.2
  61.2 28.1 all-gather.4
  304.2 71.1 reduce-scatter.6
  379.1 71.2 reduce-scatter.4
  453.6 41.2 reduce-scatter.10
  498.5 61.7 reduce-scatter.8

commit v5 on v4

--- a/solution.py
+++ b/solution.py
@@ -148,8 +148,8 @@
 
 
 def line_sum(n, p_ref, o_ref, held, rs_s, rs_r, ag_s, ag_r, loc):
-    half = p_ref.shape[0] // 2
-    chunks = half // CHUNK
+    half = o_ref.shape[0] // 2
+    chunks = held.shape[0] // 2 // CHUNK
     r = lax.axis_index("row")
     last = n - 1
     place = (r, last - r)
@@ -159,10 +159,14 @@
     def rows(d, c):
         return pl.ds(pl.multiple_of((half if d == 0 else 0) + c * CHUNK, CHUNK), CHUNK)
 
+    def slot(d, c):
+        return pl.ds(pl.multiple_of((1 - d) * chunks * CHUNK + c * CHUNK, CHUNK), CHUNK)
+
+
     def onward(d, c, src):
         return pltpu.make_async_remote_copy(
-            src_ref=src.at[rows(d, c)],
-            dst_ref=held.at[rows(d, c)],
+            src_ref=src.at[rows(d, c) if src is p_ref else slot(d, c)],
+            dst_ref=held.at[slot(d, c)],
             send_sem=rs_s.at[d, c],
             recv_sem=rs_r.at[d, c],
             device_id={"row": after[d]},
@@ -171,7 +175,7 @@
 
     def back(d, c, src):
         return pltpu.make_async_remote_copy(
-            src_ref=src.at[rows(d, c)],
+            src_ref=src.at[slot(d, c) if src is held else rows(d, c)],
             dst_ref=o_ref.at[rows(d, c)],
             send_sem=ag_s.at[d, c],
             recv_sem=ag_r.at[d, c],
@@ -180,7 +184,7 @@
         )
 
     def keep(d, c):
-        return pltpu.make_async_copy(held.at[rows(d, c)], o_ref.at[rows(d, c)], loc.at[c])
+        return pltpu.make_async_copy(held.at[slot(d, c)], o_ref.at[rows(d, c)], loc.at[c])
 
     def step(t):
         for d in (0, 1):
@@ -194,9 +198,9 @@
             @pl.when((place[d] > 0) & (c >= 0) & (c < chunks))
             def _():
                 onward(d, c, p_ref).wait_recv()
-                here = rows(d, c)
+                here = slot(d, c)
                 held[here] = (
-                    held[here].astype(jnp.float32) + p_ref[here].astype(jnp.float32)
+                    held[here].astype(jnp.float32) + p_ref[rows(d, c)].astype(jnp.float32)
                 ).astype(jnp.bfloat16)
 
                 @pl.when(place[d] < last)
@@ -285,25 +289,6 @@
     return pltpu.CompilerParams(
         collective_id=collective_id, has_side_effects=True, vmem_limit_bytes=mib * 2**20
     )
-
-
-def sum_row_kernel(n, p_ref, o_ref, *line):
-    greet_row(n)
-    step, drain = line_sum(n, p_ref, o_ref, *line)[:2]
-    loop(0, line_steps(n, p_ref.shape[0]), step)
-    drain()
-
-
-def sum_row(partial_low):
-    return pl.pallas_call(
-        partial(sum_row_kernel, lax.axis_size("row")),
-        out_shape=low_shape(*partial_low.shape),
-        in_specs=[IN_VMEM],
-        out_specs=IN_HBM,
-        scratch_shapes=line_scratch(partial_low.shape),
-        compiler_params=kernel_params(0, 16),
-        cost_estimate=COST,
-    )(partial_low)
 
 
 TILE = 512
@@ -624,88 +609,542 @@
             total[:width] += term
 
 
-def attend_sum_kernel(
-    n, prefix_ref, p_ref, projected, d_context, n1_hbm, ctx_hbm, branch_hbm,
-    o_ref, d_proj, d_bias, d_wqkv, d_wout,
-    n1, ctx, branch, d_key, d_value, load_sem, *line,
+def plane_scatter(pieces, sems):
+    ids, mine, theirs = plane_partners()
+    near_send, near_recv, far_send, far_recv, last_send, last_recv, load_sem = sems
+    count = len(pieces)
+
+    def remote(src, dst, send, recv, to):
+        return pltpu.make_async_remote_copy(
+            src_ref=src,
+            dst_ref=dst,
+            send_sem=send,
+            recv_sem=recv,
+            device_id=ids[to],
+            device_id_type=MESH_IDS,
+        )
+
+    def near(i, k):
+        block, to, _, _, _ = pieces[k]
+        place = theirs[KINDS[i]]
+        return remote(block(place), to(i), near_send.at[i, k], near_recv.at[i, k], "near")
+
+    def load(i, k):
+        block, _, own, _, _ = pieces[k]
+        return pltpu.make_async_copy(block(mine[KINDS[i]]), own(i), load_sem.at[i, k])
+
+    def far(k):
+        _, _, own, to, _ = pieces[k]
+        return remote(own(3), to(), far_send.at[k], far_recv.at[k], "x" if k % 2 == 0 else "y")
+
+    def last(i, k):
+        _, _, own, _, to = pieces[k]
+        return remote(
+            own(i), to(i - 1), last_send.at[i - 1, k], last_recv.at[i - 1, k], KINDS[i]
+        )
+
+    def add(target, term):
+        flat = target.shape[0]
+
+        def some(r):
+            here = pl.ds(pl.multiple_of(r * 128, 128), 128)
+            target[here] = (
+                target[here].astype(jnp.float32) + term[here].astype(jnp.float32)
+            ).astype(jnp.bfloat16)
+
+        loop(0, flat // 128, some)
+
+    def start():
+        for i in (3, 1, 2, 0):
+            for k in range(count):
+                near(i, k).start()
+                load(i, k).start()
+
+    def pair():
+        for i in (3, 1, 2, 0):
+            for k in range(count):
+                near(i, k).wait_recv()
+                load(i, k).wait()
+                add(pieces[k][2](i), pieces[k][1](i))
+                if i == 3:
+                    far(k).start()
+                elif i == 1 + k % 2:
+                    last(i, k).start()
+
+    def cross():
+        for k in range(count):
+            far(k).wait_recv()
+            i = 2 - k % 2
+            add(pieces[k][2](i), pieces[k][3]())
+            last(i, k).start()
+
+    def collect(k):
+        for i in (1, 2):
+            last(i, k).wait_recv()
+        return pieces[k][2](0), pieces[k][4](0), pieces[k][4](1)
+
+    def finish():
+        for k in range(count):
+            for i in range(4):
+                near(i, k).wait_send()
+            far(k).wait_send()
+            for i in (1, 2):
+                last(i, k).wait_send()
+
+    return start, pair, cross, collect, finish
+
+
+def sums_out(kind, vectors, slots, send_sem, recv_sem):
+    ids = plane_partners()[0]
+
+    def copy(i):
+        return pltpu.make_async_remote_copy(
+            src_ref=vectors,
+            dst_ref=slots.at[i],
+            send_sem=send_sem.at[kind, i],
+            recv_sem=recv_sem.at[kind, i],
+            device_id=ids[("near", "x", "y")[i]],
+            device_id_type=MESH_IDS,
+        )
+
+    def begin(i):
+        copy(i).start()
+
+    def end(i):
+        copy(i).wait()
+        vectors[...] += slots[i]
+
+    return begin, end
+
+
+SLICE = 64
+RING = 4
+
+
+def backward_kernel(
+    n, spread, prefix_ref, projected, d_bin, b_out, gain1, gain2,
+    mlp_hbm, n1_hbm, ctx_hbm, w_qkv_hbm, w_out_hbm, src_hbm, attn_hbm, g_hbm, dn2_hbm,
+    mlp_sum, d_inputs, d_hidden, d_wqkv, d_wout, sum_wqkv, sum_wout, early, late,
+    p, d_context, n1, ctx, branch, d_key, d_value, d_proj, w_stage, total, weights, ring,
+    p_sem, slice_sem, load_sem, store_sem, ring_in, ring_out, *more,
 ):
+    lines, more = more[:12], more[12:]
+    tokens, depth = p.shape
+    width = projected.shape[2]
+    half = tokens // 2
+    chunks = half // CHUNK
+    blocks = tokens // BLOCK
+    part = BLOCK // 2
+    per_block = part // CHUNK
+    travel = LAG * 2 * (n - 1)
+    prefix = prefix_ref[0]
+
+    def sides(j, size):
+        return (
+            pl.ds(pl.multiple_of(j * size, size), size),
+            pl.ds(pl.multiple_of(half + j * size, size), size),
+        )
+
+    p_loads = [
+        [
+            pltpu.make_async_copy(mlp_hbm.at[rows], p.at[rows], p_sem.at[side, j])
+            for side, rows in enumerate((pl.ds(j * part, part), pl.ds(half + j * part, part)))
+        ]
+        for j in range(blocks)
+    ]
+    for loads in p_loads:
+        for load in loads:
+            load.start()
+    w_out_load = pltpu.make_async_copy(w_out_hbm, total.at[pl.ds(0, width)], load_sem.at[0])
+    w_out_load.start()
     loads = [
-        pltpu.make_async_copy(src, dst, load_sem.at[i])
-        for i, (src, dst) in enumerate(((n1_hbm, n1), (ctx_hbm, ctx), (branch_hbm, branch)))
+        pltpu.make_async_copy(src, dst, load_sem.at[1 + i])
+        for i, (src, dst) in enumerate(
+            ((n1_hbm, n1), (ctx_hbm, ctx), (w_qkv_hbm, weights), (src_hbm, n1))
+        )
     ]
-    for load in loads:
+    early[...] = jnp.zeros_like(early)
+    late[...] = jnp.zeros_like(late)
+    early[4:5] = d_bin[...]
+    others = []
+    if spread:
+        slots_e, slots_l, small_s, small_r = more[:4]
+        qkv_near, qkv_own, qkv_far, qkv_last, out_near, out_own, out_far, out_last = more[4:12]
+        qkv_sum, out_sum, sum_sem = more[12:15]
+        others = list(plane_partners()[0].values())
+        early_begin, early_end = sums_out(0, early, slots_e, small_s, small_r)
+        late_begin, late_end = sums_out(1, late, slots_l, small_s, small_r)
+        places = 8
+        deep, wide = depth // places, depth // places
+        size = deep // 2
+        tall = width // 2
+
+        def qkv_piece(c, k):
+            def block(place):
+                there = pl.ds(pl.multiple_of(place * deep + k * size, size), size)
+                return d_wqkv.at[c, there]
+
+            some = pl.ds(k * size, size)
+            return (
+                block,
+                lambda i: qkv_near.at[i, c, some],
+                lambda i: qkv_own.at[i, c, some],
+                lambda: qkv_far.at[c, some],
+                lambda i: qkv_last.at[i, c, some],
+            )
+
+        def out_piece(k):
+            some = pl.ds(k * tall, tall)
+
+            def block(place):
+                cols = pl.ds(pl.multiple_of(place * wide, wide), wide)
+                return d_wout.at[some, cols]
+
+            return (
+                block,
+                lambda i: out_near.at[i, some],
+                lambda i: out_own.at[i, some],
+                lambda: out_far.at[some],
+                lambda i: out_last.at[i, some],
+            )
+
+        pieces = [qkv_piece(c, k) for c in range(3) for k in range(2)]
+        pieces += [out_piece(k) for k in range(2)]
+        start_scatter, pair, cross, collect, finish_scatter = plane_scatter(pieces, more[15:])
+        stores = [
+            pltpu.make_async_copy(qkv_sum, sum_wqkv, sum_sem.at[0]),
+            pltpu.make_async_copy(out_sum, sum_wout, sum_sem.at[1]),
+        ]
+
+        def total_of(k):
+            own, one, two = collect(k)
+            if k < 6:
+                target = qkv_sum.at[k // 2, pl.ds((k % 2) * size, size)]
+            else:
+                target = out_sum.at[pl.ds((k % 2) * tall, tall)]
+
+            def some(r):
+                here = pl.ds(pl.multiple_of(r * 128, 128), 128)
+                target[here] = (
+                    own[here].astype(jnp.float32)
+                    + one[here].astype(jnp.float32)
+                    + two[here].astype(jnp.float32)
+                )
+
+            loop(0, target.shape[0] // 128, some)
+
+    greet_row(n, others)
+    step1, _, settle1, finish1 = line_sum(n, p, mlp_sum, *lines[:6])
+    step2, _, settle2, finish2 = line_sum(n, p, total, *lines[6:])
+
+    def both_steps(t):
+        step1(t)
+        step2(t - chunks)
+
+    slices = tokens // SLICE
+
+    def slice_rows(k):
+        return pl.ds(pl.multiple_of(k * SLICE, SLICE), SLICE)
+
+    def slice_slot(k, i):
+        return pl.ds(pl.multiple_of(half + (lax.rem(k, 2) * 4 + i) * SLICE, SLICE), SLICE)
+
+    def slice_loads(k):
+        return [
+            pltpu.make_async_copy(
+                src.at[slice_rows(k)], total.at[slice_slot(k, i)], slice_sem.at[lax.rem(k, 2), i]
+            )
+            for i, src in enumerate((dn2_hbm, attn_hbm, src_hbm, g_hbm))
+        ]
+
+    def hidden_store(k):
+        return pltpu.make_async_copy(
+            ring.at[lax.rem(k, RING)], d_hidden.at[slice_rows(k)], ring_out.at[lax.rem(k, RING), 0]
+        )
+
+    def norm_slice(k):
+        @pl.when(k + 1 < slices)
+        def _():
+            for load in slice_loads(k + 1):
+                load.start()
+
+        for load in slice_loads(k):
+            load.wait()
+
+        @pl.when(k >= RING)
+        def _():
+            hidden_store(k - RING).wait()
+
+        dn, attn, source, g = (total[slice_slot(k, i)].astype(jnp.float32) for i in range(4))
+        _, scaled, inverse = norm_forward(source + attn + b_out[...], 1.0, 0.0)
+        grad = g + norm_backward(dn, scaled, inverse, gain2[...])
+        low = grad.astype(jnp.bfloat16)
+        branch[slice_rows(k)] = low
+        for i, term in enumerate((low.astype(jnp.float32), dn * scaled, dn, g)):
+            early[i : i + 1] += jnp.sum(term, axis=0, keepdims=True)
+        ring[lax.rem(k, RING)] = grad
+        hidden_store(k).start()
+
+    for load in slice_loads(0):
         load.start()
-    greet_row(n)
-    step, drain = line_sum(n, p_ref, o_ref, *line)[:2]
-    steps = line_steps(n, p_ref.shape[0])
-    prefix = prefix_ref[0]
+    norm_ticks = 4
+    for load in p_loads[0]:
+        load.wait()
+
+    def norm_tick(t):
+        step1(t)
+        loop(t * (slices // norm_ticks), (t + 1) * (slices // norm_ticks), norm_slice)
+
+    loop(0, norm_ticks, norm_tick)
+    for k in range(slices - RING, slices):
+        hidden_store(k).wait()
+    for some in p_loads[1:]:
+        for load in some:
+            load.wait()
+    for load in loads[:3]:
+        load.start()
+    w_out_load.wait()
+
+    def context_rows(i):
+        rows = pl.ds(pl.multiple_of(i * BLOCK, BLOCK), BLOCK)
+        d_context[rows] = dot(branch[rows], total[:width], 1, 1).astype(jnp.bfloat16)
+
+    loop(0, tokens // BLOCK, context_rows)
+
     q, k, v = (projected.at[c] for c in range(3))
-    blocks = q.shape[0] // QUERY_ROWS
-    heads = q.shape[1] // HEAD_DIM
+    q_blocks = tokens // QUERY_ROWS
+    heads = width // HEAD_DIM
+    head_ticks = q_blocks // 2
 
     def head(h):
         cols = pl.ds(pl.multiple_of(h * HEAD_DIM, HEAD_DIM), HEAD_DIM)
         k_t = k[:, cols].T
-        for j in range(blocks):
-            step(h * blocks + j)
+        for j in range(q_blocks):
+            if j % 2 == 0:
+                step1(norm_ticks + h * head_ticks + j // 2)
             attend_piece(
-                blocks - 1 - j, prefix, cols, q, k, v, k_t, d_context, d_proj, d_key, d_value,
+                q_blocks - 1 - j, prefix, cols, q, k, v, k_t, d_context, d_proj, d_key, d_value,
                 j == 0,
             )
         d_proj[1, :, cols] = (d_key[...] * HEAD_DIM ** (-0.5)).astype(jnp.bfloat16)
         d_proj[2, :, cols] = d_value[...].astype(jnp.bfloat16)
-        for b, c in ((0, 0), (1, 2)):
-            d_bias[b : b + 1, cols] = jnp.sum(
-                d_proj[c, :, cols].astype(jnp.float32), axis=0, keepdims=True
+
+    loop(0, heads, head)
+    for b, c in ((0, 0), (1, 2)):
+        early[5:6, b * width : (b + 1) * width] = jnp.sum(
+            d_proj[c].astype(jnp.float32), axis=0, keepdims=True
+        )
+    for load in loads[:3]:
+        load.wait()
+    tick = norm_ticks + heads * head_ticks
+    tiles = depth // TILE
+
+    def tile_store(c, m):
+        some = pl.ds(m * TILE, TILE)
+        out = d_wqkv.at[c, some] if c < 3 else d_wout.at[:, some]
+        return pltpu.make_async_copy(w_stage.at[m % 2], out, store_sem.at[m % 2])
+
+    for c in range(4):
+        step1(tick + c)
+        for m in range(tiles):
+            some = slice(m * TILE, (m + 1) * TILE)
+            if c or m > 1:
+                before = (c, m - 2) if m > 1 else (c - 1, tiles + m - 2)
+                tile_store(*before).wait()
+            if c < 3:
+                term = dot(n1[:, some], d_proj[c], 0, 0)
+            else:
+                term = dot(ctx[...], branch[:, some], 0, 0)
+            w_stage[m % 2] = term.astype(jnp.bfloat16)
+            tile_store(c, m).start()
+    for m in (tiles - 2, tiles - 1):
+        tile_store(3, m).wait()
+    loads[3].start()
+    if tick + 4 < chunks:
+        loop(tick + 4, chunks, step1)
+    if spread:
+        start_scatter()
+
+    def gradient(j):
+        loop(j * per_block, (j + 1) * per_block, settle1)
+        low_rows, high_rows = sides(j, part)
+        rows = [
+            jnp.concatenate([d_proj[c, low_rows], d_proj[c, high_rows]], axis=0) for c in range(3)
+        ]
+        for i in range(0, depth, TILE):
+            cols = slice(i, i + TILE)
+            term = dot(rows[0], weights[0, cols], 1, 1)
+            for c in (1, 2):
+                term += dot(rows[c], weights[c, cols], 1, 1)
+            term = term.astype(jnp.bfloat16)
+            p[low_rows, cols] = term[:part]
+            p[high_rows, cols] = term[part:]
+
+    def hidden_loads(c):
+        return [
+            pltpu.make_async_copy(
+                d_hidden.at[rows],
+                ring.at[lax.rem(c, RING), pl.ds(side * CHUNK, CHUNK)],
+                ring_in.at[lax.rem(c, RING), side],
             )
-
-    loop(0, heads, head)
-    for load in loads:
-        load.wait()
-    begin = heads * blocks
-    tiles = n1.shape[1] // TILE
-
-    for c in range(3):
-
-        def body(t):
-            step(t)
-            m = pl.ds(pl.multiple_of((t - begin - c * tiles) * TILE, TILE), TILE)
-            d_wqkv[c, m] = dot(n1[:, m], d_proj[c], 0, 0).astype(jnp.bfloat16)
-            if c == 0:
-                d_wout[:, m] = dot(ctx[...], branch[:, m], 0, 0).astype(jnp.bfloat16)
-
-        loop(begin + c * tiles, begin + (c + 1) * tiles, body)
-    loop(begin + 3 * tiles, steps, step)
-    drain()
-
-
-def attend_sum(prefix_len, partial_low, projected, d_context, normed1, context, d_branch):
-    _, tokens, width = projected.shape
-    depth = normed1.shape[1]
+            for side, rows in enumerate(sides(c, CHUNK))
+        ]
+
+    def input_stores(c):
+        return [
+            pltpu.make_async_copy(
+                ring.at[lax.rem(c, RING), pl.ds(side * CHUNK, CHUNK)],
+                d_inputs.at[rows],
+                ring_out.at[lax.rem(c, RING), side],
+            )
+            for side, rows in enumerate(sides(c, CHUNK))
+        ]
+
+    def norm_rows(c):
+        settle2(c)
+        for load in hidden_loads(c):
+            load.wait()
+        for side, rows in enumerate(sides(c, CHUNK)):
+            _, scaled, inverse = norm_forward(n1[rows].astype(jnp.float32), 1.0, 0.0)
+            grad = total[rows].astype(jnp.float32)
+            late[0:1] += jnp.sum(grad * scaled, axis=0, keepdims=True)
+            late[1:2] += jnp.sum(grad, axis=0, keepdims=True)
+            here = pl.ds(side * CHUNK, CHUNK)
+            ring[lax.rem(c, RING), here] += norm_backward(grad, scaled, inverse, gain1[...])
+        for store in input_stores(c):
+            store.start()
+
+        @pl.when(c >= 2)
+        def _():
+            for store in input_stores(c - 2):
+                store.wait()
+
+        @pl.when(c + 2 < chunks)
+        def _():
+            for load in hidden_loads(c + 2):
+                load.start()
+
+    arrival = chunks + travel
+
+    def tick_of(t):
+        both_steps(t)
+
+        @pl.when(t >= arrival)
+        def _():
+            norm_rows(t - arrival)
+
+    for j in range(blocks):
+        gradient(j)
+        if j == blocks - 1:
+            for c in range(2):
+                for load in hidden_loads(c):
+                    load.start()
+            loads[3].wait()
+        begin = chunks + j * per_block
+        loop(begin, begin + per_block, tick_of if j == blocks - 1 else both_steps)
+        if spread and j == 0:
+            pair()
+        if spread and j == 2:
+            cross()
+            for i in range(3):
+                early_begin(i)
+                early_end(i)
+    begin = chunks + blocks * per_block
+    middle = begin + per_block
+    loop(begin, middle, tick_of)
+    if spread:
+        for k in range(len(pieces)):
+            total_of(k)
+        for store in stores:
+            store.start()
+    loop(middle, arrival + chunks, tick_of)
+    if spread:
+        for i in range(3):
+            late_begin(i)
+            late_end(i)
+    for c in (chunks - 2, chunks - 1):
+        for store in input_stores(c):
+            store.wait()
+    if spread:
+        finish_scatter()
+        for store in stores:
+            store.wait()
+    finish1()
+    finish2()
+
+
+def backward(
+    prefix_len, projected, d_bin, b_out, gain1, gain2, mlp_partial, normed1, context, w_qkv, w_out,
+    inputs, attn_sum, d_output, summed2,
+):
+    tokens, depth = inputs.shape
+    width = w_out.shape[0]
+    spread = (lax.axis_size("dp"), lax.axis_size("col")) == (2, 4)
     dma = pltpu.SemaphoreType.DMA
-    return pl.pallas_call(
-        partial(attend_sum_kernel, lax.axis_size("row")),
+    buffer = lambda *shape: pltpu.VMEM(shape, jnp.bfloat16)
+    wide_buffer = lambda *shape: pltpu.VMEM(shape, jnp.float32)
+    single = lambda *shape: jax.ShapeDtypeStruct(shape, jnp.float32)
+    sums, scatter_scratch = [single(8, 128), single(8, 128)], []
+    if spread:
+        block, side = (3, depth // 8, width), (width, depth // 8)
+        sums = [single(*block), single(*side)]
+        scatter_scratch = [wide_buffer(3, 8, depth), wide_buffer(3, 8, depth)]
+        scatter_scratch += [dma((2, 3)), dma((2, 3))]
+        for shape in (block, side):
+            scatter_scratch += [
+                buffer(4, *shape), buffer(4, *shape), buffer(*shape), buffer(2, *shape)
+            ]
+        scatter_scratch += [wide_buffer(*block), wide_buffer(*side)]
+        scatter_scratch += [dma((2,)), dma((4, 8)), dma((4, 8)), dma((8,)), dma((8,))]
+        scatter_scratch += [dma((2, 8)), dma((2, 8)), dma((4, 8))]
+    out = pl.pallas_call(
+        partial(backward_kernel, lax.axis_size("row"), spread),
         out_shape=[
-            low_shape(*partial_low.shape),
-            low_shape(3, tokens, width),
-            jax.ShapeDtypeStruct((2, width), jnp.float32),
+            low_shape(tokens, depth),
+            single(tokens, depth),
+            single(tokens, depth),
             low_shape(3, depth, width),
             low_shape(width, depth),
+            *sums,
+            single(8, depth),
+            single(8, depth),
         ],
-        in_specs=[pl.BlockSpec(memory_space=pltpu.SMEM)] + [IN_VMEM] * 3 + [IN_HBM] * 3,
-        out_specs=[IN_HBM] + [IN_VMEM] * 4,
+        in_specs=[pl.BlockSpec(memory_space=pltpu.SMEM)] + [IN_VMEM] * 5 + [IN_HBM] * 9,
+        out_specs=[IN_HBM] * 7 + [IN_VMEM] * 2,
         scratch_shapes=[
-            pltpu.VMEM((tokens, depth), jnp.bfloat16),
-            pltpu.VMEM((tokens, width), jnp.bfloat16),
-            pltpu.VMEM((tokens, depth), jnp.bfloat16),
-            pltpu.VMEM((tokens, HEAD_DIM), jnp.float32),
-            pltpu.VMEM((tokens, HEAD_DIM), jnp.float32),
-            dma((3,)),
+            buffer(tokens, depth),
+            buffer(tokens, width),
+            buffer(tokens, depth),
+            buffer(tokens, width),
+            buffer(tokens, depth),
+            wide_buffer(tokens, HEAD_DIM),
+            wide_buffer(tokens, HEAD_DIM),
+            buffer(3, tokens, width),
+            buffer(2, TILE, TILE),
+            buffer(tokens, depth),
+            buffer(*w_qkv.shape),
+            wide_buffer(RING, SLICE, depth),
+            dma((2, tokens // BLOCK)),
+            dma((2, 4)),
+            dma((5,)),
+            dma((2,)),
+            dma((RING, 2)),
+            dma((RING, 2)),
         ]
-        + line_scratch(partial_low.shape),
-        compiler_params=kernel_params(2, 56),
+        + line_scratch((tokens, depth))
+        + line_scratch((tokens, depth))
+        + scatter_scratch,
+        compiler_params=kernel_params(2, 63),
         cost_estimate=COST,
-    )(prefix_len, partial_low, projected, d_context, normed1, context, d_branch)
+    )(
+        prefix_len, projected, d_bin, b_out[None], gain1[None], gain2[None], mlp_partial, normed1,
+        context, w_qkv, w_out, inputs, attn_sum, d_output, summed2,
+    )
+    mlp_sum, d_inputs, _, d_wqkv, d_wout, sum_wqkv, sum_wout, early, late = out
+    if not spread:
+        early, late = lax.psum((early, late), ("dp", "col"))
+        sum_wqkv, sum_wout = scatter_low(d_wqkv, 1), scatter_low(d_wout, 1)
+    return mlp_sum, d_inputs, sum_wqkv, sum_wout, early, late
 
 
 def scatter_low(grad, dim):
@@ -746,7 +1185,7 @@
         full_in = lax.all_gather(full_in, ("dp", "col"), axis=0, tiled=True)
         full_down = lax.all_gather(full_down, ("dp", "col"), axis=1, tiled=True)
     source = inputs.astype(jnp.float32)
-    normed1, scaled1, inverse1 = norm_forward(source, norm1_gain, norm1_shift)
+    normed1, _, _ = norm_forward(source, norm1_gain, norm1_shift)
     normed1_low = normed1.astype(jnp.bfloat16)
     projected = jnp.einsum("td,cdn->ctn", normed1_low, full_qkv, preferred_element_type=jnp.float32)
     bias_rows = jnp.stack([b_qv[0], jnp.zeros_like(b_qv[0]), b_qv[1]])
@@ -756,66 +1195,30 @@
         context_low, full_out, b_out, norm2_gain, norm2_shift, b_in,
         inputs, full_in, full_down, d_output,
     )
-    grad_bin = grad_bin[0]
-    hidden = source + attn_sum.astype(jnp.float32) + b_out
-    _, scaled2, inverse2 = norm_forward(hidden, norm2_gain, norm2_shift)
-    grad_top = d_output.astype(jnp.float32)
-    grad_bdown = jnp.sum(grad_top, axis=0)
-    grad_normed2 = summed2.astype(jnp.float32)
-    grad_gain2 = jnp.sum(grad_normed2 * scaled2, axis=0)
-    grad_shift2 = jnp.sum(grad_normed2, axis=0)
-    grad_hidden = grad_top + norm_backward(grad_normed2, scaled2, inverse2, norm2_gain)
-    grad_branch = grad_hidden.astype(jnp.bfloat16)
-    grad_bout = jnp.sum(grad_branch.astype(jnp.float32), axis=0)
-    grad_context = jnp.einsum(
-        "td,rd->tr", grad_branch, full_out, preferred_element_type=jnp.float32
-    ).astype(jnp.bfloat16)
-    mlp_sum, grad_projected, grad_bqv, grad_wqkv, grad_wout = attend_sum(
-        prefix_len, mlp_partial, projected, grad_context, normed1_low, context_low, grad_branch
-    )
-    output = (hidden + mlp_sum.astype(jnp.float32) + b_down).astype(jnp.bfloat16)
-    norm1_partial = jnp.einsum(
-        "ctn,cdn->td", grad_projected, full_qkv, preferred_element_type=jnp.float32
-    )
     sent_win = scatter_low(grad_win, 0)
     sent_wdown = scatter_low(grad_wdown, 1)
-    norm1_low = norm1_partial.astype(jnp.bfloat16)
-    grad_wqkv, grad_wout, sent_win, sent_wdown = lax.optimization_barrier(
-        (grad_wqkv, grad_wout, sent_win, sent_wdown)
+    mlp_sum, d_inputs, sent_wqkv, sent_wout, early, late = backward(
+        prefix_len, projected, grad_bin, b_out, norm1_gain, norm2_gain, mlp_partial, normed1_low,
+        context_low, full_qkv, full_out, inputs, attn_sum, d_output, summed2,
     )
-    sent_wout, sent_wqkv = scatter_low(grad_wout, 1), scatter_low(grad_wqkv, 1)
-    grad_normed1 = sum_row(norm1_low).astype(jnp.float32)
-    grad_gain1 = jnp.sum(grad_normed1 * scaled1, axis=0)
-    grad_shift1 = jnp.sum(grad_normed1, axis=0)
-    d_inputs = grad_hidden + norm_backward(grad_normed1, scaled1, inverse1, norm1_gain)
-    small = lax.psum(
-        (
-            grad_gain1,
-            grad_shift1,
-            grad_bqv,
-            grad_bout,
-            grad_gain2,
-            grad_shift2,
-            grad_bin,
-            grad_bdown,
-        ),
-        ("dp", "col"),
-    )
+    hidden = source + attn_sum.astype(jnp.float32) + b_out
+    output = (hidden + mlp_sum.astype(jnp.float32) + b_down).astype(jnp.bfloat16)
+    width = b_qv.shape[1]
     return (
         output,
         d_inputs,
-        small[0],
-        small[1],
+        late[0],
+        late[1],
         sent_wqkv,
-        small[2],
+        early[5, : 2 * width].reshape(2, width),
         sent_wout,
-        small[3],
-        small[4],
-        small[5],
+        early[0],
+        early[1],
+        early[2],
         sent_win,
-        small[6],
+        early[4],
         sent_wdown,
-        small[7],
+        early[3],
     )
 
 

time: 635 us -> 602 us (0.948)
  other arithmetic: 62.9 us -> 27.4 us
  Pallas kernels: 452 us -> 482 us
  blocking collectives: 23.4 us -> 0 us
  matrix products: 23.2 us -> 10.1 us
  local copies, waits for them, and re-layouts: 5.46 us -> 15 us
    psum x1 -> x0, blocking collectives: 23.4 us -> none  [local(): lax.psum((grad_gain1, grad_shift1, grad_bqv, grad_bout, grad_gain2, grad_...]
    pallas_call x2 -> x1, Pallas kernels: 226 us -> 245 us  [backward(): pl.pallas_call(partial(backward_kernel, lax.axis_size('row'), spread), ou...]
    reduce_sum x3 -> x0, other arithmetic: 18 us -> none  [the longest x1 8.23 us: local(): grad_bout = jnp.sum(grad_branch.astype(jnp.float32), axis=0)]
    add x1 -> x0, other arithmetic: 13.6 us -> none  [local(): grad_hidden + norm_backward(grad_normed1, scaled1, inverse1, norm1_gain)]
    dot_general x2 -> x0, matrix products: 13.1 us -> none  [the longest x1 9.79 us: local(): jnp.einsum('ctn,cdn->td', grad_projected, full_qkv, preferred_element_typ...]
    pallas_call x1, Pallas kernels: 215 us -> 226 us  [mlp_sums(): pl.pallas_call(partial(mlp_sums_kernel, lax.axis_size('row'), spread), ou...]
    convert_element_type x0 -> x1, other arithmetic: none -> 7.82 us  [local(): (hidden + mlp_sum.astype(jnp.float32) + b_down).astype(jnp.bfloat16)]
    unnamed x42 -> x27, local copies, waits for them, and re-layouts: 5.38 us -> 11.8 us
  transfers between devices with their start and end apart: 6 -> 4, of which waited for: 3 -> 2; matrix products, arithmetic and copies ran while one was open for 12% -> 6% of each run, Pallas kernels for 38% -> 43%
where the time goes in v5:
time: 602 us; the launch traced here: 595 us
  Pallas kernels  482 us (80%)
  waiting for transfers between devices  44.8 us (7%)
  other arithmetic  27.4 us (5%)
  between operations  15.2 us (3%)
  local copies, waits for them, and re-layouts  15 us (2%)
  matrix products  10.1 us (2%)
    pallas_call x1, Pallas kernels, backward(): pl.pallas_call(partial(backward_kernel, lax.axis_size('row'), spread), ou...  245 us
    pallas_call x1, Pallas kernels, mlp_sums(): pl.pallas_call(partial(mlp_sums_kernel, lax.axis_size('row'), spread), ou...  226 us
    all_gather x1, waiting for transfers between devices, local(): lax.all_gather(low_mats[0], ('dp', 'col'), axis=1, tiled=True)  37.5 us
  transfers between devices with their start and end apart: 4, of which 2 were waited for; matrix products, arithmetic and copies ran while one was open for 6% of the time, Pallas kernels for 43%

profile of v5, /device:TPU:0, one launch (start us, length us, event | category | flops | bytes accessed | tf_op | source)
XLA Modules:
  0.0 594.8 jit_solution(12756231876916115366)
XLA Ops:
  7.2 0.0 all-gather.3.cloned.1.call-start
  7.2 2.5 convert_element_type.40
  9.8 0.0 all-gather.5.cloned.1.call-start
  9.9 1.8 convert_element_type.43
  11.7 0.0 reduce-scatter.5.cloned.1.call-start
  12.5 3.0 convert_reduce_fusion
  15.5 1.1 convert_element_type.44.w_in_hbm
  16.6 0.1 pad.1.clone
  16.7 1.2 fusion.2
  18.0 0.1 pad_maximum_fusion
  18.1 3.2 fusion.5.n1_hbm
  21.2 37.5 %all-gather.3.cloned.1.call-done.w_qkv_hbm = bf16[3,2048,512]{2,1,0:T(8,128)(2,1)} async-done(((bf16[3,256,512]{2,1,0:T(8,128)(2,1)}), bf16[3,2048,512]{2,1,0:T(8,128)(2,1)}) %all-gather.3.cloned.1.call-update) | async-done | bytes 6291472 | tf_op jit(solution)/shard_map/all_gather | solution.py:1179
  58.8 10.1 %fusion.12.projected = bf16[3,1024,512]{2,1,0:T(8,128)(2,1)S(1)} fusion(f32[3,512]{1,0:T(4,128)S(1)} %pad_maximum_fusion, bf16[3,2048,512]{2,1,0:T(8,128)(2,1)} %all-gather.3.cloned.1.call-done.w_qkv_hbm, bf16[1024,2048]{1,0:T(8,128)(2,1)} %fusion.5.n1_hbm), kind=kOutput, calls=%fused_computation.16 | convolution fusion | flops 6445596672 | bytes 13637632 | tf_op jit(solution)/shard_map/td,cdn->ctn/dot_general | solution.py:1190
  68.9 1.2 convert_element_type.45.w_down_hbm
  70.1 0.8 copy-done
  70.9 10.9 %shard_map.254.ctx.ctx_hbm = bf16[1024,512]{1,0:T(8,128)(2,1)S(1)} custom-call(s32[1]{0:T(128)S(6)} %copy.32.prefix_ref, bf16[3,1024,512]{2,1,0:T(8,128)(2,1)S(1)} %fusion.12.projected), custom_call_target="tpu_custom_call" | custom-call | flops 1000 | bytes 1000 | tf_op jit(solution)/shard_map/pallas_call | solution.py:583
  81.8 1.0 copy-done.1
  82.8 6.6 %all-gather.5.cloned.1.call-done.w_out.w_out_hbm = bf16[512,2048]{1,0:T(8,128)(2,1)} async-done(((bf16[512,256]{1,0:T(8,128)(2,1)}), bf16[512,2048]{1,0:T(8,128)(2,1)}) %all-gather.5.cloned.1.call-update) | async-done | bytes 2097168 | tf_op jit(solution)/shard_map/all_gather | solution.py:1180
  89.4 226.2 %shard_map.255 = (bf16[1024,2048]{1,0:T(8,128)(2,1)}, bf16[1024,2048]{1,0:T(8,128)(2,1)}, bf16[1024,2048]{1,0:T(8,128)(2,1)}, bf16[2048,2048]{1,0:T(8,128)(2,1)}...) custom-call(bf16[1024,512]{1,0:T(8,128)(2,1)} %copy-done.1, ...), custom_call_target="tpu_custom_call" | custom-call | flops 1000 | bytes 1000 | tf_op jit(solution)/shard_map/pallas_call | solution.py:510
  315.6 0.0 reduce-scatter.5.cloned.1.call-update
  315.6 0.0 reduce-scatter.3.cloned.1.call-start
  315.7 0.5 reduce-scatter.3.cloned.1.call-update
  316.2 245.2 %shard_map.256 = (bf16[1024,2048]{1,0:T(8,128)(2,1)}, f32[1024,2048]{1,0:T(8,128)}, f32[1024,2048]{1,0:T(8,128)}, bf16[3,2048,512]{2,1,0:T(8,128)(2,1)}, bf16[51...) custom-call(s32[1]{0:T(128)S(6)} %copy.32.prefix_ref, ...), custom_call_target="tpu_custom_call" | custom-call | flops 1000 | bytes 1000 | tf_op jit(solution)/shard_map/pallas_call | solution.py:1100
  561.4 0.8 slice_reduce_fusion
  562.2 0.6 reshape_squeeze.3
  562.8 1.7 fusion.15
  564.5 7.8 %fusion.9 = bf16[1024,2048]{1,0:T(8,128)(2,1)} fusion(bf16[1024,2048]{1,0:T(8,128)(2,1)} %src_hbm.3, bf16[1024,2048]{1,0:T(8,128)(2,1)} %get-tuple-element.30, bf16[1024,2048]{1,0:T(8,128)(2,1)} %get-tuple-element.26.attn_hbm, f32[2048]{0:T(1024)S(1)} %copy-done.9, f32[2048]{0:T(1024)S(1)} %copy-done.7), kind=kLoop, calls=%fused_computation.12 | loop fusion | flops 16777216 | bytes 16793600 | tf_op jit(solution)/shard_map/convert_element_type | solution.py:1205
  572.4 2.7 convert_element_type.50
  575.1 2.8 convert_element_type.49
  577.9 8.0 %copy.33 = f32[1024,2048]{1,0:T(8,128)} copy(f32[1024,2048]{1,0:T(8,128)} %get-tuple-element.64) | data formatting | bytes 16777216
  585.9 1.1 copy.34
  587.0 0.8 copy.35
  (29 shorter events, 0.1 us)
Async XLA Ops:
  7.2 8.3 %copy-start.3 = (f32[256,2048]{1,0:T(8,128)S(1)}, f32[256,2048]{1,0:T(8,128)}, u32[]{:S(2)}) copy-start(f32[256,2048]{1,0:T(8,128)} %param.25) | copy-start | bytes 6291460
  7.2 51.6 %all-gather.3.cloned.1.call-start = ((), (), s32[]{:S(2)}) async-start(), calls=%async_computation.2 | async-start | bytes 7077888 | tf_op jit(solution)/shard_map/all_gather | solution.py:1179
  9.8 8.2 %copy-start.11 = (f32[2,512]{1,0:T(2,128)S(1)}, f32[2,512]{1,0:T(2,128)}, u32[]{:S(2)}) copy-start(f32[2,512]{1,0:T(2,128)} %param.20) | copy-start | bytes 12292
  9.8 8.3 %copy-start.8 = (f32[2048]{0:T(1024)S(1)}, f32[2048]{0:T(1024)}, u32[]{:S(2)}) copy-start(f32[2048]{0:T(1024)} %param.17) | copy-start | bytes 24580
  9.8 8.2 %copy-start.10 = (f32[2048]{0:T(1024)S(1)}, f32[2048]{0:T(1024)}, u32[]{:S(2)}) copy-start(f32[2048]{0:T(1024)} %param.18) | copy-start | bytes 24580
  9.8 79.6 %all-gather.5.cloned.1.call-start = ((), (), s32[]{:S(2)}) async-start(), calls=%async_computation.3 | async-start | bytes 2359296 | tf_op jit(solution)/shard_map/all_gather | solution.py:1180
  11.7 560.7 %reduce-scatter.5.cloned.1.call-start = ((), (), s32[]{:S(2)}) async-start(), calls=%async_computation.5 | async-start | bytes 9437184 | tf_op jit(solution)/shard_map/reduce_scatter | solution.py:1151
  11.7 5.0 copy-start.2
  21.2 47.7 %copy-start.4 = (f32[2048,256]{1,0:T(8,128)S(1)}, f32[2048,256]{1,0:T(8,128)}, u32[]{:S(2)}) copy-start(f32[2048,256]{1,0:T(8,128)} %param.27) | copy-start | bytes 6291460
  68.9 2.0 copy-start
  81.8 1.0 copy-start.1
  315.6 259.4 %reduce-scatter.3.cloned.1.call-start = ((), (), s32[]{:S(2)}) async-start(), calls=%async_computation.4 | async-start | bytes 9437184 | tf_op jit(solution)/shard_map/reduce_scatter | solution.py:1151
  316.2 248.3 %copy-start.7 = (f32[2048]{0:T(1024)S(1)}, f32[2048]{0:T(1024)}, u32[]{:S(2)}) copy-start(f32[2048]{0:T(1024)} %param.22) | copy-start | bytes 24580
  316.2 248.3 %copy-start.9 = (f32[2048]{0:T(1024)S(1)}, f32[2048]{0:T(1024)}, u32[]{:S(2)}) copy-start(f32[2048]{0:T(1024)} %param.28) | copy-start | bytes 24580
  577.8 8.0 %copy-start.5 = (f32[3,256,512]{2,1,0:T(8,128)S(1)}, f32[3,256,512]{2,1,0:T(8,128)}, u32[]{:S(2)}) copy-start(f32[3,256,512]{2,1,0:T(8,128)} %get-tuple-element.67) | copy-start | bytes 4718596
  577.9 9.2 %copy-start.6 = (f32[512,256]{1,0:T(8,128)S(1)}, f32[512,256]{1,0:T(8,128)}, u32[]{:S(2)}) copy-start(f32[512,256]{1,0:T(8,128)} %get-tuple-element.69) | copy-start | bytes 1572868
Sparse Core Ops, SparseCore 0:
  10.5 48.2 all-gather.2
  61.2 28.1 all-gather.4
  315.7 68.8 reduce-scatter.4
  388.3 95.1 reduce-scatter.2

commit v6 on v5

--- a/solution.py
+++ b/solution.py
@@ -292,6 +292,7 @@
 
 
 TILE = 512
+FEW = 16
 BLOCK = 256
 
 
@@ -400,13 +401,13 @@
             copy.wait()
 
         def few(k):
-            here = pl.ds(pl.multiple_of(k * 64, 64), 64)
-            there = pl.ds(pl.multiple_of(j * BLOCK + k * 64, 64), 64)
+            here = pl.ds(pl.multiple_of(k * FEW, FEW), FEW)
+            there = pl.ds(pl.multiple_of(j * BLOCK + k * FEW, FEW), FEW)
             source = rows_b[here].astype(jnp.float32)
             hidden = source + rows_a[here].astype(jnp.float32) + b_out[...]
             normed[there] = norm_forward(hidden, gain[...], shift[...])[0].astype(jnp.bfloat16)
 
-        loop(0, BLOCK // 64, few)
+        loop(0, BLOCK // FEW, few)
 
     def mlp_out(j):
         return [
@@ -552,6 +553,100 @@
 QUERY_ROWS = 256
 
 
+def head_kernel(
+    prefix_ref, src, gain, shift, b_q, b_v, w_qkv_hbm, w_out_hbm,
+    normed, projected, context, full_qkv, full_out,
+    weights, w_out, store_sem, *sems,
+):
+    tokens, depth = src.shape
+    width = projected.shape[2]
+    deep, wide = w_qkv_hbm.shape[1], w_out_hbm.shape[1]
+    size, tall = deep // 2, width // 2
+
+    def qkv_piece(c, k, place):
+        there = pl.ds(pl.multiple_of(place * deep + k * size, size), size)
+        return w_qkv_hbm.at[c, pl.ds(k * size, size)], weights.at[c, there]
+
+    def out_piece(k, place):
+        some = pl.ds(k * tall, tall)
+        cols = pl.ds(pl.multiple_of(place * wide, wide), wide)
+        return w_out_hbm.at[some], w_out.at[some, cols]
+
+    qkv_pieces = [partial(qkv_piece, c, k) for c in range(3) for k in range(2)]
+    out_pieces = [partial(out_piece, k) for k in range(2)]
+    others, start1, arrive1, far1, finish1 = plane_gather(qkv_pieces, *sems[:5])
+    _, start2, arrive2, far2, finish2 = plane_gather(out_pieces, *sems[5:])
+    bar = pltpu.get_barrier_semaphore()
+    for other in others:
+        pl.semaphore_signal(bar, inc=1, device_id=other, device_id_type=MESH_IDS)
+    pl.semaphore_wait(bar, len(others))
+    start1()
+
+    def few(r):
+        here = pl.ds(pl.multiple_of(r * FEW, FEW), FEW)
+        rows = norm_forward(src[here].astype(jnp.float32), gain[...], shift[...])[0]
+        normed[here] = rows.astype(jnp.bfloat16)
+
+    loop(0, tokens // FEW, few)
+    for k in range(len(qkv_pieces)):
+        arrive1(k)
+    start2()
+    for k in range(len(qkv_pieces)):
+        far1(k)
+    finish1()
+    stores = [pltpu.make_async_copy(weights, full_qkv, store_sem.at[0])]
+    stores[0].start()
+    for c in range(3):
+
+        def rows_of(i):
+            here = pl.ds(pl.multiple_of(i * BLOCK, BLOCK), BLOCK)
+            term = dot(normed[here], weights[c], 1, 0)
+            if c != 1:
+                term += (b_q if c == 0 else b_v)[...]
+            projected[c, here] = term.astype(jnp.bfloat16)
+
+        loop(0, tokens // BLOCK, rows_of)
+    for k in range(len(out_pieces)):
+        arrive2(k)
+    attend_kernel(prefix_ref, projected, context)
+    for k in range(len(out_pieces)):
+        far2(k)
+    finish2()
+    stores.append(pltpu.make_async_copy(w_out, full_out, store_sem.at[1]))
+    stores[1].start()
+    for store in stores:
+        store.wait()
+
+
+def head(prefix_len, inputs, gain, shift, b_qv, w_qkv, w_out):
+    tokens, depth = inputs.shape
+    width = w_out.shape[0]
+    dma = pltpu.SemaphoreType.DMA
+    return pl.pallas_call(
+        head_kernel,
+        out_shape=[
+            low_shape(tokens, depth),
+            low_shape(3, tokens, width),
+            low_shape(tokens, width),
+            low_shape(3, depth, width),
+            low_shape(width, depth),
+        ],
+        in_specs=[pl.BlockSpec(memory_space=pltpu.SMEM)] + [IN_VMEM] * 5 + [IN_HBM] * 2,
+        out_specs=[IN_VMEM] * 3 + [IN_HBM] * 2,
+        scratch_shapes=[
+            pltpu.VMEM((3, depth, width), jnp.bfloat16),
+            pltpu.VMEM((width, depth), jnp.bfloat16),
+            dma((2,)),
+        ]
+        + [dma((4, 6))] * 4
+        + [dma((6,))]
+        + [dma((4, 2))] * 4
+        + [dma((2,))],
+        compiler_params=kernel_params(3, 40),
+        cost_estimate=COST,
+    )(prefix_len, inputs, gain[None], shift[None], b_qv[:1], b_qv[1:], w_qkv, w_out)
+
+
 def block_probs(i, prefix, cols, q, k):
     start = i * QUERY_ROWS
     width = max(start + QUERY_ROWS, q.shape[0] // 2)
@@ -725,7 +820,7 @@
     n, spread, prefix_ref, projected, d_bin, b_out, gain1, gain2,
     mlp_hbm, n1_hbm, ctx_hbm, w_qkv_hbm, w_out_hbm, src_hbm, attn_hbm, g_hbm, dn2_hbm,
     mlp_sum, d_inputs, d_hidden, d_wqkv, d_wout, sum_wqkv, sum_wout, early, late,
-    p, d_context, n1, ctx, branch, d_key, d_value, d_proj, w_stage, total, weights, ring,
+    p, d_context, n1, ctx, branch, d_key, d_value, d_proj, w_stage, total, weights, ring, partial_sums,
     p_sem, slice_sem, load_sem, store_sem, ring_in, ring_out, *more,
 ):
     lines, more = more[:12], more[12:]
@@ -766,6 +861,7 @@
     early[...] = jnp.zeros_like(early)
     late[...] = jnp.zeros_like(late)
     early[4:5] = d_bin[...]
+    partial_sums[...] = jnp.zeros_like(partial_sums)
     others = []
     if spread:
         slots_e, slots_l, small_s, small_r = more[:4]
@@ -875,14 +971,21 @@
         def _():
             hidden_store(k - RING).wait()
 
-        dn, attn, source, g = (total[slice_slot(k, i)].astype(jnp.float32) for i in range(4))
-        _, scaled, inverse = norm_forward(source + attn + b_out[...], 1.0, 0.0)
-        grad = g + norm_backward(dn, scaled, inverse, gain2[...])
-        low = grad.astype(jnp.bfloat16)
-        branch[slice_rows(k)] = low
-        for i, term in enumerate((low.astype(jnp.float32), dn * scaled, dn, g)):
-            early[i : i + 1] += jnp.sum(term, axis=0, keepdims=True)
-        ring[lax.rem(k, RING)] = grad
+        def few(r):
+            rows = [
+                pl.ds(pl.multiple_of(half + (lax.rem(k, 2) * 4 + i) * SLICE + r * FEW, FEW), FEW)
+                for i in range(4)
+            ]
+            dn, attn, source, g = (total[some].astype(jnp.float32) for some in rows)
+            _, scaled, inverse = norm_forward(source + attn + b_out[...], 1.0, 0.0)
+            grad = g + norm_backward(dn, scaled, inverse, gain2[...])
+            low = grad.astype(jnp.bfloat16)
+            branch[pl.ds(pl.multiple_of(k * SLICE + r * FEW, FEW), FEW)] = low
+            for i, term in enumerate((low.astype(jnp.float32), dn * scaled, dn, g)):
+                partial_sums[8 * i : 8 * i + 8] += term[:8] + term[8:]
+            ring[lax.rem(k, RING), pl.ds(pl.multiple_of(r * FEW, FEW), FEW)] = grad
+
+        loop(0, SLICE // FEW, few)
         hidden_store(k).start()
 
     for load in slice_loads(0):
@@ -896,6 +999,8 @@
         loop(t * (slices // norm_ticks), (t + 1) * (slices // norm_ticks), norm_slice)
 
     loop(0, norm_ticks, norm_tick)
+    for i in range(4):
+        early[i : i + 1] = jnp.sum(partial_sums[8 * i : 8 * i + 8], axis=0, keepdims=True)
     for k in range(slices - RING, slices):
         hidden_store(k).wait()
     for some in p_loads[1:]:
@@ -910,6 +1015,7 @@
         d_context[rows] = dot(branch[rows], total[:width], 1, 1).astype(jnp.bfloat16)
 
     loop(0, tokens // BLOCK, context_rows)
+    partial_sums[...] = jnp.zeros_like(partial_sums)
 
     q, k, v = (projected.at[c] for c in range(3))
     q_blocks = tokens // QUERY_ROWS
@@ -1005,12 +1111,14 @@
         for load in hidden_loads(c):
             load.wait()
         for side, rows in enumerate(sides(c, CHUNK)):
-            _, scaled, inverse = norm_forward(n1[rows].astype(jnp.float32), 1.0, 0.0)
-            grad = total[rows].astype(jnp.float32)
-            late[0:1] += jnp.sum(grad * scaled, axis=0, keepdims=True)
-            late[1:2] += jnp.sum(grad, axis=0, keepdims=True)
-            here = pl.ds(side * CHUNK, CHUNK)
-            ring[lax.rem(c, RING), here] += norm_backward(grad, scaled, inverse, gain1[...])
+            for r in range(CHUNK // FEW):
+                some = pl.ds(pl.multiple_of(rows.start + r * FEW, FEW), FEW)
+                _, scaled, inverse = norm_forward(n1[some].astype(jnp.float32), 1.0, 0.0)
+                grad = total[some].astype(jnp.float32)
+                for i, term in enumerate((grad * scaled, grad)):
+                    partial_sums[8 * i : 8 * i + 8] += term[:8] + term[8:]
+                here = pl.ds(side * CHUNK + r * FEW, FEW)
+                ring[lax.rem(c, RING), here] += norm_backward(grad, scaled, inverse, gain1[...])
         for store in input_stores(c):
             store.start()
 
@@ -1042,15 +1150,17 @@
             loads[3].wait()
         begin = chunks + j * per_block
         loop(begin, begin + per_block, tick_of if j == blocks - 1 else both_steps)
-        if spread and j == 0:
-            pair()
-        if spread and j == 2:
-            cross()
-            for i in range(3):
-                early_begin(i)
-                early_end(i)
+        if spread:
+            if j == 0:
+                pair()
+            else:
+                early_end(j - 1)
+            if j < blocks - 1:
+                early_begin(j)
+            else:
+                cross()
     begin = chunks + blocks * per_block
-    middle = begin + per_block
+    middle = begin + 2 * per_block
     loop(begin, middle, tick_of)
     if spread:
         for k in range(len(pieces)):
@@ -1058,6 +1168,8 @@
         for store in stores:
             store.start()
     loop(middle, arrival + chunks, tick_of)
+    for i in range(2):
+        late[i : i + 1] = jnp.sum(partial_sums[8 * i : 8 * i + 8], axis=0, keepdims=True)
     if spread:
         for i in range(3):
             late_begin(i)
@@ -1124,6 +1236,7 @@
             buffer(tokens, depth),
             buffer(*w_qkv.shape),
             wide_buffer(RING, SLICE, depth),
+            wide_buffer(32, depth),
             dma((2, tokens // BLOCK)),
             dma((2, 4)),
             dma((5,)),
@@ -1175,22 +1288,25 @@
         w_in.astype(jnp.bfloat16),
         w_down.astype(jnp.bfloat16),
     )
-    full_qkv, full_out, full_in, full_down = (
-        lax.all_gather(low_mats[0], ("dp", "col"), axis=1, tiled=True),
-        lax.all_gather(low_mats[1], ("dp", "col"), axis=1, tiled=True),
-        low_mats[2],
-        low_mats[3],
-    )
-    if (lax.axis_size("dp"), lax.axis_size("col")) != (2, 4):
+    full_in, full_down = low_mats[2:]
+    source = inputs.astype(jnp.float32)
+    if (lax.axis_size("dp"), lax.axis_size("col")) == (2, 4):
+        normed1_low, projected, context_low, full_qkv, full_out = head(
+            prefix_len, inputs, norm1_gain, norm1_shift, b_qv, low_mats[0], low_mats[1]
+        )
+    else:
+        full_qkv = lax.all_gather(low_mats[0], ("dp", "col"), axis=1, tiled=True)
+        full_out = lax.all_gather(low_mats[1], ("dp", "col"), axis=1, tiled=True)
         full_in = lax.all_gather(full_in, ("dp", "col"), axis=0, tiled=True)
         full_down = lax.all_gather(full_down, ("dp", "col"), axis=1, tiled=True)
-    source = inputs.astype(jnp.float32)
-    normed1, _, _ = norm_forward(source, norm1_gain, norm1_shift)
-    normed1_low = normed1.astype(jnp.bfloat16)
-    projected = jnp.einsum("td,cdn->ctn", normed1_low, full_qkv, preferred_element_type=jnp.float32)
-    bias_rows = jnp.stack([b_qv[0], jnp.zeros_like(b_qv[0]), b_qv[1]])
-    projected = (projected + bias_rows[:, None, :]).astype(jnp.bfloat16)
-    context_low = attend(prefix_len, projected)
+        normed1, _, _ = norm_forward(source, norm1_gain, norm1_shift)
+        normed1_low = normed1.astype(jnp.bfloat16)
+        projected = jnp.einsum(
+            "td,cdn->ctn", normed1_low, full_qkv, preferred_element_type=jnp.float32
+        )
+        bias_rows = jnp.stack([b_qv[0], jnp.zeros_like(b_qv[0]), b_qv[1]])
+        projected = (projected + bias_rows[:, None, :]).astype(jnp.bfloat16)
+        context_low = attend(prefix_len, projected)
     attn_sum, summed2, mlp_partial, grad_wdown, grad_win, grad_bin = mlp_sums(
         context_low, full_out, b_out, norm2_gain, norm2_shift, b_in,
         inputs, full_in, full_down, d_output,

time: 602 us -> 572 us (0.950)
  waiting for transfers between devices: 44.8 us -> 0.72 us
  Pallas kernels: 482 us -> 512 us
  matrix products: 10.1 us -> 0 us
  other arithmetic: 27.4 us -> 18.1 us
    pallas_call x1, Pallas kernels: 10.9 us -> 56.9 us  [head(): pl.pallas_call(head_kernel, out_shape=[low_shape(tokens, depth), low_shap...]
    all_gather x2 -> x0, waiting for transfers between devices: 44.2 us -> none  [the longest x1 37.5 us: local(): lax.all_gather(low_mats[0], ('dp', 'col'), axis=1, tiled=True)]
    pallas_call x1, Pallas kernels: 245 us -> 233 us  [backward(): pl.pallas_call(partial(backward_kernel, lax.axis_size('row'), spread), ou...]
    dot_general x1 -> x0, matrix products: 10.1 us -> none  [local(): jnp.einsum('td,cdn->ctn', normed1_low, full_qkv, preferred_element_type=j...]
  transfers between devices with their start and end apart: 4 -> 2, of which waited for: 2 -> 0; matrix products, arithmetic and copies ran while one was open for 6% -> 2% of each run, Pallas kernels for 43% -> 41%
where the time goes in v6:
time: 572 us; the launch traced here: 567 us
  Pallas kernels  512 us (90%)
  local copies, waits for them, and re-layouts  20.3 us (4%)
  other arithmetic  18.1 us (3%)
  between operations  15.2 us (3%)
    pallas_call x1, Pallas kernels, backward(): pl.pallas_call(partial(backward_kernel, lax.axis_size('row'), spread), ou...  233 us
    pallas_call x1, Pallas kernels, mlp_sums(): pl.pallas_call(partial(mlp_sums_kernel, lax.axis_size('row'), spread), ou...  222 us
    pallas_call x1, Pallas kernels, head(): pl.pallas_call(head_kernel, out_shape=[low_shape(tokens, depth), low_shap...  56.9 us
    unnamed x27, local copies, waits for them, and re-layouts  16 us
  transfers between devices with their start and end apart: 2, of which 0 were waited for; matrix products, arithmetic and copies ran while one was open for 2% of the time, Pallas kernels for 41%

profile of v6, /device:TPU:0, one launch (start us, length us, event | category | flops | bytes accessed | tf_op | source)
XLA Modules:
  0.0 566.8 jit_solution(4153835882684622195)
XLA Ops:
  7.2 0.0 reduce-scatter.5.cloned.1.call-start
  8.0 1.1 fusion.2
  9.2 1.1 convert_element_type.32.w_out_hbm
  10.2 0.0 copy-start.4
  10.2 0.0 copy-start.5
  10.3 1.5 convert_element_type.31.w_qkv_hbm
  11.8 1.1 convert_element_type.33.w_in_hbm
  12.9 1.1 convert_element_type.34.w_down_hbm
  14.0 0.0 copy-done.4
  14.0 56.9 %shard_map.254 = (bf16[1024,2048]{1,0:T(8,128)(2,1)S(1)}, bf16[3,1024,512]{2,1,0:T(8,128)(2,1)S(1)}, bf16[1024,512]{1,0:T(8,128)(2,1)S(1)}, bf16[3,2048,512]{2,1,0:T(8,128)(2,1)}, bf16[512,2048]{1,0:T(8,128)(2,1)S(1)}) custom-call(s32[1]{0:T(128)S(6)} %copy.32.prefix_ref, bf16[1024,2048]{1,0:T(8,128)(2,1)} %src_hbm.3, f32[1,2048]{1,0:T(1,128)S(1)} %bitcast.14, ...), custom_call_target="tpu_custom_call" | custom-call | flops 1000 | bytes 1000 | tf_op jit(solution)/shard_map/pallas_call | solution.py:625
  70.9 0.0 copy-start
  70.9 1.3 copy-done
  72.2 2.0 copy-done.1
  74.2 1.0 copy-done.2
  75.2 1.7 copy-done.3
  76.9 222.4 %shard_map.255 = (bf16[1024,2048]{1,0:T(8,128)(2,1)}, bf16[1024,2048]{1,0:T(8,128)(2,1)}, bf16[1024,2048]{1,0:T(8,128)(2,1)}, bf16[2048,2048]{1,0:T(8,128)(2,1)}...) custom-call(bf16[1024,512]{1,0:T(8,128)(2,1)} %copy-done.2, bf16[512,2048]{1,0:T(8,128)(2,1)} %copy-done, ...), custom_call_target="tpu_custom_call" | custom-call | flops 1000 | bytes 1000 | tf_op jit(solution)/shard_map/pallas_call | solution.py:511
  299.3 0.0 reduce-scatter.5.cloned.1.call-update
  299.3 0.0 reduce-scatter.3.cloned.1.call-start
  299.4 0.7 reduce-scatter.3.cloned.1.call-update
  300.1 0.0 copy-start.10
  300.1 0.0 copy-start.11
  300.1 233.2 %shard_map.256 = (bf16[1024,2048]{1,0:T(8,128)(2,1)}, f32[1024,2048]{1,0:T(8,128)}, f32[1024,2048]{1,0:T(8,128)}, bf16[3,2048,512]{2,1,0:T(8,128)(2,1)}, bf16[51...) custom-call(s32[1]{0:T(128)S(6)} %copy.32.prefix_ref, ...), custom_call_target="tpu_custom_call" | custom-call | flops 1000 | bytes 1000 | tf_op jit(solution)/shard_map/pallas_call | solution.py:1212
  533.3 0.8 slice_reduce_fusion
  534.1 0.6 reshape_squeeze.3
  534.7 1.8 fusion
  536.5 0.0 copy-done.10
  536.5 7.8 %add_convert_fusion = bf16[1024,2048]{1,0:T(8,128)(2,1)} fusion(bf16[1024,2048]{1,0:T(8,128)(2,1)} %get-tuple-element.40, bf16[1024,2048]{1,0:T(8,128)(2,1)} %get-tuple-element.33.attn_hbm, bf16[1024,2048]{1,0:T(8,128)(2,1)} %src_hbm.3, f32[2048]{0:T(1024)S(1)} %copy-done.11, f32[2048]{0:T(1024)S(1)} %copy-done.10), kind=kLoop, calls=%fused_computation | loop fusion | flops 16777216 | bytes 16793600 | tf_op jit(solution)/shard_map/convert_element_type | solution.py:1321
  544.3 2.7 convert_element_type.39
  547.0 2.8 convert_element_type.38
  549.8 8.0 %copy.33 = f32[1024,2048]{1,0:T(8,128)} copy(f32[1024,2048]{1,0:T(8,128)} %get-tuple-element.74) | data formatting | bytes 16777216
  557.8 1.1 copy.34
  559.0 0.8 copy.35
  (15 shorter events, 0.0 us)
Async XLA Ops:
  7.2 4.6 copy-start.6
  7.2 537.1 %reduce-scatter.5.cloned.1.call-start = ((), (), s32[]{:S(2)}) async-start(), calls=%async_computation.3 | async-start | bytes 9437184 | tf_op jit(solution)/shard_map/reduce_scatter | solution.py:1264
  7.2 5.7 %copy-start.7 = (f32[2048,256]{1,0:T(8,128)S(1)}, f32[2048,256]{1,0:T(8,128)}, u32[]{:S(2)}) copy-start(f32[2048,256]{1,0:T(8,128)} %param.27) | copy-start | bytes 6291460
  10.2 3.8 copy-start.4
  10.2 3.8 copy-start.5
  70.9 1.3 copy-start
  72.2 2.0 copy-start.1
  74.2 1.0 copy-start.2
  75.2 1.7 copy-start.3
  299.3 247.7 %reduce-scatter.3.cloned.1.call-start = ((), (), s32[]{:S(2)}) async-start(), calls=%async_computation.2 | async-start | bytes 9437184 | tf_op jit(solution)/shard_map/reduce_scatter | solution.py:1264
  300.1 236.5 %copy-start.10 = (f32[2048]{0:T(1024)S(1)}, f32[2048]{0:T(1024)}, u32[]{:S(2)}) copy-start(f32[2048]{0:T(1024)} %param.22) | copy-start | bytes 24580
  300.1 236.4 %copy-start.11 = (f32[2048]{0:T(1024)S(1)}, f32[2048]{0:T(1024)}, u32[]{:S(2)}) copy-start(f32[2048]{0:T(1024)} %param.28) | copy-start | bytes 24580
  549.8 8.0 %copy-start.8 = (f32[3,256,512]{2,1,0:T(8,128)S(1)}, f32[3,256,512]{2,1,0:T(8,128)}, u32[]{:S(2)}) copy-start(f32[3,256,512]{2,1,0:T(8,128)} %get-tuple-element.77) | copy-start | bytes 4718596
  549.8 9.2 %copy-start.9 = (f32[512,256]{1,0:T(8,128)S(1)}, f32[512,256]{1,0:T(8,128)}, u32[]{:S(2)}) copy-start(f32[512,256]{1,0:T(8,128)} %get-tuple-element.79) | copy-start | bytes 1572868
Sparse Core Ops, SparseCore 0:
  299.4 70.4 reduce-scatter.4
  373.8 92.2 reduce-scatter.2

commit v7 on v6

--- a/solution.py
+++ b/solution.py
@@ -401,13 +401,13 @@
             copy.wait()
 
         def few(k):
-            here = pl.ds(pl.multiple_of(k * FEW, FEW), FEW)
-            there = pl.ds(pl.multiple_of(j * BLOCK + k * FEW, FEW), FEW)
+            here = pl.ds(pl.multiple_of(k * 64, 64), 64)
+            there = pl.ds(pl.multiple_of(j * BLOCK + k * 64, 64), 64)
             source = rows_b[here].astype(jnp.float32)
             hidden = source + rows_a[here].astype(jnp.float32) + b_out[...]
             normed[there] = norm_forward(hidden, gain[...], shift[...])[0].astype(jnp.bfloat16)
 
-        loop(0, BLOCK // FEW, few)
+        loop(0, BLOCK // 64, few)
 
     def mlp_out(j):
         return [
@@ -555,8 +555,8 @@
 
 def head_kernel(
     prefix_ref, src, gain, shift, b_q, b_v, w_qkv_hbm, w_out_hbm,
-    normed, projected, context, full_qkv, full_out,
-    weights, w_out, store_sem, *sems,
+    normed_out, projected_out, context_out, full_qkv, full_out,
+    weights, w_out, normed, projected, context, store_sem, *sems,
 ):
     tokens, depth = src.shape
     width = projected.shape[2]
@@ -572,31 +572,50 @@
         cols = pl.ds(pl.multiple_of(place * wide, wide), wide)
         return w_out_hbm.at[some], w_out.at[some, cols]
 
-    qkv_pieces = [partial(qkv_piece, c, k) for c in range(3) for k in range(2)]
-    out_pieces = [partial(out_piece, k) for k in range(2)]
-    others, start1, arrive1, far1, finish1 = plane_gather(qkv_pieces, *sems[:5])
-    _, start2, arrive2, far2, finish2 = plane_gather(out_pieces, *sems[5:])
+    parts = [[partial(qkv_piece, c, k) for k in range(2)] for c in range(3)]
+    parts.append([partial(out_piece, k) for k in range(2)])
+    others = list(plane_partners()[0].values())
+    start, arrive, far, finish = zip(
+        *[plane_gather(part, *sems[5 * i : 5 * i + 5])[1:] for i, part in enumerate(parts)]
+    )
     bar = pltpu.get_barrier_semaphore()
     for other in others:
         pl.semaphore_signal(bar, inc=1, device_id=other, device_id_type=MESH_IDS)
     pl.semaphore_wait(bar, len(others))
-    start1()
+    start[0]()
+    start[1]()
 
     def few(r):
         here = pl.ds(pl.multiple_of(r * FEW, FEW), FEW)
         rows = norm_forward(src[here].astype(jnp.float32), gain[...], shift[...])[0]
         normed[here] = rows.astype(jnp.bfloat16)
 
-    loop(0, tokens // FEW, few)
-    for k in range(len(qkv_pieces)):
-        arrive1(k)
-    start2()
-    for k in range(len(qkv_pieces)):
-        far1(k)
-    finish1()
-    stores = [pltpu.make_async_copy(weights, full_qkv, store_sem.at[0])]
+    loop(0, tokens // FEW // 4, lambda r: [few(4 * r + i) for i in range(4)])
+    stores = [
+        pltpu.make_async_copy(src, dst, store_sem.at[i])
+        for i, (src, dst) in enumerate(
+            (
+                (normed, normed_out),
+                (weights, full_qkv),
+                (projected, projected_out),
+                (w_out, full_out),
+                (context, context_out),
+            )
+        )
+    ]
     stores[0].start()
+    for i in range(2):
+        for k in range(2):
+            arrive[i](k)
+    start[2]()
     for c in range(3):
+        if c == 2:
+            for k in range(2):
+                arrive[2](k)
+            start[3]()
+        for k in range(2):
+            far[c](k)
+        finish[c]()
 
         def rows_of(i):
             here = pl.ds(pl.multiple_of(i * BLOCK, BLOCK), BLOCK)
@@ -606,14 +625,16 @@
             projected[c, here] = term.astype(jnp.bfloat16)
 
         loop(0, tokens // BLOCK, rows_of)
-    for k in range(len(out_pieces)):
-        arrive2(k)
+    stores[1].start()
+    stores[2].start()
+    for k in range(2):
+        arrive[3](k)
     attend_kernel(prefix_ref, projected, context)
-    for k in range(len(out_pieces)):
-        far2(k)
-    finish2()
-    stores.append(pltpu.make_async_copy(w_out, full_out, store_sem.at[1]))
-    stores[1].start()
+    stores[4].start()
+    for k in range(2):
+        far[3](k)
+    finish[3]()
+    stores[3].start()
     for store in stores:
         store.wait()
 
@@ -632,16 +653,16 @@
             low_shape(width, depth),
         ],
         in_specs=[pl.BlockSpec(memory_space=pltpu.SMEM)] + [IN_VMEM] * 5 + [IN_HBM] * 2,
-        out_specs=[IN_VMEM] * 3 + [IN_HBM] * 2,
+        out_specs=[IN_HBM] * 5,
         scratch_shapes=[
             pltpu.VMEM((3, depth, width), jnp.bfloat16),
             pltpu.VMEM((width, depth), jnp.bfloat16),
-            dma((2,)),
+            pltpu.VMEM((tokens, depth), jnp.bfloat16),
+            pltpu.VMEM((3, tokens, width), jnp.bfloat16),
+            pltpu.VMEM((tokens, width), jnp.bfloat16),
+            dma((5,)),
         ]
-        + [dma((4, 6))] * 4
-        + [dma((6,))]
-        + [dma((4, 2))] * 4
-        + [dma((2,))],
+        + ([dma((4, 2))] * 4 + [dma((2,))]) * 4,
         compiler_params=kernel_params(3, 40),
         cost_estimate=COST,
     )(prefix_len, inputs, gain[None], shift[None], b_qv[:1], b_qv[1:], w_qkv, w_out)
@@ -985,7 +1006,8 @@
                 partial_sums[8 * i : 8 * i + 8] += term[:8] + term[8:]
             ring[lax.rem(k, RING), pl.ds(pl.multiple_of(r * FEW, FEW), FEW)] = grad
 
-        loop(0, SLICE // FEW, few)
+        for r in range(SLICE // FEW):
+            few(r)
         hidden_store(k).start()
 
     for load in slice_loads(0):

time: 572 us -> 556 us (0.972)
  Pallas kernels: 512 us -> 496 us
    pallas_call x1, Pallas kernels: 222 us -> 215 us  [mlp_sums(): pl.pallas_call(partial(mlp_sums_kernel, lax.axis_size('row'), spread), ou...]
    pallas_call x1, Pallas kernels: 233 us -> 227 us  [backward(): pl.pallas_call(partial(backward_kernel, lax.axis_size('row'), spread), ou...]
where the time goes in v7:
time: 556 us; the launch traced here: 551 us
  Pallas kernels  496 us (89%)
  local copies, waits for them, and re-layouts  20.3 us (4%)
  other arithmetic  18.1 us (3%)
  between operations  15.2 us (3%)
    pallas_call x1, Pallas kernels, backward(): pl.pallas_call(partial(backward_kernel, lax.axis_size('row'), spread), ou...  227 us
    pallas_call x1, Pallas kernels, mlp_sums(): pl.pallas_call(partial(mlp_sums_kernel, lax.axis_size('row'), spread), ou...  215 us
    pallas_call x1, Pallas kernels, head(): pl.pallas_call(head_kernel, out_shape=[low_shape(tokens, depth), low_shap...  54 us
    unnamed x27, local copies, waits for them, and re-layouts  16 us
  transfers between devices with their start and end apart: 2, of which 0 were waited for; matrix products, arithmetic and copies ran while one was open for 2% of the time, Pallas kernels for 41%

profile of v7, /device:TPU:0, one launch (start us, length us, event | category | flops | bytes accessed | tf_op | source)
XLA Modules:
  0.0 550.7 jit_solution(17890834657637213194)
XLA Ops:
  7.2 0.0 copy-start.6
  7.2 0.0 reduce-scatter.5.cloned.1.call-start
  7.2 0.0 copy-start.7
  8.0 1.1 fusion.2
  9.2 1.1 convert_element_type.32.w_out_hbm
  10.2 0.0 copy-start.4
  10.2 0.0 copy-start.5
  10.3 1.5 convert_element_type.31.w_qkv_hbm
  11.8 1.1 convert_element_type.33.w_in_hbm
  12.9 1.1 convert_element_type.34.w_down_hbm
  14.0 54.0 %shard_map.254 = (bf16[1024,2048]{1,0:T(8,128)(2,1)S(1)}, bf16[3,1024,512]{2,1,0:T(8,128)(2,1)S(1)}, bf16[1024,512]{1,0:T(8,128)(2,1)S(1)}, bf16[3,2048,512]{2,1,0:T(8,128)(2,1)}, bf16[512,2048]{1,0:T(8,128)(2,1)S(1)}) custom-call(s32[1]{0:T(128)S(6)} %copy.32.prefix_ref, bf16[1024,2048]{1,0:T(8,128)(2,1)} %src_hbm.3, f32[1,2048]{1,0:T(1,128)S(1)} %bitcast.14, ...), custom_call_target="tpu_custom_call" | custom-call | flops 1000 | bytes 1000 | tf_op jit(solution)/shard_map/pallas_call | solution.py:646
  68.0 0.0 copy-start
  68.0 1.3 copy-done
  69.3 2.0 copy-done.1
  71.3 1.0 copy-done.2
  72.3 1.7 copy-done.3
  74.0 215.3 %shard_map.255 = (bf16[1024,2048]{1,0:T(8,128)(2,1)}, bf16[1024,2048]{1,0:T(8,128)(2,1)}, bf16[1024,2048]{1,0:T(8,128)(2,1)}, bf16[2048,2048]{1,0:T(8,128)(2,1)}...) custom-call(bf16[1024,512]{1,0:T(8,128)(2,1)} %copy-done.2, bf16[512,2048]{1,0:T(8,128)(2,1)} %copy-done, ...), custom_call_target="tpu_custom_call" | custom-call | flops 1000 | bytes 1000 | tf_op jit(solution)/shard_map/pallas_call | solution.py:511
  289.3 0.0 reduce-scatter.5.cloned.1.call-update
  289.3 0.0 reduce-scatter.3.cloned.1.call-start
  289.4 0.7 reduce-scatter.3.cloned.1.call-update
  290.1 0.0 copy-start.10
  290.1 0.0 copy-start.11
  290.1 227.1 %shard_map.256 = (bf16[1024,2048]{1,0:T(8,128)(2,1)}, f32[1024,2048]{1,0:T(8,128)}, f32[1024,2048]{1,0:T(8,128)}, bf16[3,2048,512]{2,1,0:T(8,128)(2,1)}, bf16[51...) custom-call(s32[1]{0:T(128)S(6)} %copy.32.prefix_ref, ...), custom_call_target="tpu_custom_call" | custom-call | flops 1000 | bytes 1000 | tf_op jit(solution)/shard_map/pallas_call | solution.py:1234
  517.1 0.8 slice_reduce_fusion
  517.9 0.6 reshape_squeeze.3
  518.5 1.8 fusion
  520.4 7.8 %add_convert_fusion = bf16[1024,2048]{1,0:T(8,128)(2,1)} fusion(bf16[1024,2048]{1,0:T(8,128)(2,1)} %get-tuple-element.40, bf16[1024,2048]{1,0:T(8,128)(2,1)} %get-tuple-element.33.attn_hbm, bf16[1024,2048]{1,0:T(8,128)(2,1)} %src_hbm.3, f32[2048]{0:T(1024)S(1)} %copy-done.11, f32[2048]{0:T(1024)S(1)} %copy-done.10), kind=kLoop, calls=%fused_computation | loop fusion | flops 16777216 | bytes 16793600 | tf_op jit(solution)/shard_map/convert_element_type | solution.py:1343
  528.2 2.7 convert_element_type.39
  530.9 2.8 convert_element_type.38
  533.7 8.0 %copy.33 = f32[1024,2048]{1,0:T(8,128)} copy(f32[1024,2048]{1,0:T(8,128)} %get-tuple-element.74) | data formatting | bytes 16777216
  541.7 1.1 copy.34
  542.8 0.8 copy.35
  (15 shorter events, 0.0 us)
Async XLA Ops:
  7.2 4.6 copy-start.6
  7.2 521.0 %reduce-scatter.5.cloned.1.call-start = ((), (), s32[]{:S(2)}) async-start(), calls=%async_computation.3 | async-start | bytes 9437184 | tf_op jit(solution)/shard_map/reduce_scatter | solution.py:1286
  7.2 5.7 %copy-start.7 = (f32[2048,256]{1,0:T(8,128)S(1)}, f32[2048,256]{1,0:T(8,128)}, u32[]{:S(2)}) copy-start(f32[2048,256]{1,0:T(8,128)} %param.27) | copy-start | bytes 6291460
  10.2 3.8 copy-start.4
  10.2 3.8 copy-start.5
  68.0 1.3 copy-start
  69.3 2.0 copy-start.1
  71.3 1.0 copy-start.2
  72.3 1.7 copy-start.3
  289.3 241.5 %reduce-scatter.3.cloned.1.call-start = ((), (), s32[]{:S(2)}) async-start(), calls=%async_computation.2 | async-start | bytes 9437184 | tf_op jit(solution)/shard_map/reduce_scatter | solution.py:1286
  290.1 230.3 %copy-start.10 = (f32[2048]{0:T(1024)S(1)}, f32[2048]{0:T(1024)}, u32[]{:S(2)}) copy-start(f32[2048]{0:T(1024)} %param.22) | copy-start | bytes 24580
  290.1 230.3 %copy-start.11 = (f32[2048]{0:T(1024)S(1)}, f32[2048]{0:T(1024)}, u32[]{:S(2)}) copy-start(f32[2048]{0:T(1024)} %param.28) | copy-start | bytes 24580
  533.6 8.0 %copy-start.8 = (f32[3,256,512]{2,1,0:T(8,128)S(1)}, f32[3,256,512]{2,1,0:T(8,128)}, u32[]{:S(2)}) copy-start(f32[3,256,512]{2,1,0:T(8,128)} %get-tuple-element.77) | copy-start | bytes 4718596
  533.7 9.2 %copy-start.9 = (f32[512,256]{1,0:T(8,128)S(1)}, f32[512,256]{1,0:T(8,128)}, u32[]{:S(2)}) copy-start(f32[512,256]{1,0:T(8,128)} %get-tuple-element.79) | copy-start | bytes 1572868
Sparse Core Ops, SparseCore 0:
  289.4 70.8 reduce-scatter.4
  364.2 93.9 reduce-scatter.2

commit v8 on v7

--- a/solution.py
+++ b/solution.py
@@ -663,7 +663,7 @@
             dma((5,)),
         ]
         + ([dma((4, 2))] * 4 + [dma((2,))]) * 4,
-        compiler_params=kernel_params(3, 40),
+        compiler_params=kernel_params(3, 62),
         cost_estimate=COST,
     )(prefix_len, inputs, gain[None], shift[None], b_qv[:1], b_qv[1:], w_qkv, w_out)
 
@@ -838,11 +838,11 @@
 
 
 def backward_kernel(
-    n, spread, prefix_ref, projected, d_bin, b_out, gain1, gain2,
+    n, spread, prefix_ref, projected, d_bin, b_out, b_down, gain1, gain2,
     mlp_hbm, n1_hbm, ctx_hbm, w_qkv_hbm, w_out_hbm, src_hbm, attn_hbm, g_hbm, dn2_hbm,
-    mlp_sum, d_inputs, d_hidden, d_wqkv, d_wout, sum_wqkv, sum_wout, early, late,
+    mlp_sum, output, d_inputs, d_hidden, d_wqkv, d_wout, sum_wqkv, sum_wout, early, late,
     p, d_context, n1, ctx, branch, d_key, d_value, d_proj, w_stage, total, weights, ring, partial_sums,
-    p_sem, slice_sem, load_sem, store_sem, ring_in, ring_out, *more,
+    p_sem, slice_sem, load_sem, store_sem, ring_in, ring_out, out_in, out_store, *more,
 ):
     lines, more = more[:12], more[12:]
     tokens, depth = p.shape
@@ -1154,6 +1154,45 @@
             for load in hidden_loads(c + 2):
                 load.start()
 
+    def out_slot(c, i, side):
+        begin = (lax.rem(c, 2) * 4 + i) * 2 * CHUNK + side * CHUNK
+        return pl.ds(pl.multiple_of(begin, CHUNK), CHUNK)
+
+    def out_loads(c):
+        return [
+            pltpu.make_async_copy(
+                src.at[rows], branch.at[out_slot(c, i, side)], out_in.at[i, side]
+            )
+            for i, src in enumerate((src_hbm, attn_hbm, mlp_sum))
+            for side, rows in enumerate(sides(c, CHUNK))
+        ]
+
+    def out_stores(c):
+        return [
+            pltpu.make_async_copy(
+                branch.at[out_slot(c, 3, side)], output.at[rows], out_store.at[lax.rem(c, 2), side]
+            )
+            for side, rows in enumerate(sides(c, CHUNK))
+        ]
+
+    def output_rows(c):
+        for load in out_loads(c):
+            load.wait()
+
+        @pl.when(c >= 2)
+        def _():
+            for store in out_stores(c - 2):
+                store.wait()
+
+        for side in range(2):
+            source, attn, mlp = (
+                branch[out_slot(c, i, side)].astype(jnp.float32) for i in range(3)
+            )
+            whole = source + attn + b_out[...] + mlp + b_down[...]
+            branch[out_slot(c, 3, side)] = whole.astype(jnp.bfloat16)
+        for store in out_stores(c):
+            store.start()
+
     arrival = chunks + travel
 
     def tick_of(t):
@@ -1171,7 +1210,14 @@
                     load.start()
             loads[3].wait()
         begin = chunks + j * per_block
-        loop(begin, begin + per_block, tick_of if j == blocks - 1 else both_steps)
+
+        def with_output(t):
+            for load in out_loads(t - chunks):
+                load.start()
+            (tick_of if j == blocks - 1 else both_steps)(t)
+            output_rows(t - chunks)
+
+        loop(begin, begin + per_block, with_output)
         if spread:
             if j == 0:
                 pair()
@@ -1179,11 +1225,12 @@
                 early_end(j - 1)
             if j < blocks - 1:
                 early_begin(j)
-            else:
-                cross()
     begin = chunks + blocks * per_block
-    middle = begin + 2 * per_block
-    loop(begin, middle, tick_of)
+    middle = begin + 2 * per_block + 2
+    loop(begin, begin + per_block, tick_of)
+    if spread:
+        cross()
+    loop(begin + per_block, middle, tick_of)
     if spread:
         for k in range(len(pieces)):
             total_of(k)
@@ -1197,7 +1244,7 @@
             late_begin(i)
             late_end(i)
     for c in (chunks - 2, chunks - 1):
-        for store in input_stores(c):
+        for store in input_stores(c) + out_stores(c):
             store.wait()
     if spread:
         finish_scatter()
@@ -1208,7 +1255,7 @@
 
 
 def backward(
-    prefix_len, projected, d_bin, b_out, gain1, gain2, mlp_partial, normed1, context, w_qkv, w_out,
+    prefix_len, projected, d_bin, b_out, b_down, gain1, gain2, mlp_partial, normed1, context, w_qkv, w_out,
     inputs, attn_sum, d_output, summed2,
 ):
     tokens, depth = inputs.shape
@@ -1235,6 +1282,7 @@
         partial(backward_kernel, lax.axis_size("row"), spread),
         out_shape=[
             low_shape(tokens, depth),
+            low_shape(tokens, depth),
             single(tokens, depth),
             single(tokens, depth),
             low_shape(3, depth, width),
@@ -1243,8 +1291,8 @@
             single(8, depth),
             single(8, depth),
         ],
-        in_specs=[pl.BlockSpec(memory_space=pltpu.SMEM)] + [IN_VMEM] * 5 + [IN_HBM] * 9,
-        out_specs=[IN_HBM] * 7 + [IN_VMEM] * 2,
+        in_specs=[pl.BlockSpec(memory_space=pltpu.SMEM)] + [IN_VMEM] * 6 + [IN_HBM] * 9,
+        out_specs=[IN_HBM] * 8 + [IN_VMEM] * 2,
         scratch_shapes=[
             buffer(tokens, depth),
             buffer(tokens, width),
@@ -1265,6 +1313,8 @@
             dma((2,)),
             dma((RING, 2)),
             dma((RING, 2)),
+            dma((3, 2)),
+            dma((2, 2)),
         ]
         + line_scratch((tokens, depth))
         + line_scratch((tokens, depth))
@@ -1272,14 +1322,14 @@
         compiler_params=kernel_params(2, 63),
         cost_estimate=COST,
     )(
-        prefix_len, projected, d_bin, b_out[None], gain1[None], gain2[None], mlp_partial, normed1,
+        prefix_len, projected, d_bin, b_out[None], b_down[None], gain1[None], gain2[None], mlp_partial, normed1,
         context, w_qkv, w_out, inputs, attn_sum, d_output, summed2,
     )
-    mlp_sum, d_inputs, _, d_wqkv, d_wout, sum_wqkv, sum_wout, early, late = out
+    _, output, d_inputs, _, d_wqkv, d_wout, sum_wqkv, sum_wout, early, late = out
     if not spread:
         early, late = lax.psum((early, late), ("dp", "col"))
         sum_wqkv, sum_wout = scatter_low(d_wqkv, 1), scatter_low(d_wout, 1)
-    return mlp_sum, d_inputs, sum_wqkv, sum_wout, early, late
+    return output, d_inputs, sum_wqkv, sum_wout, early, late
 
 
 def scatter_low(grad, dim):
@@ -1335,12 +1385,10 @@
     )
     sent_win = scatter_low(grad_win, 0)
     sent_wdown = scatter_low(grad_wdown, 1)
-    mlp_sum, d_inputs, sent_wqkv, sent_wout, early, late = backward(
-        prefix_len, projected, grad_bin, b_out, norm1_gain, norm2_gain, mlp_partial, normed1_low,
+    output, d_inputs, sent_wqkv, sent_wout, early, late = backward(
+        prefix_len, projected, grad_bin, b_out, b_down, norm1_gain, norm2_gain, mlp_partial, normed1_low,
         context_low, full_qkv, full_out, inputs, attn_sum, d_output, summed2,
     )
-    hidden = source + attn_sum.astype(jnp.float32) + b_out
-    output = (hidden + mlp_sum.astype(jnp.float32) + b_down).astype(jnp.bfloat16)
     width = b_qv.shape[1]
     return (
         output,

time: 556 us -> 548 us (0.986)
  other arithmetic: 18.1 us -> 11.8 us
    convert_element_type x1 -> x0, other arithmetic: 7.78 us -> none  [local(): (hidden + mlp_sum.astype(jnp.float32) + b_down).astype(jnp.bfloat16)]
    unnamed x27 -> x14, local copies, waits for them, and re-layouts: 16 us -> 11.6 us
  transfers between devices with their start and end apart: 2 -> 2, of which waited for: 0 -> 0; matrix products, arithmetic and copies ran while one was open for 2% -> 1% of each run, Pallas kernels for 41% -> 42%
where the time goes in v8:
time: 548 us; the launch traced here: 542 us
  Pallas kernels  498 us (91%)
  local copies, waits for them, and re-layouts  16.4 us (3%)
  between operations  15.1 us (3%)
  other arithmetic  11.8 us (2%)
    pallas_call x1, Pallas kernels, backward(): pl.pallas_call(partial(backward_kernel, lax.axis_size('row'), spread), ou...  227 us
    pallas_call x1, Pallas kernels, mlp_sums(): pl.pallas_call(partial(mlp_sums_kernel, lax.axis_size('row'), spread), ou...  215 us
    pallas_call x1, Pallas kernels, head(): pl.pallas_call(head_kernel, out_shape=[low_shape(tokens, depth), low_shap...  55.4 us
    unnamed x14, local copies, waits for them, and re-layouts  11.6 us
  transfers between devices with their start and end apart: 2, of which 0 were waited for; matrix products, arithmetic and copies ran while one was open for 1% of the time, Pallas kernels for 42%

profile of v8, /device:TPU:0, one launch (start us, length us, event | category | flops | bytes accessed | tf_op | source)
XLA Modules:
  0.0 542.1 jit_solution(7903893114954330809)
XLA Ops:
  7.2 0.0 copy-start.1
  7.2 0.0 reduce-scatter.5.cloned.1.call-start
  7.2 0.0 copy-start.2
  8.0 1.7 fusion.2
  9.7 1.8 convert_element_type.19.w_out_hbm
  11.5 2.4 convert_element_type.18.w_qkv_hbm
  13.9 0.0 copy-done.1
  13.9 1.1 convert_element_type.20.w_in_hbm
  15.0 0.0 copy-done.2
  15.0 1.1 convert_element_type.21.w_down_hbm
  16.1 55.4 %shard_map.254 = (bf16[1024,2048]{1,0:T(8,128)(2,1)}, bf16[3,1024,512]{2,1,0:T(8,128)(2,1)}, bf16[1024,512]{1,0:T(8,128)(2,1)}, bf16[3,2048,512]{2,1,0:T(8,128)(2,1)}, bf16[512,2048]{1,0:T(8,128)(2,1)}) custom-call(s32[1]{0:T(128)S(6)} %copy.33.prefix_ref, bf16[1024,2048]{1,0:T(8,128)(2,1)} %src_hbm.3, f32[1,2048]{1,0:T(1,128)} %bitcast.14, ...), custom_call_target="tpu_custom_call" | custom-call | flops 1000 | bytes 1000 | tf_op jit(solution)/shard_map/pallas_call | solution.py:646
  71.5 215.3 %shard_map.255 = (bf16[1024,2048]{1,0:T(8,128)(2,1)}, bf16[1024,2048]{1,0:T(8,128)(2,1)}, bf16[1024,2048]{1,0:T(8,128)(2,1)}, bf16[2048,2048]{1,0:T(8,128)(2,1)}...) custom-call(bf16[1024,512]{1,0:T(8,128)(2,1)} %get-tuple-element.32.ctx.ctx_hbm, ...), custom_call_target="tpu_custom_call" | custom-call | flops 1000 | bytes 1000 | tf_op jit(solution)/shard_map/pallas_call | solution.py:511
  286.8 0.0 reduce-scatter.5.cloned.1.call-update
  286.9 0.0 reduce-scatter.3.cloned.1.call-start
  286.9 0.7 reduce-scatter.3.cloned.1.call-update
  287.6 227.2 %shard_map.256 = (bf16[1024,2048]{1,0:T(8,128)(2,1)}, bf16[1024,2048]{1,0:T(8,128)(2,1)}, f32[1024,2048]{1,0:T(8,128)}, f32[1024,2048]{1,0:T(8,128)}, bf16[3,204...) custom-call(s32[1]{0:T(128)S(6)} %copy.33.prefix_ref, ...), custom_call_target="tpu_custom_call" | custom-call | flops 1000 | bytes 1000 | tf_op jit(solution)/shard_map/pallas_call | solution.py:1281
  514.8 0.8 slice_reduce_fusion
  515.6 0.6 reshape_squeeze.3
  516.2 1.7 fusion
  517.9 0.0 reduce-scatter.5.cloned.1.call-done
  517.9 2.7 convert_element_type.23
  520.6 0.0 reduce-scatter.3.cloned.1.call-done
  520.6 2.8 convert_element_type.22
  523.4 0.0 copy-start
  523.4 5.1 copy.34
  528.5 1.1 copy-done
  529.6 0.0 copy-start.3
  529.6 3.5 copy.35
  533.1 0.0 copy-done.3
  533.1 1.1 copy.36
  534.2 0.0 copy-done.4
  534.2 0.8 copy.37
  (1 shorter events, 0.0 us)
Async XLA Ops:
  7.2 6.7 %copy-start.1 = (f32[256,2048]{1,0:T(8,128)S(1)}, f32[256,2048]{1,0:T(8,128)}, u32[]{:S(2)}) copy-start(f32[256,2048]{1,0:T(8,128)} %param.25) | copy-start | bytes 6291460
  7.2 510.7 %reduce-scatter.5.cloned.1.call-start = ((), (), s32[]{:S(2)}) async-start(), calls=%async_computation.3 | async-start | bytes 9437184 | tf_op jit(solution)/shard_map/reduce_scatter | solution.py:1336
  7.2 7.8 %copy-start.2 = (f32[2048,256]{1,0:T(8,128)S(1)}, f32[2048,256]{1,0:T(8,128)}, u32[]{:S(2)}) copy-start(f32[2048,256]{1,0:T(8,128)} %param.27) | copy-start | bytes 6291460
  286.9 233.8 %reduce-scatter.3.cloned.1.call-start = ((), (), s32[]{:S(2)}) async-start(), calls=%async_computation.2 | async-start | bytes 9437184 | tf_op jit(solution)/shard_map/reduce_scatter | solution.py:1336
  523.4 6.2 %copy-start = (f32[1024,2048]{1,0:T(8,128)S(1)}, f32[1024,2048]{1,0:T(8,128)}, u32[]{:S(2)}) copy-start(f32[1024,2048]{1,0:T(8,128)} %get-tuple-element.74) | copy-start | bytes 25165828
  529.6 3.5 copy-start.3
  529.6 4.7 copy-start.4
Sparse Core Ops, SparseCore 0:
  287.0 70.9 reduce-scatter.4
  361.8 92.4 reduce-scatter.2

commit v9 on v8

--- a/solution.py
+++ b/solution.py
@@ -1217,11 +1217,13 @@
             (tick_of if j == blocks - 1 else both_steps)(t)
             output_rows(t - chunks)
 
-        loop(begin, begin + per_block, with_output)
+        if spread and j == 0:
+            loop(begin, begin + 2, with_output)
+            pair()
+            begin = begin + 2
+        loop(begin, chunks + (j + 1) * per_block, with_output)
         if spread:
-            if j == 0:
-                pair()
-            else:
+            if j > 0:
                 early_end(j - 1)
             if j < blocks - 1:
                 early_begin(j)

time: 548 us -> 547 us (level)
  no operation moved by 1% of the time
where the time goes in v9:
time: 547 us; the launch traced here: 542 us
  Pallas kernels  497 us (91%)
  local copies, waits for them, and re-layouts  16.4 us (3%)
  between operations  15.1 us (3%)
  other arithmetic  11.8 us (2%)
    pallas_call x1, Pallas kernels, backward(): pl.pallas_call(partial(backward_kernel, lax.axis_size('row'), spread), ou...  227 us
    pallas_call x1, Pallas kernels, mlp_sums(): pl.pallas_call(partial(mlp_sums_kernel, lax.axis_size('row'), spread), ou...  215 us
    pallas_call x1, Pallas kernels, head(): pl.pallas_call(head_kernel, out_shape=[low_shape(tokens, depth), low_shap...  55.4 us
    unnamed x14, local copies, waits for them, and re-layouts  11.6 us
  transfers between devices with their start and end apart: 2, of which 0 were waited for; matrix products, arithmetic and copies ran while one was open for 1% of the time, Pallas kernels for 42%

profile of v9, /device:TPU:0, one launch (start us, length us, event | category | flops | bytes accessed | tf_op | source)
XLA Modules:
  0.0 541.6 jit_solution(9491300352833012612)
XLA Ops:
  7.2 0.0 copy-start.1
  7.2 0.0 reduce-scatter.5.cloned.1.call-start
  7.2 0.0 copy-start.2
  8.0 1.7 fusion.2
  9.7 1.8 convert_element_type.19.w_out_hbm
  11.5 2.4 convert_element_type.18.w_qkv_hbm
  13.9 0.0 copy-done.1
  13.9 1.1 convert_element_type.20.w_in_hbm
  15.0 0.0 copy-done.2
  15.0 1.1 convert_element_type.21.w_down_hbm
  16.1 55.4 %shard_map.254 = (bf16[1024,2048]{1,0:T(8,128)(2,1)}, bf16[3,1024,512]{2,1,0:T(8,128)(2,1)}, bf16[1024,512]{1,0:T(8,128)(2,1)}, bf16[3,2048,512]{2,1,0:T(8,128)(2,1)}, bf16[512,2048]{1,0:T(8,128)(2,1)}) custom-call(s32[1]{0:T(128)S(6)} %copy.33.prefix_ref, bf16[1024,2048]{1,0:T(8,128)(2,1)} %src_hbm.3, f32[1,2048]{1,0:T(1,128)} %bitcast.14, ...), custom_call_target="tpu_custom_call" | custom-call | flops 1000 | bytes 1000 | tf_op jit(solution)/shard_map/pallas_call | solution.py:646
  71.5 215.3 %shard_map.255 = (bf16[1024,2048]{1,0:T(8,128)(2,1)}, bf16[1024,2048]{1,0:T(8,128)(2,1)}, bf16[1024,2048]{1,0:T(8,128)(2,1)}, bf16[2048,2048]{1,0:T(8,128)(2,1)}...) custom-call(bf16[1024,512]{1,0:T(8,128)(2,1)} %get-tuple-element.32.ctx.ctx_hbm, ...), custom_call_target="tpu_custom_call" | custom-call | flops 1000 | bytes 1000 | tf_op jit(solution)/shard_map/pallas_call | solution.py:511
  286.8 0.0 reduce-scatter.5.cloned.1.call-update
  286.9 0.0 reduce-scatter.3.cloned.1.call-start
  286.9 0.7 reduce-scatter.3.cloned.1.call-update
  287.6 226.7 %shard_map.256 = (bf16[1024,2048]{1,0:T(8,128)(2,1)}, bf16[1024,2048]{1,0:T(8,128)(2,1)}, f32[1024,2048]{1,0:T(8,128)}, f32[1024,2048]{1,0:T(8,128)}, bf16[3,204...) custom-call(s32[1]{0:T(128)S(6)} %copy.33.prefix_ref, ...), custom_call_target="tpu_custom_call" | custom-call | flops 1000 | bytes 1000 | tf_op jit(solution)/shard_map/pallas_call | solution.py:1283
  514.3 0.8 slice_reduce_fusion
  515.1 0.6 reshape_squeeze.3
  515.7 1.7 fusion
  517.4 0.0 reduce-scatter.5.cloned.1.call-done
  517.4 2.7 convert_element_type.23
  520.1 0.0 reduce-scatter.3.cloned.1.call-done
  520.1 2.8 convert_element_type.22
  522.9 0.0 copy-start
  522.9 5.1 copy.34
  527.9 1.1 copy-done
  529.0 0.0 copy-start.3
  529.0 3.5 copy.35
  532.6 0.0 copy-done.3
  532.6 1.1 copy.36
  533.7 0.0 copy-done.4
  533.7 0.8 copy.37
  (1 shorter events, 0.0 us)
Async XLA Ops:
  7.2 6.7 %copy-start.1 = (f32[256,2048]{1,0:T(8,128)S(1)}, f32[256,2048]{1,0:T(8,128)}, u32[]{:S(2)}) copy-start(f32[256,2048]{1,0:T(8,128)} %param.25) | copy-start | bytes 6291460
  7.2 510.2 %reduce-scatter.5.cloned.1.call-start = ((), (), s32[]{:S(2)}) async-start(), calls=%async_computation.3 | async-start | bytes 9437184 | tf_op jit(solution)/shard_map/reduce_scatter | solution.py:1338
  7.2 7.8 %copy-start.2 = (f32[2048,256]{1,0:T(8,128)S(1)}, f32[2048,256]{1,0:T(8,128)}, u32[]{:S(2)}) copy-start(f32[2048,256]{1,0:T(8,128)} %param.27) | copy-start | bytes 6291460
  286.9 233.2 %reduce-scatter.3.cloned.1.call-start = ((), (), s32[]{:S(2)}) async-start(), calls=%async_computation.2 | async-start | bytes 9437184 | tf_op jit(solution)/shard_map/reduce_scatter | solution.py:1338
  522.9 6.2 %copy-start = (f32[1024,2048]{1,0:T(8,128)S(1)}, f32[1024,2048]{1,0:T(8,128)}, u32[]{:S(2)}) copy-start(f32[1024,2048]{1,0:T(8,128)} %get-tuple-element.74) | copy-start | bytes 25165828
  529.0 3.5 copy-start.3
  529.0 4.7 copy-start.4
Sparse Core Ops, SparseCore 0:
  287.0 70.9 reduce-scatter.4
  361.8 82.3 reduce-scatter.2
